TPU v7x, 32 devices: a whole 2x2x4 slice. The times are simulated.
32 devices in a mesh: dp: 4 (over z), seq: 8 (over y, x, core).
Axes of the slice: x: 2, y: 2, z: 4, core: 2. Of those that a mesh axis runs over, the one named last changes fastest.
Arguments:
- inputs: bfloat16 [4, 1024, 4096], P('dp', 'seq'), may hold values from -6 to 6
- out_grads: bfloat16 [4, 1024, 14336], P('dp', 'seq'), may hold values from -6 to 6
- valid: int32 [4, 1024], P('dp', 'seq'), may hold values 0 or 1
- doc_blocks: int32 [4, 4], P('dp'), may hold values from 1 to 4, 8 in all within a row
- doc_ids: int32 [16], replicated, may hold values from 0 to 15, each once
- proj_in: bfloat16 [4096, 64], P('seq'), may hold values from -0.09375 to 0.09375
- proj_out: bfloat16 [14336, 64], P('seq'), may hold values from -0.046875 to 0.046875
- test_grads: bfloat16 [256, 4096], P('seq'), may hold values from -192 to 192
Outputs:
- scores: float32 [16, 256], P(None, 'seq')
Inputs may be any that keep to these rules, and one draw needn't show every extreme that they name: `doc_blocks`: each group's lengths sum to 8; the largest is 4 in every group. `doc_ids`: every document number appears once.
All inputs are finite; a program needn't handle non-finite values. No bound on the sum of `valid` on one device may be relied on, other than what follows from the above.
Results may differ from a plain program's by a relative error of at most 0.0003.
Values may be sent and summed in bfloat16 or wider, within the bound.
No kernel may reach another device: no remote copies, remote signals or barrier semaphores. Data moves between devices by JAX's collectives and lax.ppermute only.
A program may use at most 64 MiB of HBM per device.

v0:
```python
import jax
import jax.numpy as jnp
from jax import lax
from jax.sharding import PartitionSpec as P

PROJ_OUT = 64
FEAT = 4096
BLOCK = 128
DOC_GRP = 4


def per_device(inputs, out_grads, valid, doc_blocks, doc_ids, proj_in, proj_out, test_grads):
    tokens = inputs[0]
    outgrad = out_grads[0]
    slots = tokens.shape[0]
    columns = tokens
    px = jnp.dot(
        columns,
        lax.all_gather(proj_in, "seq", axis=0, tiled=True),
        preferred_element_type=jnp.float32,
    )
    columns = outgrad
    pg = jnp.dot(
        columns,
        lax.all_gather(proj_out, "seq", axis=0, tiled=True),
        preferred_element_type=jnp.float32,
    )
    ends = jnp.cumsum(doc_blocks[0])
    position = lax.axis_index("seq") * slots + jnp.arange(slots, dtype=jnp.int32)
    blk = position // BLOCK
    owner = jnp.sum((blk[:, None] >= ends[None, :]).astype(jnp.int32), axis=1)
    onehot = (
        (owner[:, None] == jnp.arange(DOC_GRP, dtype=jnp.int32)[None, :]) & (valid[0][:, None] == 1)
    ).astype(jnp.float32)
    weighted = (onehot[:, :, None] * pg[:, None, :]).reshape(slots, DOC_GRP * PROJ_OUT)
    partial_grads = jnp.dot(weighted.T, px, precision=lax.Precision.HIGHEST).reshape(DOC_GRP, FEAT)
    ndocs = DOC_GRP * lax.axis_size("dp")
    group_grads = lax.psum(partial_grads, "seq")
    doc_grads = lax.all_gather(group_grads, "dp", axis=0, tiled=True)
    gram = jnp.dot(doc_grads, doc_grads.T, precision=lax.Precision.HIGHEST)
    cross = jnp.dot(doc_grads, test_grads.astype(jnp.float32).T, precision=lax.Precision.HIGHEST)
    damp = 0.1 * jnp.trace(gram) / ndocs
    matrix = gram / ndocs + damp * jnp.eye(ndocs, dtype=jnp.float32)
    factor = jnp.linalg.cholesky(matrix)
    middle = lax.linalg.triangular_solve(factor, cross, left_side=True, lower=True)
    solved = lax.linalg.triangular_solve(
        factor, middle, left_side=True, lower=True, transpose_a=True
    )
    placing = (doc_ids[None, :] == jnp.arange(ndocs, dtype=jnp.int32)[:, None]).astype(jnp.float32)
    return jnp.dot(placing, solved, precision=lax.Precision.HIGHEST)


def solution(mesh):
    in_specs = (
        P("dp", "seq", None),
        P("dp", "seq", None),
        P("dp", "seq"),
        P("dp", None),
        P(),
        P("seq", None),
        P("seq", None),
        P("seq", None),
    )
    out_specs = P(None, "seq")
    return jax.shard_map(
        per_device, mesh=mesh, in_specs=in_specs, out_specs=out_specs, check_vma=False
    )
```

profile of v0, /device:TPU:0, one launch (start us, length us, event | category | flops | bytes accessed | tf_op | source)
XLA Modules:
  0.0 124.8 jit_solution(5688418271160069802)
XLA Ops:
  6.5 0.7 all-gather.3.cloned.1.call-update
  7.3 0.8 reduce-window.8
  8.1 0.1 convert_reduce_fusion
  8.2 11.6 %all_gather.10 = bf16[4096,64]{0,1:T(8,128)(2,1)S(1)} all-gather(bf16[512,64]{0,1:T(8,128)(2,1)} %param.13), channel_id=1, replica_groups=mesh['dp'=4,'seq'=8] {'seq'}, dimensions={0}, use_global_device_ids=true | all-gather | bytes 589824 | tf_op jit(solution)/shard_map/all_gather | solution.py:19
  19.8 0.7 compare_bitcast_fusion
  20.5 0.5 fusion.2
  21.0 17.7 %all-gather.3.cloned.1.call-done = bf16[14336,64]{0,1:T(8,128)(2,1)} async-done(((bf16[1792,64]{0,1:T(8,128)(2,1)}), bf16[14336,64]{0,1:T(8,128)(2,1)}) %all-gather.3.cloned.1.call-update) | async-done | bytes 1835024 | tf_op jit(solution)/shard_map/all_gather | solution.py:25
  38.8 4.0 %fusion = f32[128,64]{0,1:T(8,128)S(1)} fusion(bf16[14336,64]{0,1:T(8,128)(2,1)} %all-gather.3.cloned.1.call-done, bf16[1,128,14336]{2,1,0:T(8,128)(2,1)} %param.9), kind=kOutput, calls=%fused_computation | convolution fusion | flops 234881024 | bytes 5537792 | tf_op jit(solution)/shard_map/dot_general | solution.py:23
  42.8 0.3 fusion.15
  43.1 0.7 reshape.111
  43.8 52.6 %all-reduce.2.cloned.1.call-done = f32[4,4096]{1,0:T(4,128)} async-done(((f32[4,4096]{1,0:T(4,128)}), f32[4,4096]{1,0:T(4,128)}) %all-reduce.2.cloned.1.call-update) | async-done | bytes 65552 | tf_op jit(solution)/shard_map/psum | solution.py:38
  96.4 14.1 %all-gather = f32[4,4,4096]{2,1,0:T(4,128)S(1)} all-gather(f32[1,4,4096]{2,1,0:T(4,128)} %bitcast.37), channel_id=1, replica_groups=mesh['dp'=4,'seq'=8] {'dp'}, dimensions={0}, use_global_device_ids=true | all-gather | bytes 327680 | tf_op jit(solution)/shard_map/all_gather | solution.py:39
  110.5 0.1 reshape.113
  110.6 1.1 select_reduce_fusion.1
  111.7 0.3 fusion.16
  112.0 0.1 copy.19
  112.1 0.1 copy.20
  112.9 1.4 %cholesky.17 = f32[16,16]{1,0:T(8,128)S(1)} custom-call(f32[16,16]{1,0:T(8,128)S(1)} %fusion.10), custom_call_target="Cholesky" | custom-call | tf_op jit(solution)/shard_map/jit(cholesky)/cholesky | solution.py:44
  114.4 0.6 compare_reduce_fusion
  115.0 0.6 fusion.4
  115.7 1.2 custom-call.8
  116.9 0.2 fusion.7
  117.1 0.1 fusion.5
  117.2 0.7 fusion.11
  (15 shorter events, 0.2 us)
Async XLA Ops:
  6.5 14.0 %copy-start = (bf16[1,128,4096]{2,1,0:T(8,128)(2,1)S(1)}, bf16[1,128,4096]{2,1,0:T(8,128)(2,1)}, u32[]{:S(2)}) copy-start(bf16[1,128,4096]{2,1,0:T(8,128)(2,1)} %param.8) | copy-start | bytes 3145732
  6.5 32.2 %all-gather.3.cloned.1.call-start = ((), (), s32[]{:S(2)}) async-start(), calls=%async_computation | async-start | bytes 2064384 | tf_op jit(solution)/shard_map/all_gather | solution.py:25
  7.3 89.2 %all-reduce.2.cloned.1.call-start = ((), (), s32[]{:S(2)}) async-start(), calls=%async_computation.1 | async-start | bytes 131072 | tf_op jit(solution)/shard_map/psum | solution.py:38
  21.0 90.7 %copy-start.1 = (bf16[32,4096]{1,0:T(8,128)(2,1)S(1)}, bf16[32,4096]{1,0:T(8,128)(2,1)}, u32[]{:S(2)}) copy-start(bf16[32,4096]{1,0:T(8,128)(2,1)} %param.15) | copy-start | bytes 786436
  21.0 96.2 %copy-start.2 = (s32[16]{0:T(128)S(1)}, s32[16]{0:T(128)}, u32[]{:S(2)}) copy-start(s32[16]{0:T(128)} %param.12) | copy-start | bytes 196
Sparse Core Ops, SparseCore 0:
  9.3 29.4 all-gather.2
  43.9 52.4 all-reduce.1
where the time goes:
time: 125 us
  waiting for transfers between devices  71.1 us (57%)
  blocking collectives  25.7 us (21%)
  between operations  14.2 us (11%)
  matrix products  7.23 us (6%)
  other arithmetic  5.62 us (4%)
    psum x1, waiting for transfers between devices, per_device(): group_grads = lax.psum(partial_grads, 'seq')  52.6 us
    all_gather x1, waiting for transfers between devices, per_device(): lax.all_gather(proj_out, 'seq', axis=0, tiled=True)  17.7 us
    all_gather x1, blocking collectives, per_device(): doc_grads = lax.all_gather(group_grads, 'dp', axis=0, tiled=True)  14.1 us
    all_gather x1, blocking collectives, per_device(): lax.all_gather(proj_in, 'seq', axis=0, tiled=True)  11.6 us
    dot_general x1, matrix products, per_device(): jnp.dot(columns, lax.all_gather(proj_out, 'seq', axis=0, tiled=True), pre...  3.99 us
  transfers between devices with their start and end apart: 2, of which 2 were waited for; matrix products, arithmetic and copies ran while one was open for 2% of the time, Pallas kernels for 0%

commit v1 on v0

v1 whole, which is shorter than its diff:
```python
import jax
import jax.numpy as jnp
from jax import lax
from jax.sharding import PartitionSpec as P

BLOCK = 128
HIGH = lax.Precision.HIGHEST


def owner_weights(doc_blocks, valid, slots):
    ends = jnp.cumsum(doc_blocks[0])
    position = lax.axis_index("seq") * slots + jnp.arange(slots, dtype=jnp.int32)
    owner = jnp.sum((position // BLOCK)[:, None] >= ends[None, :], axis=1)
    mine = owner[None, :] == jnp.arange(ends.shape[0])[:, None]
    return (mine & (valid[0][None, :] == 1)).astype(jnp.float32)


def solve_and_place(gram, cross, doc_ids):
    ndocs = gram.shape[0]
    damp = 0.1 * jnp.trace(gram) / ndocs
    matrix = gram / ndocs + damp * jnp.eye(ndocs, dtype=jnp.float32)
    factor = jnp.linalg.cholesky(matrix)
    middle = lax.linalg.triangular_solve(factor, cross, left_side=True, lower=True)
    solved = lax.linalg.triangular_solve(
        factor, middle, left_side=True, lower=True, transpose_a=True
    )
    placing = (doc_ids[None, :] == jnp.arange(ndocs, dtype=jnp.int32)[:, None]).astype(jnp.float32)
    return jnp.dot(placing, solved, precision=HIGH)


def any_mesh(inputs, out_grads, valid, doc_blocks, doc_ids, proj_in, proj_out, test_grads):
    px = jnp.dot(inputs[0], lax.all_gather(proj_in, "seq", tiled=True), preferred_element_type=jnp.float32)
    pg = jnp.dot(out_grads[0], lax.all_gather(proj_out, "seq", tiled=True), preferred_element_type=jnp.float32)
    weights = owner_weights(doc_blocks, valid, px.shape[0])
    weighted = weights[:, None, :] * pg.T[None, :, :]
    grads = jnp.einsum("jat,tb->jab", weighted, px, precision=HIGH)
    grads = lax.psum(grads.reshape(grads.shape[0], -1), "seq")
    grads = lax.all_gather(grads, "dp", tiled=True)
    gram = jnp.dot(grads, grads.T, precision=HIGH)
    cross = jnp.dot(grads, test_grads.astype(jnp.float32).T, precision=HIGH)
    return solve_and_place(gram, cross, doc_ids)


def paired_chips(inputs, out_grads, valid, doc_blocks, doc_ids, proj_in, proj_out, test_grads):
    seq = lax.axis_index("seq")
    dp = lax.axis_index("dp")
    core = seq & 1

    def swap(x, bits):
        return lax.ppermute(x, "seq", [(i, i ^ b) for i, b in enumerate(bits)])

    first, second, other = (2, 4) * 4, (4, 2) * 4, (1,) * 8

    def gather(own):
        a = swap(own, first)
        b = swap(own, second)
        c = swap(a, second)
        near = [own, a, b, c]
        far = [swap(x, other) for x in near]
        return near, far

    def project(tokens, own):
        near, far = gather(own)
        rows = own.shape[0]
        one = 2 + 2 * core
        two = 6 - one
        ids = [seq, seq ^ one, seq ^ two, seq ^ 6]
        far_ids = [seq ^ 1, seq ^ 1 ^ two, seq ^ 1 ^ one, seq ^ 7]
        total = 0.0
        for i, w in zip(ids + far_ids, near + far):
            part = lax.dynamic_slice(tokens, (0, i * rows), (tokens.shape[0], rows))
            total = total + jnp.dot(part, w, preferred_element_type=jnp.float32)
        return total

    pg = project(out_grads[0], proj_out)
    px = project(inputs[0], proj_in)
    weights = owner_weights(doc_blocks, valid, px.shape[0])
    weighted = weights[:, None, :] * pg.T[None, :, :]
    grads = jnp.einsum("jat,tb->jab", weighted, px, precision=HIGH)
    docs, aa, bb = grads.shape
    halves = grads.reshape(docs, 2, aa // 2, bb)
    keep = lax.dynamic_index_in_dim(halves, core, 1, keepdims=False)
    send = lax.dynamic_index_in_dim(halves, 1 - core, 1, keepdims=False)
    mine = keep + swap(send, other)
    mine = (mine + swap(mine, (6,) * 8)) + (swap(mine, (2,) * 8) + swap(mine, (4,) * 8))
    ndp = lax.axis_size("dp")
    every = [mine] + [lax.ppermute(mine, "dp", [(i, i ^ k) for i in range(ndp)]) for k in range(1, ndp)]
    allg = jnp.zeros((ndp,) + mine.shape, jnp.float32)
    for k, m in enumerate(every):
        allg = lax.dynamic_update_slice(allg, m[None], (dp ^ k, 0, 0, 0))
    allg = allg.reshape(ndp * docs, -1)
    ntest, feat = test_grads.shape
    th = test_grads.reshape(ntest, 2, feat // 2)
    t_keep = lax.dynamic_index_in_dim(th, core, 1, keepdims=False)
    t_send = lax.dynamic_index_in_dim(th, 1 - core, 1, keepdims=False)
    t_recv = swap(t_send, other)
    gram = jnp.dot(allg, allg.T, precision=HIGH)
    cross = jnp.dot(allg, t_keep.astype(jnp.float32).T, precision=HIGH)
    far = jnp.dot(allg, t_recv.astype(jnp.float32).T, precision=HIGH)
    got = swap(jnp.concatenate([far, gram], axis=1), other)
    cross = cross + got[:, :ntest]
    gram = gram + got[:, ntest:]
    return solve_and_place(gram, cross, doc_ids)


def solution(mesh):
    in_specs = (
        P("dp", "seq", None),
        P("dp", "seq", None),
        P("dp", "seq"),
        P("dp", None),
        P(),
        P("seq", None),
        P("seq", None),
        P("seq", None),
    )
    fast = mesh.shape["seq"] == 8 and mesh.shape["dp"] == 4
    return jax.shard_map(
        paired_chips if fast else any_mesh,
        mesh=mesh, in_specs=in_specs, out_specs=P(None, "seq"), check_vma=False,
    )
```

time: 125 us -> 54.2 us (0.43)
  waiting for transfers between devices: 71.1 us -> 14.6 us
  blocking collectives: 25.7 us -> 0 us
  starting transfers between devices: 0.04 us -> 20 us
  between operations: 14.2 us -> 1.06 us
  matrix products: 7.23 us -> 10.6 us
    psum x1 -> x0, waiting for transfers between devices: 52.6 us -> none  [per_device(): group_grads = lax.psum(partial_grads, 'seq')]
    all_gather x2 -> x0, blocking collectives: 25.7 us -> none  [the longest x1 14.1 us: per_device(): doc_grads = lax.all_gather(group_grads, 'dp', axis=0, tiled=True)]
    ppermute x0 -> x23, starting transfers between devices: none -> 20 us  [the longest x20 15.5 us: swap(): return lax.ppermute(x, 'seq', [(i, i ^ b) for i, b in enumerate(bits)])]
    all_gather x1 -> x0, waiting for transfers between devices: 17.7 us -> none  [per_device(): lax.all_gather(proj_out, 'seq', axis=0, tiled=True)]
    ppermute x0 -> x23, waiting for transfers between devices: none -> 14.6 us  [the longest x20 8.56 us: swap(): return lax.ppermute(x, 'seq', [(i, i ^ b) for i, b in enumerate(bits)])]
    dot_general x6 -> x21, matrix products: 6.88 us -> 10.2 us  [the longest x16 8.52 us: project(): total = total + jnp.dot(part, w, preferred_element_type=jnp.float32)]
  transfers between devices with their start and end apart: 2 -> 23, of which waited for: 2 -> 12; matrix products, arithmetic and copies ran while one was open for 2% -> 20% of each run, Pallas kernels for 0% -> 0%
where the time goes in v1:
time: 54.2 us; the launch traced here: 53.8 us
  starting transfers between devices  20 us (37%)
  waiting for transfers between devices  14.6 us (27%)
  matrix products  10.6 us (20%)
  other arithmetic  6.51 us (12%)
  local copies, waits for them, and re-layouts  1.09 us (2%)
  between operations  1.06 us (2%)
    ppermute x20, starting transfers between devices, swap(): return lax.ppermute(x, 'seq', [(i, i ^ b) for i, b in enumerate(bits)])  15.5 us
    ppermute x20, waiting for transfers between devices, swap(): return lax.ppermute(x, 'seq', [(i, i ^ b) for i, b in enumerate(bits)])  8.56 us
    dot_general x16, matrix products, project(): total = total + jnp.dot(part, w, preferred_element_type=jnp.float32)  8.52 us
    ppermute x3, waiting for transfers between devices, paired_chips(): lax.ppermute(mine, 'dp', [(i, i ^ k) for i in range(ndp)])  5.99 us
    ppermute x3, starting transfers between devices, paired_chips(): lax.ppermute(mine, 'dp', [(i, i ^ k) for i in range(ndp)])  4.52 us
    another operation x3, other arithmetic, solve_and_place(): factor = jnp.linalg.cholesky(matrix)  2.13 us
    another operation x2, other arithmetic, solve_and_place(): lax.linalg.triangular_solve(factor, middle, left_side=True, lower=True, t...  1.88 us
  transfers between devices with their start and end apart: 23, of which 12 were waited for; matrix products, arithmetic and copies ran while one was open for 20% of the time, Pallas kernels for 0%

profile of v1, /device:TPU:0, one launch (start us, length us, event | category | flops | bytes accessed | tf_op | source)
XLA Modules:
  0.0 53.8 jit_solution(9792025238061944799)
XLA Ops:
  0.0 2.9 %collective-permute-start = (bf16[1792,64]{0,1:T(8,128)(2,1)}, bf16[1792,64]{0,1:T(8,128)(2,1)S(1)}, u32[]{:S(2)}, u32[]{:S(2)}) collective-permute-start(bf16[1792,64]{0,1:T(8,128)(2,1)} %param.14), channel_id=1, source_target_pairs={{0,2},{1,5},{2,0},{3,7},{4,6},{5,1},{6,4},{7,3},{8,10},{9,13},{10,... | collective-permute-start | bytes 688136 | tf_op jit(solution)/shard_map/ppermute | solution.py:50
  2.9 1.5 %collective-permute-start.1 = (bf16[1792,64]{0,1:T(8,128)(2,1)}, bf16[1792,64]{0,1:T(8,128)(2,1)S(1)}, u32[]{:S(2)}, u32[]{:S(2)}) collective-permute-start(bf16[1792,64]{0,1:T(8,128)(2,1)} %param.14), channel_id=1, source_target_pairs={{0,4},{1,3},{2,6},{3,1},{4,0},{5,7},{6,2},{7,5},{8,12},{9,11},{10,... | collective-permute-start | bytes 688136 | tf_op jit(solution)/shard_map/ppermute | solution.py:50
  6.5 1.3 %fusion.15 = f32[128,64]{0,1:T(8,128)S(1)} fusion(bf16[1792,64]{0,1:T(8,128)(2,1)} %param.14, bf16[1,128,14336]{2,1,0:T(8,128)(2,1)} %param.9, s32[]{:T(128)S(6)} %select_n.89), kind=kOutput, calls=%fused_computation.26 | convolution fusion | flops 29360128 | bytes 720900 | tf_op jit(solution)/shard_map/dot_general | solution.py:72
  7.9 1.0 %fusion.36 = f32[128,64]{0,1:T(8,128)S(1)} fusion(bf16[512,64]{0,1:T(8,128)(2,1)} %param.13, bf16[1,128,4096]{2,1,0:T(8,128)(2,1)S(1)} %copy-done, s32[]{:T(128)S(6)} %select_n.97), kind=kOutput, calls=%fused_computation.48 | convolution fusion | flops 8388608 | bytes 229380 | tf_op jit(solution)/shard_map/dot_general | solution.py:72
  9.1 1.4 %collective-permute-done.7 = bf16[512,64]{0,1:T(8,128)(2,1)S(1)} collective-permute-done((bf16[512,64]{0,1:T(8,128)(2,1)}, bf16[512,64]{0,1:T(8,128)(2,1)S(1)}, u32[]{:S(2)}, u32[]{:S(2)}) %collective-permute-start.7) | collective-permute-done | bytes 65568 | tf_op jit(solution)/shard_map/ppermute | solution.py:50
  10.7 1.5 %collective-permute-start.9 = (bf16[512,64]{0,1:T(8,128)(2,1)S(1)}, bf16[512,64]{0,1:T(8,128)(2,1)S(1)}, u32[]{:S(2)}, u32[]{:S(2)}) collective-permute-start(bf16[512,64]{0,1:T(8,128)(2,1)S(1)} %collective-permute-done.7), channel_id=1, source_target_pairs={{0,4},{1,3},{2,6},{3,1},{4,0},{5,7},{6,2},{7,5},{8,12},{9,11},{10,... | collective-permute-start | bytes 196616 | tf_op jit(solution)/shard_map/ppermute | solution.py:50
  12.4 1.2 %collective-permute-start.12 = (bf16[512,64]{0,1:T(8,128)(2,1)S(1)}, bf16[512,64]{0,1:T(8,128)(2,1)S(1)}, u32[]{:S(2)}, u32[]{:S(2)}) collective-permute-start(bf16[512,64]{0,1:T(8,128)(2,1)S(1)} %collective-permute-done.8), channel_id=1, source_target_pairs={{0,1},{1,0},{2,3},{3,2},{4,5},{5,4},{6,7},{7,6},{8,9},{9,8},{10,11... | collective-permute-start | bytes 196616 | tf_op jit(solution)/shard_map/ppermute | solution.py:50
  13.8 1.3 %collective-permute-done.9 = bf16[512,64]{0,1:T(8,128)(2,1)S(1)} collective-permute-done((bf16[512,64]{0,1:T(8,128)(2,1)S(1)}, bf16[512,64]{0,1:T(8,128)(2,1)S(1)}, u32[]{:S(2)}, u32[]{:S(2)}) %collective-permute-start.9) | collective-permute-done | bytes 65568 | tf_op jit(solution)/shard_map/ppermute | solution.py:50
  16.9 1.5 %collective-permute-start.2 = (bf16[1792,64]{0,1:T(8,128)(2,1)S(1)}, bf16[1792,64]{0,1:T(8,128)(2,1)S(1)}, u32[]{:S(2)}, u32[]{:S(2)}) collective-permute-start(bf16[1792,64]{0,1:T(8,128)(2,1)S(1)} %collective-permute-done), channel_id=1, source_target_pairs={{0,4},{1,3},{2,6},{3,1},{4,0},{5,7},{6,2},{7,5},{8,12},{9,11},{10,... | collective-permute-start | bytes 688136 | tf_op jit(solution)/shard_map/ppermute | solution.py:50
  18.4 1.0 %collective-permute-start.4 = (bf16[1792,64]{0,1:T(8,128)(2,1)S(1)}, bf16[1792,64]{0,1:T(8,128)(2,1)S(1)}, u32[]{:S(2)}, u32[]{:S(2)}) collective-permute-start(bf16[1792,64]{0,1:T(8,128)(2,1)S(1)} %collective-permute-done), channel_id=1, source_target_pairs={{0,1},{1,0},{2,3},{3,2},{4,5},{5,4},{6,7},{7,6},{8,9},{9,8},{10,11... | collective-permute-start | bytes 688136 | tf_op jit(solution)/shard_map/ppermute | solution.py:50
  19.4 1.3 %convolution_add_fusion.9 = f32[128,64]{0,1:T(8,128)S(1)} fusion(f32[128,64]{0,1:T(8,128)S(1)} %fusion.15, bf16[1792,64]{0,1:T(8,128)(2,1)S(1)} %collective-permute-done, bf16[1,128,14336]{2,1,0:T(8,128)(2,1)} %param.9, s32[]{:T(128)S(6)} %select_n.90), kind=kOutput, calls=%fused_computation.15 | convolution fusion | flops 29368320 | bytes 753668 | tf_op jit(solution)/shard_map/dot_general | solution.py:72
  20.7 1.3 %convolution_add_fusion.8 = f32[128,64]{0,1:T(8,128)S(1)} fusion(f32[128,64]{0,1:T(8,128)S(1)} %convolution_add_fusion.9, bf16[1792,64]{0,1:T(8,128)(2,1)S(1)} %collective-permute-done.1, bf16[1,128,14336]{2,1,0:T(8,128)(2,1)} %param.9, s32[]{:T(128)S(6)} %select_n.91), kind=kOutput, calls=%fused_computation.14 | convolution fusion | flops 29368320 | bytes 753668 | tf_op jit(solution)/shard_map/dot_general | solution.py:72
  22.0 1.3 %fusion.10 = f32[128,64]{0,1:T(8,128)S(1)} fusion(bf16[1792,64]{0,1:T(8,128)(2,1)S(1)} %collective-permute-done.3, bf16[1,128,14336]{2,1,0:T(8,128)(2,1)} %param.9, s32[]{:T(128)S(6)} %select_n.93), kind=kOutput, calls=%fused_computation.21 | convolution fusion | flops 29360128 | bytes 720900 | tf_op jit(solution)/shard_map/dot_general | solution.py:72
  26.1 0.9 %collective-permute-done.14 = f32[4,32,64]{2,1,0:T(8,128)S(1)} collective-permute-done((f32[4,32,64]{2,1,0:T(8,128)S(1)}, f32[4,32,64]{2,1,0:T(8,128)S(1)}, u32[]{:S(2)}, u32[]{:S(2)}) %collective-permute-start.14) | collective-permute-done | bytes 32800 | tf_op jit(solution)/shard_map/ppermute | solution.py:50
  27.0 2.0 %collective-permute-start.15 = (f32[4,32,64]{2,1,0:T(8,128)S(1)}, f32[4,32,64]{2,1,0:T(8,128)S(1)}, u32[]{:S(2)}, u32[]{:S(2)}) collective-permute-start(f32[4,32,64]{2,1,0:T(8,128)S(1)} %bitcast_add_fusion), channel_id=1, source_target_pairs={{0,6},{1,7},{2,4},{3,5},{4,2},{5,3},{6,0},{7,1},{8,14},{9,15},{10,... | collective-permute-start | bytes 98312 | tf_op jit(solution)/shard_map/ppermute | solution.py:50
  29.4 1.2 %collective-permute-start.17 = (f32[4,32,64]{2,1,0:T(8,128)S(1)}, f32[4,32,64]{2,1,0:T(8,128)S(1)}, u32[]{:S(2)}, u32[]{:S(2)}) collective-permute-start(f32[4,32,64]{2,1,0:T(8,128)S(1)} %bitcast_add_fusion), channel_id=1, source_target_pairs={{0,4},{1,5},{2,6},{3,7},{4,0},{5,1},{6,2},{7,3},{8,12},{9,13},{10,... | collective-permute-start | bytes 98312 | tf_op jit(solution)/shard_map/ppermute | solution.py:50
  30.7 1.7 %collective-permute-done.15 = f32[4,32,64]{2,1,0:T(8,128)S(1)} collective-permute-done((f32[4,32,64]{2,1,0:T(8,128)S(1)}, f32[4,32,64]{2,1,0:T(8,128)S(1)}, u32[]{:S(2)}, u32[]{:S(2)}) %collective-permute-start.15) | collective-permute-done | bytes 32800 | tf_op jit(solution)/shard_map/ppermute | solution.py:50
  33.8 1.8 %collective-permute-start.18 = (f32[4,32,64]{2,1,0:T(8,128)S(1)}, f32[4,32,64]{2,1,0:T(8,128)S(1)}, u32[]{:S(2)}, u32[]{:S(2)}) collective-permute-start(f32[4,32,64]{2,1,0:T(8,128)S(1)} %get-tuple-element.6), channel_id=1, source_target_pairs={{0,8},{8,0},{16,24},{24,16},{1,9},{9,1},{17,25},{25,17},{2,10},{10... | collective-permute-start | bytes 98312 | tf_op jit(solution)/shard_map/ppermute | solution.py:87
  36.3 2.7 %collective-permute-start.19 = (f32[4,32,64]{2,1,0:T(8,128)S(1)}, f32[4,32,64]{2,1,0:T(8,128)S(1)}, u32[]{:S(2)}, u32[]{:S(2)}) collective-permute-start(f32[4,32,64]{2,1,0:T(8,128)S(1)} %get-tuple-element.6), channel_id=1, source_target_pairs={{0,16},{8,24},{16,0},{24,8},{1,17},{9,25},{17,1},{25,9},{2,18},{10... | collective-permute-start | bytes 98312 | tf_op jit(solution)/shard_map/ppermute | solution.py:87
  39.0 4.1 %collective-permute-done.19 = f32[4,32,64]{2,1,0:T(8,128)S(1)} collective-permute-done((f32[4,32,64]{2,1,0:T(8,128)S(1)}, f32[4,32,64]{2,1,0:T(8,128)S(1)}, u32[]{:S(2)}, u32[]{:S(2)}) %collective-permute-start.19) | collective-permute-done | bytes 32800 | tf_op jit(solution)/shard_map/ppermute | solution.py:87
  43.2 1.9 %collective-permute-done.20 = f32[4,32,64]{2,1,0:T(8,128)S(1)} collective-permute-done((f32[4,32,64]{2,1,0:T(8,128)S(1)}, f32[4,32,64]{2,1,0:T(8,128)S(1)}, u32[]{:S(2)}, u32[]{:S(2)}) %collective-permute-start.20) | collective-permute-done | bytes 32800 | tf_op jit(solution)/shard_map/ppermute | solution.py:87
  45.8 1.2 %collective-permute-done.22 = f32[16,48]{1,0:T(8,128)S(1)} collective-permute-done((f32[16,48]{1,0:T(8,128)S(1)}, f32[16,48]{1,0:T(8,128)S(1)}, u32[]{:S(2)}, u32[]{:S(2)}) %collective-permute-start.22) | collective-permute-done | bytes 3104 | tf_op jit(solution)/shard_map/ppermute | solution.py:50
  48.4 1.5 %cholesky.17 = f32[16,16]{1,0:T(8,128)S(1)} custom-call(f32[16,16]{1,0:T(8,128)S(1)} %fusion.55), custom_call_target="Cholesky" | custom-call | tf_op jit(solution)/shard_map/jit(cholesky)/cholesky | solution.py:22
  51.2 1.2 %custom-call.8 = f32[1,16,16]{1,2,0:T(8,128)S(1)} custom-call(f32[1,16,16]{2,1,0:T(8,128)S(1)} %fusion.50), custom_call_target="InvertDiagBlocksLowerTriangular" | custom-call | tf_op jit(solution)/shard_map/triangular_solve | solution.py:24
  (79 shorter events, 14.1 us)
Async XLA Ops:
  0.0 16.9 %collective-permute-start = (bf16[1792,64]{0,1:T(8,128)(2,1)}, bf16[1792,64]{0,1:T(8,128)(2,1)S(1)}, u32[]{:S(2)}, u32[]{:S(2)}) collective-permute-start(bf16[1792,64]{0,1:T(8,128)(2,1)} %param.14), channel_id=1, source_target_pairs={{0,2},{1,5},{2,0},{3,7},{4,6},{5,1},{6,4},{7,3},{8,10},{9,13},{10,... | collective-permute-start | bytes 688136 | tf_op jit(solution)/shard_map/ppermute | solution.py:50
  2.9 16.5 %collective-permute-start.1 = (bf16[1792,64]{0,1:T(8,128)(2,1)}, bf16[1792,64]{0,1:T(8,128)(2,1)S(1)}, u32[]{:S(2)}, u32[]{:S(2)}) collective-permute-start(bf16[1792,64]{0,1:T(8,128)(2,1)} %param.14), channel_id=1, source_target_pairs={{0,4},{1,3},{2,6},{3,1},{4,0},{5,7},{6,2},{7,5},{8,12},{9,11},{10,... | collective-permute-start | bytes 688136 | tf_op jit(solution)/shard_map/ppermute | solution.py:50
  4.5 17.6 %collective-permute-start.3 = (bf16[1792,64]{0,1:T(8,128)(2,1)}, bf16[1792,64]{0,1:T(8,128)(2,1)S(1)}, u32[]{:S(2)}, u32[]{:S(2)}) collective-permute-start(bf16[1792,64]{0,1:T(8,128)(2,1)} %param.14), channel_id=1, source_target_pairs={{0,1},{1,0},{2,3},{3,2},{4,5},{5,4},{6,7},{7,6},{8,9},{9,8},{10,11... | collective-permute-start | bytes 688136 | tf_op jit(solution)/shard_map/ppermute | solution.py:50
  4.5 6.1 %collective-permute-start.7 = (bf16[512,64]{0,1:T(8,128)(2,1)}, bf16[512,64]{0,1:T(8,128)(2,1)S(1)}, u32[]{:S(2)}, u32[]{:S(2)}) collective-permute-start(bf16[512,64]{0,1:T(8,128)(2,1)} %param.13), channel_id=1, source_target_pairs={{0,2},{1,5},{2,0},{3,7},{4,6},{5,1},{6,4},{7,3},{8,10},{9,13},{10,... | collective-permute-start | bytes 196616 | tf_op jit(solution)/shard_map/ppermute | solution.py:50
  5.0 5.7 %collective-permute-start.8 = (bf16[512,64]{0,1:T(8,128)(2,1)}, bf16[512,64]{0,1:T(8,128)(2,1)S(1)}, u32[]{:S(2)}, u32[]{:S(2)}) collective-permute-start(bf16[512,64]{0,1:T(8,128)(2,1)} %param.13), channel_id=1, source_target_pairs={{0,4},{1,3},{2,6},{3,1},{4,0},{5,7},{6,2},{7,5},{8,12},{9,11},{10,... | collective-permute-start | bytes 196616 | tf_op jit(solution)/shard_map/ppermute | solution.py:50
  10.6 1.9 %collective-permute-start.10 = (bf16[512,64]{0,1:T(8,128)(2,1)}, bf16[512,64]{0,1:T(8,128)(2,1)S(1)}, u32[]{:S(2)}, u32[]{:S(2)}) collective-permute-start(bf16[512,64]{0,1:T(8,128)(2,1)} %param.13), channel_id=1, source_target_pairs={{0,1},{1,0},{2,3},{3,2},{4,5},{5,4},{6,7},{7,6},{8,9},{9,8},{10,11... | collective-permute-start | bytes 196616 | tf_op jit(solution)/shard_map/ppermute | solution.py:50
  10.7 4.3 %collective-permute-start.9 = (bf16[512,64]{0,1:T(8,128)(2,1)S(1)}, bf16[512,64]{0,1:T(8,128)(2,1)S(1)}, u32[]{:S(2)}, u32[]{:S(2)}) collective-permute-start(bf16[512,64]{0,1:T(8,128)(2,1)S(1)} %collective-permute-done.7), channel_id=1, source_target_pairs={{0,4},{1,3},{2,6},{3,1},{4,0},{5,7},{6,2},{7,5},{8,12},{9,11},{10,... | collective-permute-start | bytes 196616 | tf_op jit(solution)/shard_map/ppermute | solution.py:50
  12.4 2.9 %collective-permute-start.12 = (bf16[512,64]{0,1:T(8,128)(2,1)S(1)}, bf16[512,64]{0,1:T(8,128)(2,1)S(1)}, u32[]{:S(2)}, u32[]{:S(2)}) collective-permute-start(bf16[512,64]{0,1:T(8,128)(2,1)S(1)} %collective-permute-done.8), channel_id=1, source_target_pairs={{0,1},{1,0},{2,3},{3,2},{4,5},{5,4},{6,7},{7,6},{8,9},{9,8},{10,11... | collective-permute-start | bytes 196616 | tf_op jit(solution)/shard_map/ppermute | solution.py:50
  15.1 1.3 %collective-permute-start.11 = (bf16[512,64]{0,1:T(8,128)(2,1)S(1)}, bf16[512,64]{0,1:T(8,128)(2,1)S(1)}, u32[]{:S(2)}, u32[]{:S(2)}) collective-permute-start(bf16[512,64]{0,1:T(8,128)(2,1)S(1)} %collective-permute-done.7), channel_id=1, source_target_pairs={{0,1},{1,0},{2,3},{3,2},{4,5},{5,4},{6,7},{7,6},{8,9},{9,8},{10,11... | collective-permute-start | bytes 196616 | tf_op jit(solution)/shard_map/ppermute | solution.py:50
  15.4 1.4 %collective-permute-start.13 = (bf16[512,64]{0,1:T(8,128)(2,1)S(1)}, bf16[512,64]{0,1:T(8,128)(2,1)S(1)}, u32[]{:S(2)}, u32[]{:S(2)}) collective-permute-start(bf16[512,64]{0,1:T(8,128)(2,1)S(1)} %collective-permute-done.9), channel_id=1, source_target_pairs={{0,1},{1,0},{2,3},{3,2},{4,5},{5,4},{6,7},{7,6},{8,9},{9,8},{10,11... | collective-permute-start | bytes 196616 | tf_op jit(solution)/shard_map/ppermute | solution.py:50
  16.9 6.4 %collective-permute-start.2 = (bf16[1792,64]{0,1:T(8,128)(2,1)S(1)}, bf16[1792,64]{0,1:T(8,128)(2,1)S(1)}, u32[]{:S(2)}, u32[]{:S(2)}) collective-permute-start(bf16[1792,64]{0,1:T(8,128)(2,1)S(1)} %collective-permute-done), channel_id=1, source_target_pairs={{0,4},{1,3},{2,6},{3,1},{4,0},{5,7},{6,2},{7,5},{8,12},{9,11},{10,... | collective-permute-start | bytes 688136 | tf_op jit(solution)/shard_map/ppermute | solution.py:50
  18.4 6.1 %collective-permute-start.4 = (bf16[1792,64]{0,1:T(8,128)(2,1)S(1)}, bf16[1792,64]{0,1:T(8,128)(2,1)S(1)}, u32[]{:S(2)}, u32[]{:S(2)}) collective-permute-start(bf16[1792,64]{0,1:T(8,128)(2,1)S(1)} %collective-permute-done), channel_id=1, source_target_pairs={{0,1},{1,0},{2,3},{3,2},{4,5},{5,4},{6,7},{7,6},{8,9},{9,8},{10,11... | collective-permute-start | bytes 688136 | tf_op jit(solution)/shard_map/ppermute | solution.py:50
  19.4 4.8 %collective-permute-start.5 = (bf16[1792,64]{0,1:T(8,128)(2,1)S(1)}, bf16[1792,64]{0,1:T(8,128)(2,1)S(1)}, u32[]{:S(2)}, u32[]{:S(2)}) collective-permute-start(bf16[1792,64]{0,1:T(8,128)(2,1)S(1)} %collective-permute-done.1), channel_id=1, source_target_pairs={{0,1},{1,0},{2,3},{3,2},{4,5},{5,4},{6,7},{7,6},{8,9},{9,8},{10,11... | collective-permute-start | bytes 688136 | tf_op jit(solution)/shard_map/ppermute | solution.py:50
  23.4 1.7 %collective-permute-start.6 = (bf16[1792,64]{0,1:T(8,128)(2,1)S(1)}, bf16[1792,64]{0,1:T(8,128)(2,1)S(1)}, u32[]{:S(2)}, u32[]{:S(2)}) collective-permute-start(bf16[1792,64]{0,1:T(8,128)(2,1)S(1)} %collective-permute-done.2), channel_id=1, source_target_pairs={{0,1},{1,0},{2,3},{3,2},{4,5},{5,4},{6,7},{7,6},{8,9},{9,8},{10,11... | collective-permute-start | bytes 688136 | tf_op jit(solution)/shard_map/ppermute | solution.py:50
  24.2 28.8 %copy-start.3 = (s32[16]{0:T(128)S(1)}, s32[16]{0:T(128)}, u32[]{:S(2)}) copy-start(s32[16]{0:T(128)} %param.12) | copy-start | bytes 196
  25.6 1.3 %collective-permute-start.14 = (f32[4,32,64]{2,1,0:T(8,128)S(1)}, f32[4,32,64]{2,1,0:T(8,128)S(1)}, u32[]{:S(2)}, u32[]{:S(2)}) collective-permute-start(f32[4,32,64]{2,1,0:T(8,128)S(1)} %dynamic-slice_bitcast_fusion), channel_id=1, source_target_pairs={{0,1},{1,0},{2,3},{3,2},{4,5},{5,4},{6,7},{7,6},{8,9},{9,8},{10,11... | collective-permute-start | bytes 98312 | tf_op jit(solution)/shard_map/ppermute | solution.py:50
  27.0 5.5 %collective-permute-start.15 = (f32[4,32,64]{2,1,0:T(8,128)S(1)}, f32[4,32,64]{2,1,0:T(8,128)S(1)}, u32[]{:S(2)}, u32[]{:S(2)}) collective-permute-start(f32[4,32,64]{2,1,0:T(8,128)S(1)} %bitcast_add_fusion), channel_id=1, source_target_pairs={{0,6},{1,7},{2,4},{3,5},{4,2},{5,3},{6,0},{7,1},{8,14},{9,15},{10,... | collective-permute-start | bytes 98312 | tf_op jit(solution)/shard_map/ppermute | solution.py:50
  29.0 4.3 %collective-permute-start.16 = (f32[4,32,64]{2,1,0:T(8,128)S(1)}, f32[4,32,64]{2,1,0:T(8,128)S(1)}, u32[]{:S(2)}, u32[]{:S(2)}) collective-permute-start(f32[4,32,64]{2,1,0:T(8,128)S(1)} %bitcast_add_fusion), channel_id=1, source_target_pairs={{0,2},{1,3},{2,0},{3,1},{4,6},{5,7},{6,4},{7,5},{8,10},{9,11},{10,... | collective-permute-start | bytes 98312 | tf_op jit(solution)/shard_map/ppermute | solution.py:50
  29.4 4.3 %collective-permute-start.17 = (f32[4,32,64]{2,1,0:T(8,128)S(1)}, f32[4,32,64]{2,1,0:T(8,128)S(1)}, u32[]{:S(2)}, u32[]{:S(2)}) collective-permute-start(f32[4,32,64]{2,1,0:T(8,128)S(1)} %bitcast_add_fusion), channel_id=1, source_target_pairs={{0,4},{1,5},{2,6},{3,7},{4,0},{5,1},{6,2},{7,3},{8,12},{9,13},{10,... | collective-permute-start | bytes 98312 | tf_op jit(solution)/shard_map/ppermute | solution.py:50
  33.8 5.3 %collective-permute-start.18 = (f32[4,32,64]{2,1,0:T(8,128)S(1)}, f32[4,32,64]{2,1,0:T(8,128)S(1)}, u32[]{:S(2)}, u32[]{:S(2)}) collective-permute-start(f32[4,32,64]{2,1,0:T(8,128)S(1)} %get-tuple-element.6), channel_id=1, source_target_pairs={{0,8},{8,0},{16,24},{24,16},{1,9},{9,1},{17,25},{25,17},{2,10},{10... | collective-permute-start | bytes 98312 | tf_op jit(solution)/shard_map/ppermute | solution.py:87
  36.2 9.2 %collective-permute-start.21 = (bf16[32,2048]{1,0:T(8,128)(2,1)S(1)}, bf16[32,2048]{1,0:T(8,128)(2,1)S(1)}, u32[]{:S(2)}, u32[]{:S(2)}) collective-permute-start(bf16[32,2048]{1,0:T(8,128)(2,1)S(1)} %bitcast.115), channel_id=1, source_target_pairs={{0,1},{1,0},{2,3},{3,2},{4,5},{5,4},{6,7},{7,6},{8,9},{9,8},{10,11... | collective-permute-start | bytes 393224 | tf_op jit(solution)/shard_map/ppermute | solution.py:50
  36.3 6.9 %collective-permute-start.19 = (f32[4,32,64]{2,1,0:T(8,128)S(1)}, f32[4,32,64]{2,1,0:T(8,128)S(1)}, u32[]{:S(2)}, u32[]{:S(2)}) collective-permute-start(f32[4,32,64]{2,1,0:T(8,128)S(1)} %get-tuple-element.6), channel_id=1, source_target_pairs={{0,16},{8,24},{16,0},{24,8},{1,17},{9,25},{17,1},{25,9},{2,18},{10... | collective-permute-start | bytes 98312 | tf_op jit(solution)/shard_map/ppermute | solution.py:87
  38.9 6.1 %collective-permute-start.20 = (f32[4,32,64]{2,1,0:T(8,128)S(1)}, f32[4,32,64]{2,1,0:T(8,128)S(1)}, u32[]{:S(2)}, u32[]{:S(2)}) collective-permute-start(f32[4,32,64]{2,1,0:T(8,128)S(1)} %get-tuple-element.6), channel_id=1, source_target_pairs={{0,24},{8,16},{16,8},{24,0},{1,25},{9,17},{17,9},{25,1},{2,26},{10... | collective-permute-start | bytes 98312 | tf_op jit(solution)/shard_map/ppermute | solution.py:87
  45.8 1.2 %collective-permute-start.22 = (f32[16,48]{1,0:T(8,128)S(1)}, f32[16,48]{1,0:T(8,128)S(1)}, u32[]{:S(2)}, u32[]{:S(2)}) collective-permute-start(f32[16,48]{1,0:T(8,128)S(1)} %pad_maximum_fusion), channel_id=1, source_target_pairs={{0,1},{1,0},{2,3},{3,2},{4,5},{5,4},{6,7},{7,6},{8,9},{9,8},{10,11... | collective-permute-start | bytes 9224 | tf_op jit(solution)/shard_map/ppermute | solution.py:50
  (3 other events, 42.6 us)

commit v2 on v0

v2 whole, which is shorter than its diff:
```python
import functools

import jax
import jax.numpy as jnp
from jax import lax
from jax.experimental import pallas as pl
from jax.experimental.pallas import tpu as pltpu
from jax.sharding import PartitionSpec as P

BLOCK = 128
HIGH = lax.Precision.HIGHEST
F32 = jnp.float32
VMEM = pltpu.VMEM
LIMIT = 16 * 1024 * 1024


def any_mesh(inputs, out_grads, valid, doc_blocks, doc_ids, proj_in, proj_out, test_grads):
    px = jnp.dot(inputs[0], lax.all_gather(proj_in, "seq", tiled=True), preferred_element_type=F32)
    pg = jnp.dot(out_grads[0], lax.all_gather(proj_out, "seq", tiled=True), preferred_element_type=F32)
    slots = px.shape[0]
    ends = jnp.cumsum(doc_blocks[0])
    position = lax.axis_index("seq") * slots + jnp.arange(slots, dtype=jnp.int32)
    owner = jnp.sum((position // BLOCK)[:, None] >= ends[None, :], axis=1)
    mine = owner[None, :] == jnp.arange(ends.shape[0])[:, None]
    weights = (mine & (valid[0][None, :] == 1)).astype(F32)
    weighted = weights[:, None, :] * pg.T[None, :, :]
    grads = jnp.einsum("jat,tb->jab", weighted, px, precision=HIGH)
    grads = lax.psum(grads.reshape(grads.shape[0], -1), "seq")
    grads = lax.all_gather(grads, "dp", tiled=True)
    gram = jnp.dot(grads, grads.T, precision=HIGH)
    cross = jnp.dot(grads, test_grads.astype(F32).T, precision=HIGH)
    ndocs = gram.shape[0]
    damp = 0.1 * jnp.trace(gram) / ndocs
    factor = jnp.linalg.cholesky(gram / ndocs + damp * jnp.eye(ndocs, dtype=F32))
    middle = lax.linalg.triangular_solve(factor, cross, left_side=True, lower=True)
    solved = lax.linalg.triangular_solve(factor, middle, left_side=True, lower=True, transpose_a=True)
    placing = (doc_ids[None, :] == jnp.arange(ndocs, dtype=jnp.int32)[:, None]).astype(F32)
    return jnp.dot(placing, solved, precision=HIGH)


def place(seq, dp):
    bits = seq ^ (seq >> 1) ^ (seq >> 2) ^ dp ^ (dp >> 1)
    return bits & 1


def here():
    seq, dp = lax.axis_index("seq"), lax.axis_index("dp")
    return seq, dp, place(seq, dp)


def in_vmem(*arrays):
    return [pltpu.with_memory_space_constraint(x, VMEM) for x in arrays]


def vmem_call(body, outs, args, hbm=(), scratch=(), name=None, moved=0):
    specs = [pl.BlockSpec(memory_space=VMEM)] * len(args) + [pl.BlockSpec(memory_space=pltpu.HBM)] * len(hbm)
    far = [pltpu.with_memory_space_constraint(x, pltpu.HBM) for x in hbm]
    return pl.pallas_call(
        body,
        out_shape=[VMEM(s, d) for s, d in outs],
        in_specs=specs,
        out_specs=[pl.BlockSpec(memory_space=VMEM)] * len(outs),
        scratch_shapes=list(scratch),
        name=name,
        compiler_params=pltpu.CompilerParams(vmem_limit_bytes=LIMIT),
        cost_estimate=pl.CostEstimate(flops=0, transcendentals=0, bytes_accessed=moved),
    )(*in_vmem(*args), *far)


def source(seq, slot):
    even, odd = ((0, 0), (5, 3), (3, 5), (6, 6))[slot]
    return seq ^ jnp.where(seq & 1 == 0, even, odd)


def weights_body(valid, blocks, out_t, in_t, first, second, weights, valid_v, blocks_s, sems):
    seq, _, _ = here()
    rows_out, rows_in, size = out_t.shape[1], in_t.shape[1], first.shape[1]
    rest = rows_out - size
    copies = [
        pltpu.make_async_copy(out_t.at[:, pl.ds(0, size)], first, sems.at[0]),
        pltpu.make_async_copy(out_t.at[:, pl.ds(size, rest)], second.at[:, pl.ds(0, rest)], sems.at[1]),
        pltpu.make_async_copy(in_t, second.at[:, pl.ds(rest, rows_in)], sems.at[2]),
        pltpu.make_async_copy(valid, valid_v, sems.at[3]),
        pltpu.make_async_copy(blocks, blocks_s, sems.at[4]),
    ]
    for c in copies:
        c.start()
    for c in copies:
        c.wait()
    slots = valid.shape[1]
    blk = (seq * slots + lax.broadcasted_iota(jnp.int32, weights.shape, 1)) // BLOCK
    row = lax.broadcasted_iota(jnp.int32, weights.shape, 0)
    owner = jnp.zeros_like(blk)
    end = 0
    for j in range(blocks.shape[1]):
        end = end + blocks_s[0, j]
        owner = owner + (blk >= end).astype(jnp.int32)
    weights[...] = jnp.where((owner == row) & (valid_v[...] == 1), 1.0, 0.0)


def column_copies(og, inp, out, mine, sems):
    nseq = lax.axis_size("seq")
    wo, wi = og.shape[1] // nseq, inp.shape[1] // nseq
    copies = []
    for k in range(4):
        shard = source(mine, k)
        base = k * (wo + wi)
        copies.append(pltpu.make_async_copy(
            og.at[:, pl.ds(pl.multiple_of(shard * wo, wo), wo)], out.at[:, pl.ds(base, wo)], sems.at[2 * k]))
        copies.append(pltpu.make_async_copy(
            inp.at[:, pl.ds(pl.multiple_of(shard * wi, wi), wi)], out.at[:, pl.ds(base + wo, wi)], sems.at[2 * k + 1]))
    return copies


def send_body(_, og, inp, send, sems):
    seq, _, _ = here()
    copies = column_copies(og, inp, send, seq ^ 1, sems)
    for c in copies:
        c.start()
    for c in copies:
        c.wait()


def keep_body(_, og, inp, tests, ids, keep, t_own, t_far, rows, ids_s, sems):
    seq, _, half = here()
    hf = t_own.shape[1]
    copies = column_copies(og, inp, keep, seq, sems)
    copies.append(pltpu.make_async_copy(tests.at[:, pl.ds(pl.multiple_of(half * hf, hf), hf)], t_own, sems.at[8]))
    copies.append(pltpu.make_async_copy(tests.at[:, pl.ds(pl.multiple_of((1 - half) * hf, hf), hf)], t_far, sems.at[9]))
    copies.append(pltpu.make_async_copy(ids, ids_s, sems.at[10]))
    for c in copies:
        c.start()
    for c in copies:
        c.wait()
    for r in range(rows.shape[0]):
        rows[r:r + 1, :] = jnp.full((1, rows.shape[1]), ids_s[r], jnp.int32)


def nt(a, b, precision=None):
    return lax.dot_general(a, b, (((1,), (1,)), ((), ())), precision=precision, preferred_element_type=F32)


def project(w, near, far, base):
    cols = pl.ds(base, w.shape[1])
    return nt(w, jnp.concatenate([near[:, cols], far[:, cols]], axis=0))


def near_body(w1, w2, a1, a2, b1, b2, near, far, pg, px, *, wi):
    size = w1.shape[1]
    rest = w2.shape[1] - wi
    total, total_x = 0.0, 0.0
    for k, (x, y) in enumerate(((w1, w2), (a1, a2), (b1, b2))):
        base = k * (size + rest + wi)
        total = total + project(x[...], near, far, base)
        total = total + project(y[:, :rest], near, far, base + size)
        total_x = total_x + project(y[:, rest:], near, far, base + size + rest)
    pg[...] = total
    px[...] = total_x


def diagonal_body(c1, pg_in, near, far, pg):
    base = near.shape[1] // 4 * 3
    pg[...] = pg_in[...] + project(c1[...], near, far, base)


def last_body(c2, pg_in, px_in, near, far, out, *, wi):
    base = near.shape[1] - c2.shape[1]
    rest = c2.shape[1] - wi
    rows = pg_in.shape[0]
    out[:rows] = pg_in[...] + project(c2[:, :rest], near, far, base)
    out[rows:2 * rows] = px_in[...] + project(c2[:, rest:], near, far, base + rest)


def grads_body(mine, far, weights, weights2, grads, pgs):
    _, _, half = here()
    slots = pgs.shape[2]
    rows = mine.shape[0] // 2
    hw = rows // 2
    pairs = hw // 2
    docs = grads.shape[0] // pairs
    both = []
    for base in (0, rows):
        block = pl.ds(base, rows)
        both.append([mine[block, :slots] + far[block, slots:], mine[block, slots:] + far[block, :slots]])
    for u in range(2):
        pgs[u] = jnp.where(half == 1, both[0][u][hw:], both[0][u][:hw])
    px = jnp.concatenate(both[1], axis=1)
    tokens = jnp.concatenate([weights[...], weights2[...]], axis=1)
    parts = []
    for q in range(2):
        some = jnp.concatenate([pgs[u, pl.ds(q, pairs, stride=2), :] for u in range(2)], axis=1)
        weighted = jnp.concatenate([some * tokens[j:j + 1, :] for j in range(docs)], axis=0)
        parts.append(nt(weighted, px, HIGH))
    grads[...] = jnp.concatenate(parts, axis=1)


def products_body(m0, m1, m2, m3, t_own, t_far, out, every):
    seq, dp, _ = here()
    rows = m0.shape[0]
    for k, m in enumerate((m0, m1, m2, m3)):
        every[pl.ds(pl.multiple_of((dp ^ k) * rows, rows), rows), :] = m[...]
    docs = out.shape[0]
    pairs = every.shape[0] // docs
    flat = jnp.concatenate([every[pl.ds(i, docs, stride=pairs), :] for i in range(pairs)], axis=1)
    gram = nt(flat, flat, HIGH)
    own, far = t_own[...], t_far[...]
    core = seq & 1
    tests = jnp.concatenate([jnp.where(core == 0, own, far), jnp.where(core == 0, far, own)], axis=0)
    high = flat.astype(jnp.bfloat16)
    rest = flat - high.astype(F32)
    mid = rest.astype(jnp.bfloat16)
    low = (rest - mid.astype(F32)).astype(jnp.bfloat16)
    cross = nt(low, tests) + nt(mid, tests) + nt(high, tests)
    pad = jnp.zeros((docs, out.shape[1] - cross.shape[1] - docs), F32)
    out[...] = jnp.concatenate([cross, gram, pad], axis=1)


def solve_body(mine, far, rows, out):
    docs, tests = out.shape
    seq, _, _ = here()
    both = mine[...] + far[...]
    shape = both.shape
    row = lax.broadcasted_iota(jnp.int32, shape, 0)
    columns = [jnp.broadcast_to(both[:, 2 * tests + k:2 * tests + k + 1], shape) for k in range(docs)]
    trace = columns[0][0:1, :]
    for k in range(1, docs):
        trace = trace + columns[k][k:k + 1, :]
    damp = 0.1 * trace / docs
    columns = [c / docs + jnp.where(row == k, damp, 0.0) for k, c in enumerate(columns)]
    scale = jnp.zeros(shape, F32)
    for k in range(docs):
        inverse = 1.0 / columns[k][k:k + 1, :]
        scale = jnp.where(row == k, inverse, scale)
        factor = jnp.where(row == k, 0.0, columns[k] * inverse)
        both = both - factor * both[k:k + 1, :]
        for j in range(k + 1, docs):
            columns[j] = columns[j] - factor * columns[j][k:k + 1, :]
    solved = both * scale
    placed = jnp.zeros(shape, F32)
    for r in range(docs):
        placed = jnp.where(row == rows[r:r + 1, :], solved[r:r + 1, :], placed)
    out[...] = jnp.where(seq & 1 == 0, placed[:, :tests], placed[:, tests:2 * tests])


def paired_chips(inputs, out_grads, valid, doc_blocks, doc_ids, proj_in, proj_out, test_grads):
    ndp, nseq = lax.axis_size("dp"), lax.axis_size("seq")
    docs = doc_blocks.shape[1]
    ndocs = docs * ndp
    inp, og = inputs[0], out_grads[0]
    width = proj_out.shape[1]
    hw = width // 2
    wo, wi = proj_out.shape[0], proj_in.shape[0]
    slots = og.shape[0]
    ntest, feat = test_grads.shape
    bf = jnp.bfloat16

    def move(x, to):
        pairs = [(z * nseq + s, (lambda t: t[0] * nseq + t[1])(to(z, s))) for z in range(ndp) for s in range(nseq)]
        return lax.ppermute(x, ("dp", "seq"), pairs)

    def swap(x):
        return move(x, lambda z, s: (z, s ^ 1))

    def ring(x, step):
        return move(x, lambda z, s: (z, s ^ ((3, 5)[(s & 1) ^ step])))

    size = (wo + wi) // 256 * 128
    first, second, weights = vmem_call(
        weights_body,
        [((width, size), bf), ((width, wo + wi - size), bf), ((8, slots), F32)],
        [], hbm=[valid, doc_blocks, proj_out.T, proj_in.T],
        scratch=[VMEM((1, slots), jnp.int32), pltpu.SMEM((1, docs), jnp.int32), pltpu.SemaphoreType.DMA((5,))],
        name="weights",
    )
    a1, b1 = ring(first, 0), ring(first, 1)
    a2, b2 = ring(second, 0), ring(second, 1)
    weights2 = swap(weights)
    (tokens,) = vmem_call(
        send_body, [((slots, 4 * (wo + wi)), bf)], [weights], hbm=[og, inp],
        scratch=[pltpu.SemaphoreType.DMA((8,))], name="send", moved=1 * slots * (wo + wi) * 16,
    )
    far = swap(tokens)
    near, t_own, t_send, rows = vmem_call(
        keep_body, [((slots, 4 * (wo + wi)), bf)] + [((ntest, feat // 2), bf)] * 2 + [((ndocs, -(-(2 * ntest + ndocs) // 128) * 128), jnp.int32)],
        [tokens], hbm=[og, inp, test_grads, doc_ids],
        scratch=[pltpu.SMEM((ndocs,), jnp.int32), pltpu.SemaphoreType.DMA((11,))], name="keep", moved=1 * slots * (wo + wi) * 16,
    )
    t_far = swap(t_send)
    c1 = ring(a1, 0)
    c2 = ring(a2, 0)
    part = ((width, 2 * slots), F32)
    pg, px = vmem_call(
        functools.partial(near_body, wi=wi), [part, part],
        [first, second, a1, a2, b1, b2, near, far], name="near",
    )
    (pg,) = vmem_call(diagonal_body, [part], [c1, pg, near, far], name="diagonal")
    (mine,) = vmem_call(
        functools.partial(last_body, wi=wi), [((2 * width, 2 * slots), F32)],
        [c2, pg, px, near, far], name="last",
    )
    pairs = hw // 2
    (grads,) = vmem_call(
        grads_body, [((docs * pairs, 2 * width), F32)], [mine, swap(mine), weights, weights2],
        scratch=[VMEM((2, hw, slots), F32)], name="grads",
    )
    grads = (grads + move(grads, lambda z, s: (z, s ^ 3))) + (
        move(grads, lambda z, s: (z, s ^ 5)) + move(grads, lambda z, s: (z, s ^ 6)))
    m1 = move(grads, lambda z, s: (z ^ 1, s ^ 1))
    m2 = move(grads, lambda z, s: (z ^ 2, s ^ 1))
    m3 = move(grads, lambda z, s: (z ^ 3, s))
    lanes = -(-(2 * ntest + ndocs) // 128) * 128
    (mine,) = vmem_call(
        products_body, [((ndocs, lanes), F32)],
        [grads, m1, m2, m3, t_own, t_far],
        scratch=[VMEM((ndp * docs * pairs, 2 * width), F32)], name="products",
    )
    return pl.pallas_call(
        solve_body,
        out_shape=jax.ShapeDtypeStruct((ndocs, ntest), F32),
        in_specs=[pl.BlockSpec(memory_space=VMEM)] * 3,
        out_specs=pl.BlockSpec(memory_space=VMEM),
        name="solve",
    )(*in_vmem(mine, swap(mine), rows))


def solution(mesh):
    in_specs = (
        P("dp", "seq", None),
        P("dp", "seq", None),
        P("dp", "seq"),
        P("dp", None),
        P(),
        P("seq", None),
        P("seq", None),
        P("seq", None),
    )
    fast = mesh.shape["seq"] == 8 and mesh.shape["dp"] == 4
    return jax.shard_map(
        paired_chips if fast else any_mesh,
        mesh=mesh, in_specs=in_specs, out_specs=P(None, "seq"), check_vma=False,
    )
```

time: 125 us -> 39.7 us (0.32)
  waiting for transfers between devices: 71.1 us -> 13 us
  blocking collectives: 25.7 us -> 0 us
  starting transfers between devices: 0.04 us -> 18.3 us
  between operations: 14.2 us -> 0.12 us
  Pallas kernels: 0 us -> 8.09 us
  matrix products: 7.23 us -> 0 us
  other arithmetic: 5.62 us -> 0.01 us
    psum x1 -> x0, waiting for transfers between devices: 52.6 us -> none  [per_device(): group_grads = lax.psum(partial_grads, 'seq')]
    all_gather x2 -> x0, blocking collectives: 25.7 us -> none  [the longest x1 14.1 us: per_device(): doc_grads = lax.all_gather(group_grads, 'dp', axis=0, tiled=True)]
    ppermute x0 -> x17, starting transfers between devices: none -> 18.3 us  [move(): return lax.ppermute(x, ('dp', 'seq'), pairs)]
    all_gather x1 -> x0, waiting for transfers between devices: 17.7 us -> none  [per_device(): lax.all_gather(proj_out, 'seq', axis=0, tiled=True)]
    ppermute x0 -> x17, waiting for transfers between devices: none -> 13 us  [move(): return lax.ppermute(x, ('dp', 'seq'), pairs)]
    pallas_call x0 -> x9, Pallas kernels: none -> 8.09 us  [the longest x8 7.14 us: vmem_call(): pl.pallas_call(body, out_shape=[VMEM(s, d) for s, d in outs], in_specs=sp...]
    dot_general x6 -> x0, matrix products: 6.88 us -> none  [the longest x1 3.99 us: per_device(): jnp.dot(columns, lax.all_gather(proj_out, 'seq', axis=0, tiled=True), pre...]
    another operation x6 -> x0, other arithmetic: 4.83 us -> none  [the longest x3 2.12 us: per_device(): factor = jnp.linalg.cholesky(matrix)]
  transfers between devices with their start and end apart: 2 -> 17, of which waited for: 2 -> 7; matrix products, arithmetic and copies ran while one was open for 2% -> 0% of each run, Pallas kernels for 0% -> 8%
where the time goes in v2:
time: 39.7 us; the launch traced here: 39.5 us
  starting transfers between devices  18.3 us (46%)
  waiting for transfers between devices  13 us (33%)
  Pallas kernels  8.09 us (20%)
    ppermute x17, starting transfers between devices, move(): return lax.ppermute(x, ('dp', 'seq'), pairs)  18.3 us
    ppermute x17, waiting for transfers between devices, move(): return lax.ppermute(x, ('dp', 'seq'), pairs)  13 us
    pallas_call x8, Pallas kernels, vmem_call(): pl.pallas_call(body, out_shape=[VMEM(s, d) for s, d in outs], in_specs=sp...  7.14 us
    pallas_call x1, Pallas kernels, paired_chips(): pl.pallas_call(solve_body, out_shape=jax.ShapeDtypeStruct((ndocs, ntest),...  0.95 us
  transfers between devices with their start and end apart: 17, of which 7 were waited for; matrix products, arithmetic and copies ran while one was open for 0% of the time, Pallas kernels for 8%

profile of v2, /device:TPU:0, one launch (start us, length us, event | category | flops | bytes accessed | tf_op | source)
XLA Modules:
  0.0 39.5 jit_solution(16304838354862435988)
XLA Ops:
  0.0 1.0 %weights.1 = (bf16[64,1152]{1,0:T(8,128)(2,1)S(1)}, bf16[64,1152]{1,0:T(8,128)(2,1)S(1)}, f32[8,128]{1,0:T(8,128)S(1)}) custom-call(s32[1,128]{1,0:T(1,128)} %valid.1, s32[1,4]{1,0:T(1,128)} %blocks.1, bf16[64,1792]{1,0:T(8,128)(2,1)} %bitcast.8, bf16[64,512]{1,0:T(8,128)(2,1)} %bitcast.9), custom_call_target="tpu_custom_call" | custom-call | tf_op jit(solution)/shard_map/weights/pallas_call | solution.py:58
  1.0 1.7 %send.1._ = bf16[128,9216]{1,0:T(8,128)(2,1)S(1)} custom-call(f32[8,128]{1,0:T(8,128)S(1)} %get-tuple-element.16._.weights, bf16[128,14336]{1,0:T(8,128)(2,1)} %bitcast.4, bf16[128,4096]{1,0:T(8,128)(2,1)} %bitcast.6), custom_call_target="tpu_custom_call" | custom-call | bytes 4718592 | tf_op jit(solution)/shard_map/send/pallas_call | solution.py:58
  2.7 0.5 %collective-permute-start.6 = (bf16[128,9216]{1,0:T(8,128)(2,1)S(1)}, bf16[128,9216]{1,0:T(8,128)(2,1)S(1)}, u32[]{:S(2)}, u32[]{:S(2)}) collective-permute-start(bf16[128,9216]{1,0:T(8,128)(2,1)S(1)} %send.1._), channel_id=1, source_target_pairs={{0,1},{1,0},{2,3},{3,2},{4,5},{5,4},{6,7},{7,6},{8,9},{9,8},{10,11... | collective-permute-start | bytes 7077896 | tf_op jit(solution)/shard_map/ppermute | solution.py:259
  3.3 2.6 %collective-permute-start.2 = (bf16[64,1152]{1,0:T(8,128)(2,1)S(1)}, bf16[64,1152]{1,0:T(8,128)(2,1)S(1)}, u32[]{:S(2)}, u32[]{:S(2)}) collective-permute-start(bf16[64,1152]{1,0:T(8,128)(2,1)S(1)} %get-tuple-element.15.w1), channel_id=1, source_target_pairs={{0,3},{1,4},{2,1},{3,6},{4,7},{5,0},{6,5},{7,2},{8,11},{9,12},{10,... | collective-permute-start | bytes 442376 | tf_op jit(solution)/shard_map/ppermute | solution.py:259
  5.9 1.2 %collective-permute-start = (bf16[64,1152]{1,0:T(8,128)(2,1)S(1)}, bf16[64,1152]{1,0:T(8,128)(2,1)S(1)}, u32[]{:S(2)}, u32[]{:S(2)}) collective-permute-start(bf16[64,1152]{1,0:T(8,128)(2,1)S(1)} %get-tuple-element.14.w2), channel_id=1, source_target_pairs={{0,3},{1,4},{2,1},{3,6},{4,7},{5,0},{6,5},{7,2},{8,11},{9,12},{10,... | collective-permute-start | bytes 442376 | tf_op jit(solution)/shard_map/ppermute | solution.py:259
  7.0 0.6 %collective-permute-start.4 = (bf16[64,1152]{1,0:T(8,128)(2,1)S(1)}, bf16[64,1152]{1,0:T(8,128)(2,1)S(1)}, u32[]{:S(2)}, u32[]{:S(2)}) collective-permute-start(bf16[64,1152]{1,0:T(8,128)(2,1)S(1)} %get-tuple-element.15.w1), channel_id=1, source_target_pairs={{0,5},{1,2},{2,7},{3,0},{4,1},{5,6},{6,3},{7,4},{8,13},{9,10},{10,... | collective-permute-start | bytes 442376 | tf_op jit(solution)/shard_map/ppermute | solution.py:259
  7.7 1.3 %collective-permute-done.2.a1 = bf16[64,1152]{1,0:T(8,128)(2,1)S(1)} collective-permute-done((bf16[64,1152]{1,0:T(8,128)(2,1)S(1)}, bf16[64,1152]{1,0:T(8,128)(2,1)S(1)}, u32[]{:S(2)}, u32[]{:S(2)}) %collective-permute-start.2) | collective-permute-done | bytes 147488 | tf_op jit(solution)/shard_map/ppermute | solution.py:259
  8.9 2.2 %collective-permute-start.3 = (bf16[64,1152]{1,0:T(8,128)(2,1)S(1)}, bf16[64,1152]{1,0:T(8,128)(2,1)S(1)}, u32[]{:S(2)}, u32[]{:S(2)}) collective-permute-start(bf16[64,1152]{1,0:T(8,128)(2,1)S(1)} %collective-permute-done.2.a1), channel_id=1, source_target_pairs={{0,3},{1,4},{2,1},{3,6},{4,7},{5,0},{6,5},{7,2},{8,11},{9,12},{10,... | collective-permute-start | bytes 442376 | tf_op jit(solution)/shard_map/ppermute | solution.py:259
  11.1 1.0 %collective-permute-done.a2 = bf16[64,1152]{1,0:T(8,128)(2,1)S(1)} collective-permute-done((bf16[64,1152]{1,0:T(8,128)(2,1)S(1)}, bf16[64,1152]{1,0:T(8,128)(2,1)S(1)}, u32[]{:S(2)}, u32[]{:S(2)}) %collective-permute-start) | collective-permute-done | bytes 147488 | tf_op jit(solution)/shard_map/ppermute | solution.py:259
  12.1 2.2 %collective-permute-start.1 = (bf16[64,1152]{1,0:T(8,128)(2,1)S(1)}, bf16[64,1152]{1,0:T(8,128)(2,1)S(1)}, u32[]{:S(2)}, u32[]{:S(2)}) collective-permute-start(bf16[64,1152]{1,0:T(8,128)(2,1)S(1)} %collective-permute-done.a2), channel_id=1, source_target_pairs={{0,3},{1,4},{2,1},{3,6},{4,7},{5,0},{6,5},{7,2},{8,11},{9,12},{10,... | collective-permute-start | bytes 442376 | tf_op jit(solution)/shard_map/ppermute | solution.py:259
  14.3 1.8 %keep.1 = (bf16[128,9216]{1,0:T(8,128)(2,1)S(1)}, bf16[32,2048]{1,0:T(8,128)(2,1)S(1)}, bf16[32,2048]{1,0:T(8,128)(2,1)S(1)}, s32[16,128]{1,0:T(8,128)S(1)}) custom-call(bf16[128,9216]{1,0:T(8,128)(2,1)S(1)} %send.1._, bf16[128,14336]{1,0:T(8,128)(2,1)} %bitcast.5, bf16[128,4096]{1,0:T(8,128)(2,1)} %bitcast.7, bf16[32,4096]{1,0:T(8,128)(2,1)} %tests.1, s32[16]{0:T(128)} %ids.1), custom_call_target="tpu_custom_call" | custom-call | bytes 4718592 | tf_op jit(solution)/shard_map/keep/pallas_call | solution.py:58
  16.1 1.2 %near.1 = (f32[64,256]{1,0:T(8,128)S(1)}, f32[64,256]{1,0:T(8,128)S(1)}) custom-call(bf16[64,1152]{1,0:T(8,128)(2,1)S(1)} %get-tuple-element.15.w1, bf16[64,1152]{1,0:T(8,128)(2,1)S(1)} %get-tuple-element.14.w2, bf16[64,1152]{1,0:T(8,128)(2,1)S(1)} %collective-permute-done.2.a1, bf16[64,1152]{1,0:T(8,128)(2,1)S(1)} %collective-permute-done.a2, ...), custom_call_target="tpu_custom_call" | custom-call | tf_op jit(solution)/shard_map/near/pallas_call | solution.py:58
  17.9 0.7 %collective-permute-start.7 = (f32[128,256]{1,0:T(8,128)S(1)}, f32[128,256]{1,0:T(8,128)S(1)}, u32[]{:S(2)}, u32[]{:S(2)}) collective-permute-start(f32[128,256]{1,0:T(8,128)S(1)} %last.1.mine), channel_id=1, source_target_pairs={{0,1},{1,0},{2,3},{3,2},{4,5},{5,4},{6,7},{7,6},{8,9},{9,8},{10,11... | collective-permute-start | bytes 393224 | tf_op jit(solution)/shard_map/ppermute | solution.py:259
  18.7 1.1 %collective-permute-done.8.weights2 = f32[8,128]{1,0:T(8,128)S(1)} collective-permute-done((f32[8,128]{1,0:T(8,128)S(1)}, f32[8,128]{1,0:T(8,128)S(1)}, u32[]{:S(2)}, u32[]{:S(2)}) %collective-permute-start.8) | collective-permute-done | bytes 4128 | tf_op jit(solution)/shard_map/ppermute | solution.py:259
  20.1 2.3 %collective-permute-start.10 = (f32[64,128]{1,0:T(8,128)S(1)}, f32[64,128]{1,0:T(8,128)S(1)}, u32[]{:S(2)}, u32[]{:S(2)}) collective-permute-start(f32[64,128]{1,0:T(8,128)S(1)} %grads.1), channel_id=1, source_target_pairs={{0,5},{1,4},{2,7},{3,6},{4,1},{5,0},{6,3},{7,2},{8,13},{9,12},{10,... | collective-permute-start | bytes 98312 | tf_op jit(solution)/shard_map/ppermute | solution.py:259
  22.4 1.0 %collective-permute-start.11 = (f32[64,128]{1,0:T(8,128)S(1)}, f32[64,128]{1,0:T(8,128)S(1)}, u32[]{:S(2)}, u32[]{:S(2)}) collective-permute-start(f32[64,128]{1,0:T(8,128)S(1)} %grads.1), channel_id=1, source_target_pairs={{0,6},{1,7},{2,4},{3,5},{4,2},{5,3},{6,0},{7,1},{8,14},{9,15},{10,... | collective-permute-start | bytes 98312 | tf_op jit(solution)/shard_map/ppermute | solution.py:259
  24.1 3.1 %collective-permute-done.11 = f32[64,128]{1,0:T(8,128)S(1)} collective-permute-done((f32[64,128]{1,0:T(8,128)S(1)}, f32[64,128]{1,0:T(8,128)S(1)}, u32[]{:S(2)}, u32[]{:S(2)}) %collective-permute-start.11) | collective-permute-done | bytes 32800 | tf_op jit(solution)/shard_map/ppermute | solution.py:259
  27.2 1.1 %collective-permute-start.12 = (f32[64,128]{1,0:T(8,128)S(1)}, f32[64,128]{1,0:T(8,128)S(1)}, u32[]{:S(2)}, u32[]{:S(2)}) collective-permute-start(f32[64,128]{1,0:T(8,128)S(1)} %add_add_fusion.m0), channel_id=1, source_target_pairs={{0,9},{1,8},{2,11},{3,10},{4,13},{5,12},{6,15},{7,14},{8,1},{9,0},... | collective-permute-start | bytes 98312 | tf_op jit(solution)/shard_map/ppermute | solution.py:259
  28.4 2.7 %collective-permute-start.13 = (f32[64,128]{1,0:T(8,128)S(1)}, f32[64,128]{1,0:T(8,128)S(1)}, u32[]{:S(2)}, u32[]{:S(2)}) collective-permute-start(f32[64,128]{1,0:T(8,128)S(1)} %add_add_fusion.m0), channel_id=1, source_target_pairs={{0,17},{1,16},{2,19},{3,18},{4,21},{5,20},{6,23},{7,22},{8,25},{9,... | collective-permute-start | bytes 98312 | tf_op jit(solution)/shard_map/ppermute | solution.py:259
  31.4 1.2 %collective-permute-done.13.m2 = f32[64,128]{1,0:T(8,128)S(1)} collective-permute-done((f32[64,128]{1,0:T(8,128)S(1)}, f32[64,128]{1,0:T(8,128)S(1)}, u32[]{:S(2)}, u32[]{:S(2)}) %collective-permute-start.13) | collective-permute-done | bytes 32800 | tf_op jit(solution)/shard_map/ppermute | solution.py:259
  32.6 4.1 %collective-permute-done.14.m3 = f32[64,128]{1,0:T(8,128)S(1)} collective-permute-done((f32[64,128]{1,0:T(8,128)S(1)}, f32[64,128]{1,0:T(8,128)S(1)}, u32[]{:S(2)}, u32[]{:S(2)}) %collective-permute-start.14) | collective-permute-done | bytes 32800 | tf_op jit(solution)/shard_map/ppermute | solution.py:259
  36.8 0.5 %products.1.mine = f32[16,128]{1,0:T(8,128)S(1)} custom-call(f32[64,128]{1,0:T(8,128)S(1)} %add_add_fusion.m0, f32[64,128]{1,0:T(8,128)S(1)} %collective-permute-done.12.m1, f32[64,128]{1,0:T(8,128)S(1)} %collective-permute-done.13.m2, f32[64,128]{1,0:T(8,128)S(1)} %collective-permute-done.14.m3, bf16[32,2048]{1,0:T(8,128)(2,1)S(1)} %get-tuple-element.20.t_own, ...), custom_call_target="tpu_custom_call" | custom-call | tf_op jit(solution)/shard_map/products/pallas_call | solution.py:58
  37.3 1.2 %collective-permute-done.16.far = f32[16,128]{1,0:T(8,128)S(1)} collective-permute-done((f32[16,128]{1,0:T(8,128)S(1)}, f32[16,128]{1,0:T(8,128)S(1)}, u32[]{:S(2)}, u32[]{:S(2)}) %collective-permute-start.16) | collective-permute-done | bytes 8224 | tf_op jit(solution)/shard_map/ppermute | solution.py:259
  38.5 0.9 %solve.1 = f32[16,32]{1,0:T(8,128)} custom-call(f32[16,128]{1,0:T(8,128)S(1)} %products.1.mine, f32[16,128]{1,0:T(8,128)S(1)} %collective-permute-done.16.far, s32[16,128]{1,0:T(8,128)S(1)} %get-tuple-element.22.rows), custom_call_target="tpu_custom_call" | custom-call | tf_op jit(solution)/shard_map/solve/pallas_call | solution.py:317
  (20 shorter events, 2.2 us)
Async XLA Ops:
  2.7 13.4 %collective-permute-start.6 = (bf16[128,9216]{1,0:T(8,128)(2,1)S(1)}, bf16[128,9216]{1,0:T(8,128)(2,1)S(1)}, u32[]{:S(2)}, u32[]{:S(2)}) collective-permute-start(bf16[128,9216]{1,0:T(8,128)(2,1)S(1)} %send.1._), channel_id=1, source_target_pairs={{0,1},{1,0},{2,3},{3,2},{4,5},{5,4},{6,7},{7,6},{8,9},{9,8},{10,11... | collective-permute-start | bytes 7077896 | tf_op jit(solution)/shard_map/ppermute | solution.py:259
  3.3 5.7 %collective-permute-start.2 = (bf16[64,1152]{1,0:T(8,128)(2,1)S(1)}, bf16[64,1152]{1,0:T(8,128)(2,1)S(1)}, u32[]{:S(2)}, u32[]{:S(2)}) collective-permute-start(bf16[64,1152]{1,0:T(8,128)(2,1)S(1)} %get-tuple-element.15.w1), channel_id=1, source_target_pairs={{0,3},{1,4},{2,1},{3,6},{4,7},{5,0},{6,5},{7,2},{8,11},{9,12},{10,... | collective-permute-start | bytes 442376 | tf_op jit(solution)/shard_map/ppermute | solution.py:259
  5.9 6.2 %collective-permute-start = (bf16[64,1152]{1,0:T(8,128)(2,1)S(1)}, bf16[64,1152]{1,0:T(8,128)(2,1)S(1)}, u32[]{:S(2)}, u32[]{:S(2)}) collective-permute-start(bf16[64,1152]{1,0:T(8,128)(2,1)S(1)} %get-tuple-element.14.w2), channel_id=1, source_target_pairs={{0,3},{1,4},{2,1},{3,6},{4,7},{5,0},{6,5},{7,2},{8,11},{9,12},{10,... | collective-permute-start | bytes 442376 | tf_op jit(solution)/shard_map/ppermute | solution.py:259
  7.0 9.1 %collective-permute-start.4 = (bf16[64,1152]{1,0:T(8,128)(2,1)S(1)}, bf16[64,1152]{1,0:T(8,128)(2,1)S(1)}, u32[]{:S(2)}, u32[]{:S(2)}) collective-permute-start(bf16[64,1152]{1,0:T(8,128)(2,1)S(1)} %get-tuple-element.15.w1), channel_id=1, source_target_pairs={{0,5},{1,2},{2,7},{3,0},{4,1},{5,6},{6,3},{7,4},{8,13},{9,10},{10,... | collective-permute-start | bytes 442376 | tf_op jit(solution)/shard_map/ppermute | solution.py:259
  7.6 8.5 %collective-permute-start.5 = (bf16[64,1152]{1,0:T(8,128)(2,1)S(1)}, bf16[64,1152]{1,0:T(8,128)(2,1)S(1)}, u32[]{:S(2)}, u32[]{:S(2)}) collective-permute-start(bf16[64,1152]{1,0:T(8,128)(2,1)S(1)} %get-tuple-element.14.w2), channel_id=1, source_target_pairs={{0,5},{1,2},{2,7},{3,0},{4,1},{5,6},{6,3},{7,4},{8,13},{9,10},{10,... | collective-permute-start | bytes 442376 | tf_op jit(solution)/shard_map/ppermute | solution.py:259
  8.9 8.4 %collective-permute-start.3 = (bf16[64,1152]{1,0:T(8,128)(2,1)S(1)}, bf16[64,1152]{1,0:T(8,128)(2,1)S(1)}, u32[]{:S(2)}, u32[]{:S(2)}) collective-permute-start(bf16[64,1152]{1,0:T(8,128)(2,1)S(1)} %collective-permute-done.2.a1), channel_id=1, source_target_pairs={{0,3},{1,4},{2,1},{3,6},{4,7},{5,0},{6,5},{7,2},{8,11},{9,12},{10,... | collective-permute-start | bytes 442376 | tf_op jit(solution)/shard_map/ppermute | solution.py:259
  12.1 5.5 %collective-permute-start.1 = (bf16[64,1152]{1,0:T(8,128)(2,1)S(1)}, bf16[64,1152]{1,0:T(8,128)(2,1)S(1)}, u32[]{:S(2)}, u32[]{:S(2)}) collective-permute-start(bf16[64,1152]{1,0:T(8,128)(2,1)S(1)} %collective-permute-done.a2), channel_id=1, source_target_pairs={{0,3},{1,4},{2,1},{3,6},{4,7},{5,0},{6,5},{7,2},{8,11},{9,12},{10,... | collective-permute-start | bytes 442376 | tf_op jit(solution)/shard_map/ppermute | solution.py:259
  17.9 1.8 %collective-permute-start.7 = (f32[128,256]{1,0:T(8,128)S(1)}, f32[128,256]{1,0:T(8,128)S(1)}, u32[]{:S(2)}, u32[]{:S(2)}) collective-permute-start(f32[128,256]{1,0:T(8,128)S(1)} %last.1.mine), channel_id=1, source_target_pairs={{0,1},{1,0},{2,3},{3,2},{4,5},{5,4},{6,7},{7,6},{8,9},{9,8},{10,11... | collective-permute-start | bytes 393224 | tf_op jit(solution)/shard_map/ppermute | solution.py:259
  18.6 1.2 %collective-permute-start.8 = (f32[8,128]{1,0:T(8,128)S(1)}, f32[8,128]{1,0:T(8,128)S(1)}, u32[]{:S(2)}, u32[]{:S(2)}) collective-permute-start(f32[8,128]{1,0:T(8,128)S(1)} %get-tuple-element.16._.weights), channel_id=1, source_target_pairs={{0,1},{1,0},{2,3},{3,2},{4,5},{5,4},{6,7},{7,6},{8,9},{9,8},{10,11... | collective-permute-start | bytes 12296 | tf_op jit(solution)/shard_map/ppermute | solution.py:259
  20.1 4.0 %collective-permute-start.10 = (f32[64,128]{1,0:T(8,128)S(1)}, f32[64,128]{1,0:T(8,128)S(1)}, u32[]{:S(2)}, u32[]{:S(2)}) collective-permute-start(f32[64,128]{1,0:T(8,128)S(1)} %grads.1), channel_id=1, source_target_pairs={{0,5},{1,4},{2,7},{3,6},{4,1},{5,0},{6,3},{7,2},{8,13},{9,12},{10,... | collective-permute-start | bytes 98312 | tf_op jit(solution)/shard_map/ppermute | solution.py:259
  22.4 4.8 %collective-permute-start.11 = (f32[64,128]{1,0:T(8,128)S(1)}, f32[64,128]{1,0:T(8,128)S(1)}, u32[]{:S(2)}, u32[]{:S(2)}) collective-permute-start(f32[64,128]{1,0:T(8,128)S(1)} %grads.1), channel_id=1, source_target_pairs={{0,6},{1,7},{2,4},{3,5},{4,2},{5,3},{6,0},{7,1},{8,14},{9,15},{10,... | collective-permute-start | bytes 98312 | tf_op jit(solution)/shard_map/ppermute | solution.py:259
  23.4 3.8 %collective-permute-start.9 = (f32[64,128]{1,0:T(8,128)S(1)}, f32[64,128]{1,0:T(8,128)S(1)}, u32[]{:S(2)}, u32[]{:S(2)}) collective-permute-start(f32[64,128]{1,0:T(8,128)S(1)} %grads.1), channel_id=1, source_target_pairs={{0,3},{1,2},{2,1},{3,0},{4,7},{5,6},{6,5},{7,4},{8,11},{9,10},{10,... | collective-permute-start | bytes 98312 | tf_op jit(solution)/shard_map/ppermute | solution.py:259
  23.7 7.7 %collective-permute-start.15 = (bf16[32,2048]{1,0:T(8,128)(2,1)S(1)}, bf16[32,2048]{1,0:T(8,128)(2,1)S(1)}, u32[]{:S(2)}, u32[]{:S(2)}) collective-permute-start(bf16[32,2048]{1,0:T(8,128)(2,1)S(1)} %get-tuple-element.21), channel_id=1, source_target_pairs={{0,1},{1,0},{2,3},{3,2},{4,5},{5,4},{6,7},{7,6},{8,9},{9,8},{10,11... | collective-permute-start | bytes 393224 | tf_op jit(solution)/shard_map/ppermute | solution.py:259
  27.2 4.2 %collective-permute-start.12 = (f32[64,128]{1,0:T(8,128)S(1)}, f32[64,128]{1,0:T(8,128)S(1)}, u32[]{:S(2)}, u32[]{:S(2)}) collective-permute-start(f32[64,128]{1,0:T(8,128)S(1)} %add_add_fusion.m0), channel_id=1, source_target_pairs={{0,9},{1,8},{2,11},{3,10},{4,13},{5,12},{6,15},{7,14},{8,1},{9,0},... | collective-permute-start | bytes 98312 | tf_op jit(solution)/shard_map/ppermute | solution.py:259
  28.4 4.3 %collective-permute-start.13 = (f32[64,128]{1,0:T(8,128)S(1)}, f32[64,128]{1,0:T(8,128)S(1)}, u32[]{:S(2)}, u32[]{:S(2)}) collective-permute-start(f32[64,128]{1,0:T(8,128)S(1)} %add_add_fusion.m0), channel_id=1, source_target_pairs={{0,17},{1,16},{2,19},{3,18},{4,21},{5,20},{6,23},{7,22},{8,25},{9,... | collective-permute-start | bytes 98312 | tf_op jit(solution)/shard_map/ppermute | solution.py:259
  31.0 5.7 %collective-permute-start.14 = (f32[64,128]{1,0:T(8,128)S(1)}, f32[64,128]{1,0:T(8,128)S(1)}, u32[]{:S(2)}, u32[]{:S(2)}) collective-permute-start(f32[64,128]{1,0:T(8,128)S(1)} %add_add_fusion.m0), channel_id=1, source_target_pairs={{0,24},{1,25},{2,26},{3,27},{4,28},{5,29},{6,30},{7,31},{8,16},{9,... | collective-permute-start | bytes 98312 | tf_op jit(solution)/shard_map/ppermute | solution.py:259
  37.3 1.2 %collective-permute-start.16 = (f32[16,128]{1,0:T(8,128)S(1)}, f32[16,128]{1,0:T(8,128)S(1)}, u32[]{:S(2)}, u32[]{:S(2)}) collective-permute-start(f32[16,128]{1,0:T(8,128)S(1)} %products.1.mine), channel_id=1, source_target_pairs={{0,1},{1,0},{2,3},{3,2},{4,5},{5,4},{6,7},{7,6},{8,9},{9,8},{10,11... | collective-permute-start | bytes 24584 | tf_op jit(solution)/shard_map/ppermute | solution.py:259

commit v3 on v2

--- a/solution.py
+++ b/solution.py
@@ -39,7 +39,7 @@
 
 
 def place(seq, dp):
-    bits = seq ^ (seq >> 1) ^ (seq >> 2) ^ dp ^ (dp >> 1)
+    bits = seq ^ (seq >> 1) ^ (seq >> 2) ^ (dp >> 1)
     return bits & 1
 
 
@@ -72,7 +72,7 @@
     return seq ^ jnp.where(seq & 1 == 0, even, odd)
 
 
-def weights_body(valid, blocks, out_t, in_t, first, second, weights, valid_v, blocks_s, sems):
+def weights_body(valid, blocks, out_t, in_t, first, second, whole, weights, valid_v, blocks_s, sems):
     seq, _, _ = here()
     rows_out, rows_in, size = out_t.shape[1], in_t.shape[1], first.shape[1]
     rest = rows_out - size
@@ -80,8 +80,10 @@
         pltpu.make_async_copy(out_t.at[:, pl.ds(0, size)], first, sems.at[0]),
         pltpu.make_async_copy(out_t.at[:, pl.ds(size, rest)], second.at[:, pl.ds(0, rest)], sems.at[1]),
         pltpu.make_async_copy(in_t, second.at[:, pl.ds(rest, rows_in)], sems.at[2]),
-        pltpu.make_async_copy(valid, valid_v, sems.at[3]),
-        pltpu.make_async_copy(blocks, blocks_s, sems.at[4]),
+        pltpu.make_async_copy(out_t, whole.at[:, pl.ds(0, rows_out)], sems.at[3]),
+        pltpu.make_async_copy(in_t, whole.at[:, pl.ds(rows_out, rows_in)], sems.at[4]),
+        pltpu.make_async_copy(valid, valid_v, sems.at[5]),
+        pltpu.make_async_copy(blocks, blocks_s, sems.at[6]),
     ]
     for c in copies:
         c.start()
@@ -98,13 +100,13 @@
     weights[...] = jnp.where((owner == row) & (valid_v[...] == 1), 1.0, 0.0)
 
 
-def column_copies(og, inp, out, mine, sems):
+def column_copies(og, inp, three, last, mine, sems):
     nseq = lax.axis_size("seq")
     wo, wi = og.shape[1] // nseq, inp.shape[1] // nseq
     copies = []
     for k in range(4):
         shard = source(mine, k)
-        base = k * (wo + wi)
+        out, base = (last, 0) if k == 3 else (three, k * (wo + wi))
         copies.append(pltpu.make_async_copy(
             og.at[:, pl.ds(pl.multiple_of(shard * wo, wo), wo)], out.at[:, pl.ds(base, wo)], sems.at[2 * k]))
         copies.append(pltpu.make_async_copy(
@@ -112,63 +114,63 @@
     return copies
 
 
-def send_body(_, og, inp, send, sems):
-    seq, _, _ = here()
-    copies = column_copies(og, inp, send, seq ^ 1, sems)
-    for c in copies:
-        c.start()
-    for c in copies:
-        c.wait()
-
-
-def keep_body(_, og, inp, tests, ids, keep, t_own, t_far, rows, ids_s, sems):
+def nt(a, b, precision=None):
+    return lax.dot_general(a, b, (((1,), (1,)), ((), ())), precision=precision, preferred_element_type=F32)
+
+
+def project(w, near, base, far, shard, width, skip):
+    rows = w.shape[1]
+    start = pl.multiple_of(shard * width + skip, 128)
+    return nt(w, jnp.concatenate([near[:, pl.ds(base, rows)], far[:, pl.ds(start, rows)]], axis=0))
+
+
+def near_body(own, a1, a2, b, og2, inp2, og, inp, tests, ids, pg, px, near, t_own, t_far, rows,
+              near_s, ids_s, sems, *, wi, wo):
     seq, _, half = here()
     hf = t_own.shape[1]
-    copies = column_copies(og, inp, keep, seq, sems)
-    copies.append(pltpu.make_async_copy(tests.at[:, pl.ds(pl.multiple_of(half * hf, hf), hf)], t_own, sems.at[8]))
-    copies.append(pltpu.make_async_copy(tests.at[:, pl.ds(pl.multiple_of((1 - half) * hf, hf), hf)], t_far, sems.at[9]))
-    copies.append(pltpu.make_async_copy(ids, ids_s, sems.at[10]))
-    for c in copies:
+    size = a1.shape[1]
+    rest = wo - size
+    each = wo + wi
+    copies = column_copies(og, inp, near_s, near, seq, sems)
+    more = [
+        pltpu.make_async_copy(tests.at[:, pl.ds(pl.multiple_of(half * hf, hf), hf)], t_own, sems.at[8]),
+        pltpu.make_async_copy(tests.at[:, pl.ds(pl.multiple_of((1 - half) * hf, hf), hf)], t_far, sems.at[9]),
+        pltpu.make_async_copy(ids, ids_s, sems.at[10]),
+    ]
+    for c in copies + more:
         c.start()
-    for c in copies:
+    total, total_x = 0.0, 0.0
+    for k, w in ((0, own), (2, b), (1, None)):
+        base, shard = k * each, source(seq, k)
+        copies[2 * k].wait()
+        copies[2 * k + 1].wait()
+        if w is None:
+            total = total + project(a1[...], near_s, base, og2, shard, wo, 0)
+            total = total + project(a2[:, :rest], near_s, base + size, og2, shard, wo, size)
+            total_x = total_x + project(a2[:, rest:], near_s, base + wo, inp2, shard, wi, 0)
+        else:
+            total = total + project(w[:, :wo], near_s, base, og2, shard, wo, 0)
+            total_x = total_x + project(w[:, wo:], near_s, base + wo, inp2, shard, wi, 0)
+    pg[...] = total
+    px[...] = total_x
+    for c in copies[6:] + more:
         c.wait()
     for r in range(rows.shape[0]):
         rows[r:r + 1, :] = jnp.full((1, rows.shape[1]), ids_s[r], jnp.int32)
 
 
-def nt(a, b, precision=None):
-    return lax.dot_general(a, b, (((1,), (1,)), ((), ())), precision=precision, preferred_element_type=F32)
-
-
-def project(w, near, far, base):
-    cols = pl.ds(base, w.shape[1])
-    return nt(w, jnp.concatenate([near[:, cols], far[:, cols]], axis=0))
-
-
-def near_body(w1, w2, a1, a2, b1, b2, near, far, pg, px, *, wi):
-    size = w1.shape[1]
-    rest = w2.shape[1] - wi
-    total, total_x = 0.0, 0.0
-    for k, (x, y) in enumerate(((w1, w2), (a1, a2), (b1, b2))):
-        base = k * (size + rest + wi)
-        total = total + project(x[...], near, far, base)
-        total = total + project(y[:, :rest], near, far, base + size)
-        total_x = total_x + project(y[:, rest:], near, far, base + size + rest)
-    pg[...] = total
-    px[...] = total_x
-
-
-def diagonal_body(c1, pg_in, near, far, pg):
-    base = near.shape[1] // 4 * 3
-    pg[...] = pg_in[...] + project(c1[...], near, far, base)
-
-
-def last_body(c2, pg_in, px_in, near, far, out, *, wi):
-    base = near.shape[1] - c2.shape[1]
+def diagonal_body(c1, pg_in, near, og2, pg, *, wo):
+    seq, _, _ = here()
+    pg[...] = pg_in[...] + project(c1[...], near, 0, og2, source(seq, 3), wo, 0)
+
+
+def last_body(c2, pg_in, px_in, near, og2, inp2, out, *, wi, wo):
+    seq, _, _ = here()
     rest = c2.shape[1] - wi
     rows = pg_in.shape[0]
-    out[:rows] = pg_in[...] + project(c2[:, :rest], near, far, base)
-    out[rows:2 * rows] = px_in[...] + project(c2[:, rest:], near, far, base + rest)
+    shard = source(seq, 3)
+    out[:rows] = pg_in[...] + project(c2[:, :rest], near, wo - rest, og2, shard, wo, wo - rest)
+    out[rows:2 * rows] = px_in[...] + project(c2[:, rest:], near, wo, inp2, shard, wi, 0)
 
 
 def grads_body(mine, far, weights, weights2, grads, pgs):
@@ -194,10 +196,14 @@
     grads[...] = jnp.concatenate(parts, axis=1)
 
 
-def products_body(m0, m1, m2, m3, t_own, t_far, out, every):
+def sum_body(own, px, py, pd, out):
+    out[...] = (own[...] + px[...]) + (py[...] + pd[...])
+
+
+def products_body(m0, m3, m2, m1, t_own, t_far, out, every):
     seq, dp, _ = here()
     rows = m0.shape[0]
-    for k, m in enumerate((m0, m1, m2, m3)):
+    for k, m in zip((0, 3, 2, 1), (m0, m3, m2, m1)):
         every[pl.ds(pl.multiple_of((dp ^ k) * rows, rows), rows), :] = m[...]
     docs = out.shape[0]
     pairs = every.shape[0] // docs
@@ -265,53 +271,48 @@
         return move(x, lambda z, s: (z, s ^ ((3, 5)[(s & 1) ^ step])))
 
     size = (wo + wi) // 256 * 128
-    first, second, weights = vmem_call(
+    first, second, whole, weights = vmem_call(
         weights_body,
-        [((width, size), bf), ((width, wo + wi - size), bf), ((8, slots), F32)],
+        [((width, size), bf), ((width, wo + wi - size), bf), ((width, wo + wi), bf), ((8, slots), F32)],
         [], hbm=[valid, doc_blocks, proj_out.T, proj_in.T],
-        scratch=[VMEM((1, slots), jnp.int32), pltpu.SMEM((1, docs), jnp.int32), pltpu.SemaphoreType.DMA((5,))],
+        scratch=[VMEM((1, slots), jnp.int32), pltpu.SMEM((1, docs), jnp.int32), pltpu.SemaphoreType.DMA((7,))],
         name="weights",
     )
-    a1, b1 = ring(first, 0), ring(first, 1)
-    a2, b2 = ring(second, 0), ring(second, 1)
+    a1, a2, b = ring(first, 0), ring(second, 0), ring(whole, 1)
     weights2 = swap(weights)
-    (tokens,) = vmem_call(
-        send_body, [((slots, 4 * (wo + wi)), bf)], [weights], hbm=[og, inp],
-        scratch=[pltpu.SemaphoreType.DMA((8,))], name="send", moved=1 * slots * (wo + wi) * 16,
-    )
-    far = swap(tokens)
-    near, t_own, t_send, rows = vmem_call(
-        keep_body, [((slots, 4 * (wo + wi)), bf)] + [((ntest, feat // 2), bf)] * 2 + [((ndocs, -(-(2 * ntest + ndocs) // 128) * 128), jnp.int32)],
-        [tokens], hbm=[og, inp, test_grads, doc_ids],
-        scratch=[pltpu.SMEM((ndocs,), jnp.int32), pltpu.SemaphoreType.DMA((11,))], name="keep", moved=1 * slots * (wo + wi) * 16,
-    )
-    t_far = swap(t_send)
+    og2, inp2 = swap(og), swap(inp)
     c1 = ring(a1, 0)
     c2 = ring(a2, 0)
     part = ((width, 2 * slots), F32)
-    pg, px = vmem_call(
-        functools.partial(near_body, wi=wi), [part, part],
-        [first, second, a1, a2, b1, b2, near, far], name="near",
-    )
-    (pg,) = vmem_call(diagonal_body, [part], [c1, pg, near, far], name="diagonal")
+    lanes = -(-(2 * ntest + ndocs) // 128) * 128
+    pg, px, near, t_own, t_send, rows = vmem_call(
+        functools.partial(near_body, wi=wi, wo=wo),
+        [part, part, ((slots, wo + wi), bf)] + [((ntest, feat // 2), bf)] * 2 + [((ndocs, lanes), jnp.int32)],
+        [whole, a1, a2, b, og2, inp2], hbm=[og, inp, test_grads, doc_ids],
+        scratch=[VMEM((slots, 3 * (wo + wi)), bf), pltpu.SMEM((ndocs,), jnp.int32), pltpu.SemaphoreType.DMA((11,))],
+        name="near",
+    )
+    t_far = swap(t_send)
+    (pg,) = vmem_call(functools.partial(diagonal_body, wo=wo), [part], [c1, pg, near, og2], name="diagonal")
     (mine,) = vmem_call(
-        functools.partial(last_body, wi=wi), [((2 * width, 2 * slots), F32)],
-        [c2, pg, px, near, far], name="last",
+        functools.partial(last_body, wi=wi, wo=wo), [((2 * width, 2 * slots), F32)],
+        [c2, pg, px, near, og2, inp2], name="last",
     )
     pairs = hw // 2
     (grads,) = vmem_call(
         grads_body, [((docs * pairs, 2 * width), F32)], [mine, swap(mine), weights, weights2],
         scratch=[VMEM((2, hw, slots), F32)], name="grads",
     )
-    grads = (grads + move(grads, lambda z, s: (z, s ^ 3))) + (
-        move(grads, lambda z, s: (z, s ^ 5)) + move(grads, lambda z, s: (z, s ^ 6)))
-    m1 = move(grads, lambda z, s: (z ^ 1, s ^ 1))
+    px = move(grads, lambda z, s: (z, s ^ 3))
+    py = move(grads, lambda z, s: (z, s ^ 5))
+    pd = move(grads, lambda z, s: (z, s ^ 6))
+    grads = (grads + px) + (py + pd)
+    m3 = move(grads, lambda z, s: (z ^ 3, s ^ 1))
     m2 = move(grads, lambda z, s: (z ^ 2, s ^ 1))
-    m3 = move(grads, lambda z, s: (z ^ 3, s))
-    lanes = -(-(2 * ntest + ndocs) // 128) * 128
+    m1 = move(grads, lambda z, s: (z ^ 1, s))
     (mine,) = vmem_call(
         products_body, [((ndocs, lanes), F32)],
-        [grads, m1, m2, m3, t_own, t_far],
+        [grads, m3, m2, m1, t_own, t_far],
         scratch=[VMEM((ndp * docs * pairs, 2 * width), F32)], name="products",
     )
     return pl.pallas_call(

time: 39.7 us -> 36.4 us (0.917)
  starting transfers between devices: 18.3 us -> 15.1 us
  waiting for transfers between devices: 13 us -> 14.6 us
  Pallas kernels: 8.09 us -> 6.55 us
    ppermute x17, starting transfers between devices: 18.3 us -> 15.1 us  [move(): return lax.ppermute(x, ('dp', 'seq'), pairs)]
    ppermute x17, waiting for transfers between devices: 13 us -> 14.6 us  [move(): return lax.ppermute(x, ('dp', 'seq'), pairs)]
    pallas_call x8 -> x6, Pallas kernels: 7.14 us -> 5.6 us  [vmem_call(): pl.pallas_call(body, out_shape=[VMEM(s, d) for s, d in outs], in_specs=sp...]
  transfers between devices with their start and end apart: 17 -> 17, of which waited for: 7 -> 9; matrix products, arithmetic and copies ran while one was open for 0% -> 0% of each run, Pallas kernels for 8% -> 12%
where the time goes in v3:
time: 36.4 us; the launch traced here: 36.3 us
  starting transfers between devices  15.1 us (41%)
  waiting for transfers between devices  14.6 us (40%)
  Pallas kernels  6.55 us (18%)
    ppermute x17, starting transfers between devices, move(): return lax.ppermute(x, ('dp', 'seq'), pairs)  15.1 us
    ppermute x17, waiting for transfers between devices, move(): return lax.ppermute(x, ('dp', 'seq'), pairs)  14.6 us
    pallas_call x6, Pallas kernels, vmem_call(): pl.pallas_call(body, out_shape=[VMEM(s, d) for s, d in outs], in_specs=sp...  5.6 us
    pallas_call x1, Pallas kernels, paired_chips(): pl.pallas_call(solve_body, out_shape=jax.ShapeDtypeStruct((ndocs, ntest),...  0.95 us
  transfers between devices with their start and end apart: 17, of which 9 were waited for; matrix products, arithmetic and copies ran while one was open for 0% of the time, Pallas kernels for 12%

profile of v3, /device:TPU:0, one launch (start us, length us, event | category | flops | bytes accessed | tf_op | source)
XLA Modules:
  0.0 36.3 jit_solution(13968467586137515229)
XLA Ops:
  0.0 0.5 %collective-permute-start.5 = (bf16[128,14336]{1,0:T(8,128)(2,1)}, bf16[128,14336]{1,0:T(8,128)(2,1)S(1)}, u32[]{:S(2)}, u32[]{:S(2)}) collective-permute-start(bf16[128,14336]{1,0:T(8,128)(2,1)} %bitcast.4), channel_id=1, source_target_pairs={{0,1},{1,0},{2,3},{3,2},{4,5},{5,4},{6,7},{7,6},{8,9},{9,8},{10,11... | collective-permute-start | bytes 11010056 | tf_op jit(solution)/shard_map/ppermute | solution.py:265
  0.5 1.2 %weights.1 = (bf16[64,1152]{1,0:T(8,128)(2,1)S(1)}, bf16[64,1152]{1,0:T(8,128)(2,1)S(1)}, bf16[64,2304]{1,0:T(8,128)(2,1)S(1)}, f32[8,128]{1,0:T(8,128)S(1)}) custom-call(s32[1,128]{1,0:T(1,128)} %valid.1, s32[1,4]{1,0:T(1,128)} %blocks.1, bf16[64,1792]{1,0:T(8,128)(2,1)} %bitcast.8, bf16[64,512]{1,0:T(8,128)(2,1)} %bitcast.9), custom_call_target="tpu_custom_call" | custom-call | tf_op jit(solution)/shard_map/weights/pallas_call | solution.py:58
  1.7 2.6 %collective-permute-start.4 = (bf16[64,2304]{1,0:T(8,128)(2,1)S(1)}, bf16[64,2304]{1,0:T(8,128)(2,1)S(1)}, u32[]{:S(2)}, u32[]{:S(2)}) collective-permute-start(bf16[64,2304]{1,0:T(8,128)(2,1)S(1)} %get-tuple-element.17.own), channel_id=1, source_target_pairs={{0,5},{1,2},{2,7},{3,0},{4,1},{5,6},{6,3},{7,4},{8,13},{9,10},{10,... | collective-permute-start | bytes 884744 | tf_op jit(solution)/shard_map/ppermute | solution.py:265
  4.4 1.7 %collective-permute-start = (bf16[64,1152]{1,0:T(8,128)(2,1)S(1)}, bf16[64,1152]{1,0:T(8,128)(2,1)S(1)}, u32[]{:S(2)}, u32[]{:S(2)}) collective-permute-start(bf16[64,1152]{1,0:T(8,128)(2,1)S(1)} %get-tuple-element.15), channel_id=1, source_target_pairs={{0,3},{1,4},{2,1},{3,6},{4,7},{5,0},{6,5},{7,2},{8,11},{9,12},{10,... | collective-permute-start | bytes 442376 | tf_op jit(solution)/shard_map/ppermute | solution.py:265
  6.0 4.4 %collective-permute-done.2.a1 = bf16[64,1152]{1,0:T(8,128)(2,1)S(1)} collective-permute-done((bf16[64,1152]{1,0:T(8,128)(2,1)S(1)}, bf16[64,1152]{1,0:T(8,128)(2,1)S(1)}, u32[]{:S(2)}, u32[]{:S(2)}) %collective-permute-start.2) | collective-permute-done | bytes 147488 | tf_op jit(solution)/shard_map/ppermute | solution.py:265
  10.5 0.3 collective-permute-start.3
  10.8 1.8 %collective-permute-done.a2 = bf16[64,1152]{1,0:T(8,128)(2,1)S(1)} collective-permute-done((bf16[64,1152]{1,0:T(8,128)(2,1)S(1)}, bf16[64,1152]{1,0:T(8,128)(2,1)S(1)}, u32[]{:S(2)}, u32[]{:S(2)}) %collective-permute-start) | collective-permute-done | bytes 147488 | tf_op jit(solution)/shard_map/ppermute | solution.py:265
  12.6 1.1 %collective-permute-start.1 = (bf16[64,1152]{1,0:T(8,128)(2,1)S(1)}, bf16[64,1152]{1,0:T(8,128)(2,1)S(1)}, u32[]{:S(2)}, u32[]{:S(2)}) collective-permute-start(bf16[64,1152]{1,0:T(8,128)(2,1)S(1)} %collective-permute-done.a2), channel_id=1, source_target_pairs={{0,3},{1,4},{2,1},{3,6},{4,7},{5,0},{6,5},{7,2},{8,11},{9,12},{10,... | collective-permute-start | bytes 442376 | tf_op jit(solution)/shard_map/ppermute | solution.py:265
  13.7 3.0 %near.1 = (f32[64,256]{1,0:T(8,128)S(1)}, f32[64,256]{1,0:T(8,128)S(1)}, bf16[128,2304]{1,0:T(8,128)(2,1)S(1)}, bf16[32,2048]{1,0:T(8,128)(2,1)S(1)}, bf16[32,20...) custom-call(bf16[64,2304]{1,0:T(8,128)(2,1)S(1)} %get-tuple-element.17.own, bf16[64,1152]{1,0:T(8,128)(2,1)S(1)} %collective-permute-done.2.a1, ...), custom_call_target="tpu_custom_call" | custom-call | tf_op jit(solution)/shard_map/near/pallas_call | solution.py:58
  18.0 0.9 %collective-permute-done.8.weights2 = f32[8,128]{1,0:T(8,128)S(1)} collective-permute-done((f32[8,128]{1,0:T(8,128)S(1)}, f32[8,128]{1,0:T(8,128)S(1)}, u32[]{:S(2)}, u32[]{:S(2)}) %collective-permute-start.8) | collective-permute-done | bytes 4128 | tf_op jit(solution)/shard_map/ppermute | solution.py:265
  18.9 0.3 grads.1
  19.3 1.3 %collective-permute-start.10 = (f32[64,128]{1,0:T(8,128)S(1)}, f32[64,128]{1,0:T(8,128)S(1)}, u32[]{:S(2)}, u32[]{:S(2)}) collective-permute-start(f32[64,128]{1,0:T(8,128)S(1)} %grads.1), channel_id=1, source_target_pairs={{0,5},{1,4},{2,7},{3,6},{4,1},{5,0},{6,3},{7,2},{8,13},{9,12},{10,... | collective-permute-start | bytes 98312 | tf_op jit(solution)/shard_map/ppermute | solution.py:265
  20.6 1.7 %collective-permute-start.11 = (f32[64,128]{1,0:T(8,128)S(1)}, f32[64,128]{1,0:T(8,128)S(1)}, u32[]{:S(2)}, u32[]{:S(2)}) collective-permute-start(f32[64,128]{1,0:T(8,128)S(1)} %grads.1), channel_id=1, source_target_pairs={{0,6},{1,7},{2,4},{3,5},{4,2},{5,3},{6,0},{7,1},{8,14},{9,15},{10,... | collective-permute-start | bytes 98312 | tf_op jit(solution)/shard_map/ppermute | solution.py:265
  22.3 0.5 %collective-permute-start.15 = (bf16[32,2048]{1,0:T(8,128)(2,1)S(1)}, bf16[32,2048]{1,0:T(8,128)(2,1)S(1)}, u32[]{:S(2)}, u32[]{:S(2)}) collective-permute-start(bf16[32,2048]{1,0:T(8,128)(2,1)S(1)} %get-tuple-element.23), channel_id=1, source_target_pairs={{0,1},{1,0},{2,3},{3,2},{4,5},{5,4},{6,7},{7,6},{8,9},{9,8},{10,11... | collective-permute-start | bytes 393224 | tf_op jit(solution)/shard_map/ppermute | solution.py:265
  22.8 2.6 %collective-permute-done.11 = f32[64,128]{1,0:T(8,128)S(1)} collective-permute-done((f32[64,128]{1,0:T(8,128)S(1)}, f32[64,128]{1,0:T(8,128)S(1)}, u32[]{:S(2)}, u32[]{:S(2)}) %collective-permute-start.11) | collective-permute-done | bytes 32800 | tf_op jit(solution)/shard_map/ppermute | solution.py:265
  25.4 0.4 %collective-permute-done.9 = f32[64,128]{1,0:T(8,128)S(1)} collective-permute-done((f32[64,128]{1,0:T(8,128)S(1)}, f32[64,128]{1,0:T(8,128)S(1)}, u32[]{:S(2)}, u32[]{:S(2)}) %collective-permute-start.9) | collective-permute-done | bytes 32800 | tf_op jit(solution)/shard_map/ppermute | solution.py:265
  25.9 3.4 %collective-permute-start.12 = (f32[64,128]{1,0:T(8,128)S(1)}, f32[64,128]{1,0:T(8,128)S(1)}, u32[]{:S(2)}, u32[]{:S(2)}) collective-permute-start(f32[64,128]{1,0:T(8,128)S(1)} %add_add_fusion.m0), channel_id=1, source_target_pairs={{0,25},{1,24},{2,27},{3,26},{4,29},{5,28},{6,31},{7,30},{8,17},{9,... | collective-permute-start | bytes 98312 | tf_op jit(solution)/shard_map/ppermute | solution.py:265
  29.2 0.8 %collective-permute-start.14 = (f32[64,128]{1,0:T(8,128)S(1)}, f32[64,128]{1,0:T(8,128)S(1)}, u32[]{:S(2)}, u32[]{:S(2)}) collective-permute-start(f32[64,128]{1,0:T(8,128)S(1)} %add_add_fusion.m0), channel_id=1, source_target_pairs={{0,8},{1,9},{2,10},{3,11},{4,12},{5,13},{6,14},{7,15},{8,0},{9,1},... | collective-permute-start | bytes 98312 | tf_op jit(solution)/shard_map/ppermute | solution.py:265
  30.0 1.0 %collective-permute-done.12.m3 = f32[64,128]{1,0:T(8,128)S(1)} collective-permute-done((f32[64,128]{1,0:T(8,128)S(1)}, f32[64,128]{1,0:T(8,128)S(1)}, u32[]{:S(2)}, u32[]{:S(2)}) %collective-permute-start.12) | collective-permute-done | bytes 32800 | tf_op jit(solution)/shard_map/ppermute | solution.py:265
  31.1 2.4 %collective-permute-done.13.m2 = f32[64,128]{1,0:T(8,128)S(1)} collective-permute-done((f32[64,128]{1,0:T(8,128)S(1)}, f32[64,128]{1,0:T(8,128)S(1)}, u32[]{:S(2)}, u32[]{:S(2)}) %collective-permute-start.13) | collective-permute-done | bytes 32800 | tf_op jit(solution)/shard_map/ppermute | solution.py:265
  33.5 0.5 %products.1.mine = f32[16,128]{1,0:T(8,128)S(1)} custom-call(f32[64,128]{1,0:T(8,128)S(1)} %add_add_fusion.m0, f32[64,128]{1,0:T(8,128)S(1)} %collective-permute-done.12.m3, f32[64,128]{1,0:T(8,128)S(1)} %collective-permute-done.13.m2, f32[64,128]{1,0:T(8,128)S(1)} %collective-permute-done.14.m1, bf16[32,2048]{1,0:T(8,128)(2,1)S(1)} %get-tuple-element.22.t_own, ...), custom_call_target="tpu_custom_call" | custom-call | tf_op jit(solution)/shard_map/products/pallas_call | solution.py:58
  34.0 0.5 %collective-permute-start.16 = (f32[16,128]{1,0:T(8,128)S(1)}, f32[16,128]{1,0:T(8,128)S(1)}, u32[]{:S(2)}, u32[]{:S(2)}) collective-permute-start(f32[16,128]{1,0:T(8,128)S(1)} %products.1.mine), channel_id=1, source_target_pairs={{0,1},{1,0},{2,3},{3,2},{4,5},{5,4},{6,7},{7,6},{8,9},{9,8},{10,11... | collective-permute-start | bytes 24584 | tf_op jit(solution)/shard_map/ppermute | solution.py:265
  34.5 0.8 %collective-permute-done.16.far = f32[16,128]{1,0:T(8,128)S(1)} collective-permute-done((f32[16,128]{1,0:T(8,128)S(1)}, f32[16,128]{1,0:T(8,128)S(1)}, u32[]{:S(2)}, u32[]{:S(2)}) %collective-permute-start.16) | collective-permute-done | bytes 8224 | tf_op jit(solution)/shard_map/ppermute | solution.py:265
  35.3 0.9 %solve.1 = f32[16,32]{1,0:T(8,128)} custom-call(f32[16,128]{1,0:T(8,128)S(1)} %products.1.mine, f32[16,128]{1,0:T(8,128)S(1)} %collective-permute-done.16.far, s32[16,128]{1,0:T(8,128)S(1)} %get-tuple-element.24.rows), custom_call_target="tpu_custom_call" | custom-call | tf_op jit(solution)/shard_map/solve/pallas_call | solution.py:318
  (18 shorter events, 1.5 us)
Async XLA Ops:
  0.0 13.7 %collective-permute-start.5 = (bf16[128,14336]{1,0:T(8,128)(2,1)}, bf16[128,14336]{1,0:T(8,128)(2,1)S(1)}, u32[]{:S(2)}, u32[]{:S(2)}) collective-permute-start(bf16[128,14336]{1,0:T(8,128)(2,1)} %bitcast.4), channel_id=1, source_target_pairs={{0,1},{1,0},{2,3},{3,2},{4,5},{5,4},{6,7},{7,6},{8,9},{9,8},{10,11... | collective-permute-start | bytes 11010056 | tf_op jit(solution)/shard_map/ppermute | solution.py:265
  0.5 13.3 %collective-permute-start.6 = (bf16[128,4096]{1,0:T(8,128)(2,1)}, bf16[128,4096]{1,0:T(8,128)(2,1)S(1)}, u32[]{:S(2)}, u32[]{:S(2)}) collective-permute-start(bf16[128,4096]{1,0:T(8,128)(2,1)} %bitcast.6), channel_id=1, source_target_pairs={{0,1},{1,0},{2,3},{3,2},{4,5},{5,4},{6,7},{7,6},{8,9},{9,8},{10,11... | collective-permute-start | bytes 3145736 | tf_op jit(solution)/shard_map/ppermute | solution.py:265
  1.7 12.0 %collective-permute-start.4 = (bf16[64,2304]{1,0:T(8,128)(2,1)S(1)}, bf16[64,2304]{1,0:T(8,128)(2,1)S(1)}, u32[]{:S(2)}, u32[]{:S(2)}) collective-permute-start(bf16[64,2304]{1,0:T(8,128)(2,1)S(1)} %get-tuple-element.17.own), channel_id=1, source_target_pairs={{0,5},{1,2},{2,7},{3,0},{4,1},{5,6},{6,3},{7,4},{8,13},{9,10},{10,... | collective-permute-start | bytes 884744 | tf_op jit(solution)/shard_map/ppermute | solution.py:265
  4.3 6.2 %collective-permute-start.2 = (bf16[64,1152]{1,0:T(8,128)(2,1)S(1)}, bf16[64,1152]{1,0:T(8,128)(2,1)S(1)}, u32[]{:S(2)}, u32[]{:S(2)}) collective-permute-start(bf16[64,1152]{1,0:T(8,128)(2,1)S(1)} %get-tuple-element.16), channel_id=1, source_target_pairs={{0,3},{1,4},{2,1},{3,6},{4,7},{5,0},{6,5},{7,2},{8,11},{9,12},{10,... | collective-permute-start | bytes 442376 | tf_op jit(solution)/shard_map/ppermute | solution.py:265
  4.4 8.2 %collective-permute-start = (bf16[64,1152]{1,0:T(8,128)(2,1)S(1)}, bf16[64,1152]{1,0:T(8,128)(2,1)S(1)}, u32[]{:S(2)}, u32[]{:S(2)}) collective-permute-start(bf16[64,1152]{1,0:T(8,128)(2,1)S(1)} %get-tuple-element.15), channel_id=1, source_target_pairs={{0,3},{1,4},{2,1},{3,6},{4,7},{5,0},{6,5},{7,2},{8,11},{9,12},{10,... | collective-permute-start | bytes 442376 | tf_op jit(solution)/shard_map/ppermute | solution.py:265
  10.5 6.2 %collective-permute-start.3 = (bf16[64,1152]{1,0:T(8,128)(2,1)S(1)}, bf16[64,1152]{1,0:T(8,128)(2,1)S(1)}, u32[]{:S(2)}, u32[]{:S(2)}) collective-permute-start(bf16[64,1152]{1,0:T(8,128)(2,1)S(1)} %collective-permute-done.2.a1), channel_id=1, source_target_pairs={{0,3},{1,4},{2,1},{3,6},{4,7},{5,0},{6,5},{7,2},{8,11},{9,12},{10,... | collective-permute-start | bytes 442376 | tf_op jit(solution)/shard_map/ppermute | solution.py:265
  12.6 4.6 %collective-permute-start.1 = (bf16[64,1152]{1,0:T(8,128)(2,1)S(1)}, bf16[64,1152]{1,0:T(8,128)(2,1)S(1)}, u32[]{:S(2)}, u32[]{:S(2)}) collective-permute-start(bf16[64,1152]{1,0:T(8,128)(2,1)S(1)} %collective-permute-done.a2), channel_id=1, source_target_pairs={{0,3},{1,4},{2,1},{3,6},{4,7},{5,0},{6,5},{7,2},{8,11},{9,12},{10,... | collective-permute-start | bytes 442376 | tf_op jit(solution)/shard_map/ppermute | solution.py:265
  17.5 1.5 %collective-permute-start.7 = (f32[128,256]{1,0:T(8,128)S(1)}, f32[128,256]{1,0:T(8,128)S(1)}, u32[]{:S(2)}, u32[]{:S(2)}) collective-permute-start(f32[128,256]{1,0:T(8,128)S(1)} %last.1.mine), channel_id=1, source_target_pairs={{0,1},{1,0},{2,3},{3,2},{4,5},{5,4},{6,7},{7,6},{8,9},{9,8},{10,11... | collective-permute-start | bytes 393224 | tf_op jit(solution)/shard_map/ppermute | solution.py:265
  17.8 1.2 %collective-permute-start.8 = (f32[8,128]{1,0:T(8,128)S(1)}, f32[8,128]{1,0:T(8,128)S(1)}, u32[]{:S(2)}, u32[]{:S(2)}) collective-permute-start(f32[8,128]{1,0:T(8,128)S(1)} %get-tuple-element.21.weights), channel_id=1, source_target_pairs={{0,1},{1,0},{2,3},{3,2},{4,5},{5,4},{6,7},{7,6},{8,9},{9,8},{10,11... | collective-permute-start | bytes 12296 | tf_op jit(solution)/shard_map/ppermute | solution.py:265
  19.3 3.5 %collective-permute-start.10 = (f32[64,128]{1,0:T(8,128)S(1)}, f32[64,128]{1,0:T(8,128)S(1)}, u32[]{:S(2)}, u32[]{:S(2)}) collective-permute-start(f32[64,128]{1,0:T(8,128)S(1)} %grads.1), channel_id=1, source_target_pairs={{0,5},{1,4},{2,7},{3,6},{4,1},{5,0},{6,3},{7,2},{8,13},{9,12},{10,... | collective-permute-start | bytes 98312 | tf_op jit(solution)/shard_map/ppermute | solution.py:265
  20.6 4.8 %collective-permute-start.11 = (f32[64,128]{1,0:T(8,128)S(1)}, f32[64,128]{1,0:T(8,128)S(1)}, u32[]{:S(2)}, u32[]{:S(2)}) collective-permute-start(f32[64,128]{1,0:T(8,128)S(1)} %grads.1), channel_id=1, source_target_pairs={{0,6},{1,7},{2,4},{3,5},{4,2},{5,3},{6,0},{7,1},{8,14},{9,15},{10,... | collective-permute-start | bytes 98312 | tf_op jit(solution)/shard_map/ppermute | solution.py:265
  22.3 3.6 %collective-permute-start.9 = (f32[64,128]{1,0:T(8,128)S(1)}, f32[64,128]{1,0:T(8,128)S(1)}, u32[]{:S(2)}, u32[]{:S(2)}) collective-permute-start(f32[64,128]{1,0:T(8,128)S(1)} %grads.1), channel_id=1, source_target_pairs={{0,3},{1,2},{2,1},{3,0},{4,7},{5,6},{6,5},{7,4},{8,11},{9,10},{10,... | collective-permute-start | bytes 98312 | tf_op jit(solution)/shard_map/ppermute | solution.py:265
  22.3 7.7 %collective-permute-start.15 = (bf16[32,2048]{1,0:T(8,128)(2,1)S(1)}, bf16[32,2048]{1,0:T(8,128)(2,1)S(1)}, u32[]{:S(2)}, u32[]{:S(2)}) collective-permute-start(bf16[32,2048]{1,0:T(8,128)(2,1)S(1)} %get-tuple-element.23), channel_id=1, source_target_pairs={{0,1},{1,0},{2,3},{3,2},{4,5},{5,4},{6,7},{7,6},{8,9},{9,8},{10,11... | collective-permute-start | bytes 393224 | tf_op jit(solution)/shard_map/ppermute | solution.py:265
  25.9 5.2 %collective-permute-start.12 = (f32[64,128]{1,0:T(8,128)S(1)}, f32[64,128]{1,0:T(8,128)S(1)}, u32[]{:S(2)}, u32[]{:S(2)}) collective-permute-start(f32[64,128]{1,0:T(8,128)S(1)} %add_add_fusion.m0), channel_id=1, source_target_pairs={{0,25},{1,24},{2,27},{3,26},{4,29},{5,28},{6,31},{7,30},{8,17},{9,... | collective-permute-start | bytes 98312 | tf_op jit(solution)/shard_map/ppermute | solution.py:265
  29.2 4.3 %collective-permute-start.13 = (f32[64,128]{1,0:T(8,128)S(1)}, f32[64,128]{1,0:T(8,128)S(1)}, u32[]{:S(2)}, u32[]{:S(2)}) collective-permute-start(f32[64,128]{1,0:T(8,128)S(1)} %add_add_fusion.m0), channel_id=1, source_target_pairs={{0,17},{1,16},{2,19},{3,18},{4,21},{5,20},{6,23},{7,22},{8,25},{9,... | collective-permute-start | bytes 98312 | tf_op jit(solution)/shard_map/ppermute | solution.py:265
  29.2 4.3 %collective-permute-start.14 = (f32[64,128]{1,0:T(8,128)S(1)}, f32[64,128]{1,0:T(8,128)S(1)}, u32[]{:S(2)}, u32[]{:S(2)}) collective-permute-start(f32[64,128]{1,0:T(8,128)S(1)} %add_add_fusion.m0), channel_id=1, source_target_pairs={{0,8},{1,9},{2,10},{3,11},{4,12},{5,13},{6,14},{7,15},{8,0},{9,1},... | collective-permute-start | bytes 98312 | tf_op jit(solution)/shard_map/ppermute | solution.py:265
  34.0 1.3 %collective-permute-start.16 = (f32[16,128]{1,0:T(8,128)S(1)}, f32[16,128]{1,0:T(8,128)S(1)}, u32[]{:S(2)}, u32[]{:S(2)}) collective-permute-start(f32[16,128]{1,0:T(8,128)S(1)} %products.1.mine), channel_id=1, source_target_pairs={{0,1},{1,0},{2,3},{3,2},{4,5},{5,4},{6,7},{7,6},{8,9},{9,8},{10,11... | collective-permute-start | bytes 24584 | tf_op jit(solution)/shard_map/ppermute | solution.py:265

commit v4 on v3

--- a/solution.py
+++ b/solution.py
@@ -124,59 +124,67 @@
     return nt(w, jnp.concatenate([near[:, pl.ds(base, rows)], far[:, pl.ds(start, rows)]], axis=0))
 
 
-def near_body(own, a1, a2, b, og2, inp2, og, inp, tests, ids, pg, px, near, t_own, t_far, rows,
-              near_s, ids_s, sems, *, wi, wo):
+def keep_body(_, og, inp, tests, ids, near, late, t_own, t_far, rows, ids_s, sems):
     seq, _, half = here()
     hf = t_own.shape[1]
-    size = a1.shape[1]
-    rest = wo - size
-    each = wo + wi
-    copies = column_copies(og, inp, near_s, near, seq, sems)
-    more = [
-        pltpu.make_async_copy(tests.at[:, pl.ds(pl.multiple_of(half * hf, hf), hf)], t_own, sems.at[8]),
-        pltpu.make_async_copy(tests.at[:, pl.ds(pl.multiple_of((1 - half) * hf, hf), hf)], t_far, sems.at[9]),
-        pltpu.make_async_copy(ids, ids_s, sems.at[10]),
-    ]
-    for c in copies + more:
+    copies = column_copies(og, inp, near, late, seq, sems)
+    copies.append(pltpu.make_async_copy(tests.at[:, pl.ds(pl.multiple_of(half * hf, hf), hf)], t_own, sems.at[8]))
+    copies.append(pltpu.make_async_copy(tests.at[:, pl.ds(pl.multiple_of((1 - half) * hf, hf), hf)], t_far, sems.at[9]))
+    copies.append(pltpu.make_async_copy(ids, ids_s, sems.at[10]))
+    for c in copies:
         c.start()
-    total, total_x = 0.0, 0.0
-    for k, w in ((0, own), (2, b), (1, None)):
-        base, shard = k * each, source(seq, k)
-        copies[2 * k].wait()
-        copies[2 * k + 1].wait()
-        if w is None:
-            total = total + project(a1[...], near_s, base, og2, shard, wo, 0)
-            total = total + project(a2[:, :rest], near_s, base + size, og2, shard, wo, size)
-            total_x = total_x + project(a2[:, rest:], near_s, base + wo, inp2, shard, wi, 0)
-        else:
-            total = total + project(w[:, :wo], near_s, base, og2, shard, wo, 0)
-            total_x = total_x + project(w[:, wo:], near_s, base + wo, inp2, shard, wi, 0)
-    pg[...] = total
-    px[...] = total_x
-    for c in copies[6:] + more:
+    for c in copies:
         c.wait()
     for r in range(rows.shape[0]):
         rows[r:r + 1, :] = jnp.full((1, rows.shape[1]), ids_s[r], jnp.int32)
 
 
+def after_body(x, _, out):
+    out[...] = x[...]
+
+
+def near_body(own, a1, a2, b, og2, inp2, near, pg, px, *, wi, wo):
+    seq, _, _ = here()
+    size = a1.shape[1]
+    rest = wo - size
+    total, total_x = 0.0, 0.0
+    for k, w in ((0, own), (2, b), (1, None)):
+        base, shard = k * (wo + wi), source(seq, k)
+        if w is None:
+            total = total + project(a1[...], near, base, og2, shard, wo, 0)
+            total = total + project(a2[:, :rest], near, base + size, og2, shard, wo, size)
+            total_x = total_x + project(a2[:, rest:], near, base + wo, inp2, shard, wi, 0)
+        else:
+            total = total + project(w[:, :wo], near, base, og2, shard, wo, 0)
+            total_x = total_x + project(w[:, wo:], near, base + wo, inp2, shard, wi, 0)
+    pg[...] = total
+    px[...] = total_x
+
+
 def diagonal_body(c1, pg_in, near, og2, pg, *, wo):
     seq, _, _ = here()
     pg[...] = pg_in[...] + project(c1[...], near, 0, og2, source(seq, 3), wo, 0)
 
 
-def last_body(c2, pg_in, px_in, near, og2, inp2, out, *, wi, wo):
+def last_body(c2, pg_in, px_in, near, og2, inp2, weights, out, *, wi, wo):
     seq, _, _ = here()
     rest = c2.shape[1] - wi
     rows = pg_in.shape[0]
     shard = source(seq, 3)
     out[:rows] = pg_in[...] + project(c2[:, :rest], near, wo - rest, og2, shard, wo, wo - rest)
     out[rows:2 * rows] = px_in[...] + project(c2[:, rest:], near, wo, inp2, shard, wi, 0)
-
-
-def grads_body(mine, far, weights, weights2, grads, pgs):
+    out[2 * rows:] = jnp.concatenate([weights[...], jnp.zeros_like(weights)], axis=1)
+
+
+def halves(x):
+    high = x.astype(jnp.bfloat16)
+    return [high, (x - high.astype(F32)).astype(jnp.bfloat16)]
+
+
+def grads_body(mine, far, grads, pgs):
     _, _, half = here()
     slots = pgs.shape[2]
-    rows = mine.shape[0] // 2
+    rows = (mine.shape[0] - 8) // 2
     hw = rows // 2
     pairs = hw // 2
     docs = grads.shape[0] // pairs
@@ -187,7 +195,7 @@
     for u in range(2):
         pgs[u] = jnp.where(half == 1, both[0][u][hw:], both[0][u][:hw])
     px = jnp.concatenate(both[1], axis=1)
-    tokens = jnp.concatenate([weights[...], weights2[...]], axis=1)
+    tokens = jnp.concatenate([mine[2 * rows:, :slots], far[2 * rows:, :slots]], axis=1)
     parts = []
     for q in range(2):
         some = jnp.concatenate([pgs[u, pl.ds(q, pairs, stride=2), :] for u in range(2)], axis=1)
@@ -208,15 +216,15 @@
     docs = out.shape[0]
     pairs = every.shape[0] // docs
     flat = jnp.concatenate([every[pl.ds(i, docs, stride=pairs), :] for i in range(pairs)], axis=1)
-    gram = nt(flat, flat, HIGH)
     own, far = t_own[...], t_far[...]
     core = seq & 1
-    tests = jnp.concatenate([jnp.where(core == 0, own, far), jnp.where(core == 0, far, own)], axis=0)
-    high = flat.astype(jnp.bfloat16)
-    rest = flat - high.astype(F32)
-    mid = rest.astype(jnp.bfloat16)
-    low = (rest - mid.astype(F32)).astype(jnp.bfloat16)
-    cross = nt(low, tests) + nt(mid, tests) + nt(high, tests)
+    high, low = halves(flat)
+    ntest = 2 * own.shape[0]
+    right = [jnp.where(core == 0, own, far), jnp.where(core == 0, far, own), high, low]
+    both = nt(jnp.concatenate([high, low], axis=0), jnp.concatenate(right, axis=0))
+    top, bottom = both[:docs], both[docs:]
+    cross = top[:, :ntest] + bottom[:, :ntest]
+    gram = top[:, ntest:ntest + docs] + (top[:, ntest + docs:] + bottom[:, ntest:ntest + docs])
     pad = jnp.zeros((docs, out.shape[1] - cross.shape[1] - docs), F32)
     out[...] = jnp.concatenate([cross, gram, pad], axis=1)
 
@@ -270,7 +278,7 @@
     def ring(x, step):
         return move(x, lambda z, s: (z, s ^ ((3, 5)[(s & 1) ^ step])))
 
-    size = (wo + wi) // 256 * 128
+    size = (wo + wi) * 5 // 8 // 128 * 128
     first, second, whole, weights = vmem_call(
         weights_body,
         [((width, size), bf), ((width, wo + wi - size), bf), ((width, wo + wi), bf), ((8, slots), F32)],
@@ -279,28 +287,29 @@
         name="weights",
     )
     a1, a2, b = ring(first, 0), ring(second, 0), ring(whole, 1)
-    weights2 = swap(weights)
     og2, inp2 = swap(og), swap(inp)
+    lanes = -(-(2 * ntest + ndocs) // 128) * 128
+    three, near, t_own, t_send, rows = vmem_call(
+        keep_body,
+        [((slots, 3 * (wo + wi)), bf), ((slots, wo + wi), bf)] + [((ntest, feat // 2), bf)] * 2 + [((ndocs, lanes), jnp.int32)],
+        [whole], hbm=[og, inp, test_grads, doc_ids],
+        scratch=[pltpu.SMEM((ndocs,), jnp.int32), pltpu.SemaphoreType.DMA((11,))], name="keep",
+    )
+    (a1,) = vmem_call(after_body, [(a1.shape, bf)], [a1, rows], name="after")
     c1 = ring(a1, 0)
     c2 = ring(a2, 0)
     part = ((width, 2 * slots), F32)
-    lanes = -(-(2 * ntest + ndocs) // 128) * 128
-    pg, px, near, t_own, t_send, rows = vmem_call(
-        functools.partial(near_body, wi=wi, wo=wo),
-        [part, part, ((slots, wo + wi), bf)] + [((ntest, feat // 2), bf)] * 2 + [((ndocs, lanes), jnp.int32)],
-        [whole, a1, a2, b, og2, inp2], hbm=[og, inp, test_grads, doc_ids],
-        scratch=[VMEM((slots, 3 * (wo + wi)), bf), pltpu.SMEM((ndocs,), jnp.int32), pltpu.SemaphoreType.DMA((11,))],
-        name="near",
-    )
-    t_far = swap(t_send)
+    pg, px = vmem_call(
+        functools.partial(near_body, wi=wi, wo=wo), [part, part], [whole, a1, a2, b, og2, inp2, three], name="near",
+    )
     (pg,) = vmem_call(functools.partial(diagonal_body, wo=wo), [part], [c1, pg, near, og2], name="diagonal")
     (mine,) = vmem_call(
-        functools.partial(last_body, wi=wi, wo=wo), [((2 * width, 2 * slots), F32)],
-        [c2, pg, px, near, og2, inp2], name="last",
+        functools.partial(last_body, wi=wi, wo=wo), [((2 * width + 8, 2 * slots), F32)],
+        [c2, pg, px, near, og2, inp2, weights], name="last",
     )
     pairs = hw // 2
     (grads,) = vmem_call(
-        grads_body, [((docs * pairs, 2 * width), F32)], [mine, swap(mine), weights, weights2],
+        grads_body, [((docs * pairs, 2 * width), F32)], [mine, swap(mine)],
         scratch=[VMEM((2, hw, slots), F32)], name="grads",
     )
     px = move(grads, lambda z, s: (z, s ^ 3))
@@ -310,6 +319,7 @@
     m3 = move(grads, lambda z, s: (z ^ 3, s ^ 1))
     m2 = move(grads, lambda z, s: (z ^ 2, s ^ 1))
     m1 = move(grads, lambda z, s: (z ^ 1, s))
+    t_far = swap(t_send)
     (mine,) = vmem_call(
         products_body, [((ndocs, lanes), F32)],
         [grads, m3, m2, m1, t_own, t_far],

time: 36.4 us -> 35 us (0.962)
  waiting for transfers between devices: 14.6 us -> 10.7 us
  starting transfers between devices: 15.1 us -> 17.6 us
    ppermute x17 -> x16, waiting for transfers between devices: 14.6 us -> 10.7 us  [move(): return lax.ppermute(x, ('dp', 'seq'), pairs)]
    ppermute x17 -> x16, starting transfers between devices: 15.1 us -> 17.6 us  [move(): return lax.ppermute(x, ('dp', 'seq'), pairs)]
    pallas_call x6 -> x8, Pallas kernels: 5.6 us -> 5.51 us  [vmem_call(): pl.pallas_call(body, out_shape=[VMEM(s, d) for s, d in outs], in_specs=sp...]
  transfers between devices with their start and end apart: 17 -> 16, of which waited for: 9 -> 9; matrix products, arithmetic and copies ran while one was open for 0% -> 0% of each run, Pallas kernels for 12% -> 13%
where the time goes in v4:
time: 35 us; the launch traced here: 34.9 us
  starting transfers between devices  17.6 us (50%)
  waiting for transfers between devices  10.7 us (31%)
  Pallas kernels  6.46 us (18%)
    ppermute x16, starting transfers between devices, move(): return lax.ppermute(x, ('dp', 'seq'), pairs)  17.6 us
    ppermute x16, waiting for transfers between devices, move(): return lax.ppermute(x, ('dp', 'seq'), pairs)  10.7 us
    pallas_call x8, Pallas kernels, vmem_call(): pl.pallas_call(body, out_shape=[VMEM(s, d) for s, d in outs], in_specs=sp...  5.51 us
    pallas_call x1, Pallas kernels, paired_chips(): pl.pallas_call(solve_body, out_shape=jax.ShapeDtypeStruct((ndocs, ntest),...  0.95 us
  transfers between devices with their start and end apart: 16, of which 9 were waited for; matrix products, arithmetic and copies ran while one was open for 0% of the time, Pallas kernels for 13%

profile of v4, /device:TPU:0, one launch (start us, length us, event | category | flops | bytes accessed | tf_op | source)
XLA Modules:
  0.0 34.9 jit_solution(17982971484328795191)
XLA Ops:
  0.0 0.5 %collective-permute-start.5 = (bf16[128,14336]{1,0:T(8,128)(2,1)}, bf16[128,14336]{1,0:T(8,128)(2,1)S(1)}, u32[]{:S(2)}, u32[]{:S(2)}) collective-permute-start(bf16[128,14336]{1,0:T(8,128)(2,1)} %bitcast.4), channel_id=1, source_target_pairs={{0,1},{1,0},{2,3},{3,2},{4,5},{5,4},{6,7},{7,6},{8,9},{9,8},{10,11... | collective-permute-start | bytes 11010056 | tf_op jit(solution)/shard_map/ppermute | solution.py:273
  0.5 1.2 %weights.1 = (bf16[64,1408]{1,0:T(8,128)(2,1)S(1)}, bf16[64,896]{1,0:T(8,128)(2,1)S(1)}, bf16[64,2304]{1,0:T(8,128)(2,1)S(1)}, f32[8,128]{1,0:T(8,128)S(1)}) custom-call(s32[1,128]{1,0:T(1,128)} %valid.1, s32[1,4]{1,0:T(1,128)} %blocks.1, bf16[64,1792]{1,0:T(8,128)(2,1)} %bitcast.8, bf16[64,512]{1,0:T(8,128)(2,1)} %bitcast.9), custom_call_target="tpu_custom_call" | custom-call | tf_op jit(solution)/shard_map/weights/pallas_call | solution.py:58
  1.7 2.6 %collective-permute-start.2 = (bf16[64,1408]{1,0:T(8,128)(2,1)S(1)}, bf16[64,1408]{1,0:T(8,128)(2,1)S(1)}, u32[]{:S(2)}, u32[]{:S(2)}) collective-permute-start(bf16[64,1408]{1,0:T(8,128)(2,1)S(1)} %get-tuple-element.17), channel_id=1, source_target_pairs={{0,3},{1,4},{2,1},{3,6},{4,7},{5,0},{6,5},{7,2},{8,11},{9,12},{10,... | collective-permute-start | bytes 540680 | tf_op jit(solution)/shard_map/ppermute | solution.py:273
  4.4 1.7 %collective-permute-start = (bf16[64,896]{1,0:T(8,128)(2,1)S(1)}, bf16[64,896]{1,0:T(8,128)(2,1)S(1)}, u32[]{:S(2)}, u32[]{:S(2)}) collective-permute-start(bf16[64,896]{1,0:T(8,128)(2,1)S(1)} %get-tuple-element.16), channel_id=1, source_target_pairs={{0,3},{1,4},{2,1},{3,6},{4,7},{5,0},{6,5},{7,2},{8,11},{9,12},{10,... | collective-permute-start | bytes 344072 | tf_op jit(solution)/shard_map/ppermute | solution.py:273
  6.0 1.8 %keep.1 = (bf16[128,6912]{1,0:T(8,128)(2,1)S(1)}, bf16[128,2304]{1,0:T(8,128)(2,1)S(1)}, bf16[32,2048]{1,0:T(8,128)(2,1)S(1)}, bf16[32,2048]{1,0:T(8,128)(2,1)S(1)}, s32[16,128]{1,0:T(8,128)S(1)}) custom-call(bf16[64,2304]{1,0:T(8,128)(2,1)S(1)} %get-tuple-element.18._.own, bf16[128,14336]{1,0:T(8,128)(2,1)} %bitcast.5, bf16[128,4096]{1,0:T(8,128)(2,1)} %bitcast.7, ...), custom_call_target="tpu_custom_call" | custom-call | tf_op jit(solution)/shard_map/keep/pallas_call | solution.py:58
  7.8 1.4 %collective-permute-done.2.x = bf16[64,1408]{1,0:T(8,128)(2,1)S(1)} collective-permute-done((bf16[64,1408]{1,0:T(8,128)(2,1)S(1)}, bf16[64,1408]{1,0:T(8,128)(2,1)S(1)}, u32[]{:S(2)}, u32[]{:S(2)}) %collective-permute-start.2) | collective-permute-done | bytes 180256 | tf_op jit(solution)/shard_map/ppermute | solution.py:273
  9.3 2.3 %collective-permute-start.3 = (bf16[64,1408]{1,0:T(8,128)(2,1)S(1)}, bf16[64,1408]{1,0:T(8,128)(2,1)S(1)}, u32[]{:S(2)}, u32[]{:S(2)}) collective-permute-start(bf16[64,1408]{1,0:T(8,128)(2,1)S(1)} %after.1.a1), channel_id=1, source_target_pairs={{0,3},{1,4},{2,1},{3,6},{4,7},{5,0},{6,5},{7,2},{8,11},{9,12},{10,... | collective-permute-start | bytes 540680 | tf_op jit(solution)/shard_map/ppermute | solution.py:273
  11.6 2.1 %collective-permute-start.1 = (bf16[64,896]{1,0:T(8,128)(2,1)S(1)}, bf16[64,896]{1,0:T(8,128)(2,1)S(1)}, u32[]{:S(2)}, u32[]{:S(2)}) collective-permute-start(bf16[64,896]{1,0:T(8,128)(2,1)S(1)} %collective-permute-done.a2), channel_id=1, source_target_pairs={{0,3},{1,4},{2,1},{3,6},{4,7},{5,0},{6,5},{7,2},{8,11},{9,12},{10,... | collective-permute-start | bytes 344072 | tf_op jit(solution)/shard_map/ppermute | solution.py:273
  13.7 1.2 %near.1 = (f32[64,256]{1,0:T(8,128)S(1)}, f32[64,256]{1,0:T(8,128)S(1)}) custom-call(bf16[64,2304]{1,0:T(8,128)(2,1)S(1)} %get-tuple-element.18._.own, bf16[64,1408]{1,0:T(8,128)(2,1)S(1)} %after.1.a1, bf16[64,896]{1,0:T(8,128)(2,1)S(1)} %collective-permute-done.a2, bf16[64,2304]{1,0:T(8,128)(2,1)S(1)} %collective-permute-done.4.b, ...), custom_call_target="tpu_custom_call" | custom-call | tf_op jit(solution)/shard_map/near/pallas_call | solution.py:58
  14.9 0.4 %diagonal.1.pg_in = f32[64,256]{1,0:T(8,128)S(1)} custom-call(bf16[64,1408]{1,0:T(8,128)(2,1)S(1)} %collective-permute-done.3.c1, f32[64,256]{1,0:T(8,128)S(1)} %get-tuple-element.21.pg_in, bf16[128,2304]{1,0:T(8,128)(2,1)S(1)} %get-tuple-element.22.near, bf16[128,14336]{1,0:T(8,128)(2,1)S(1)} %collective-permute-done.5.og2), custom_call_target="tpu_custom_call" | custom-call | tf_op jit(solution)/shard_map/diagonal/pallas_call | solution.py:58
  15.2 0.8 %collective-permute-done.1.c2 = bf16[64,896]{1,0:T(8,128)(2,1)S(1)} collective-permute-done((bf16[64,896]{1,0:T(8,128)(2,1)S(1)}, bf16[64,896]{1,0:T(8,128)(2,1)S(1)}, u32[]{:S(2)}, u32[]{:S(2)}) %collective-permute-start.1) | collective-permute-done | bytes 114720 | tf_op jit(solution)/shard_map/ppermute | solution.py:273
  16.4 1.3 %collective-permute-done.7.far = f32[136,256]{1,0:T(8,128)S(1)} collective-permute-done((f32[136,256]{1,0:T(8,128)S(1)}, f32[136,256]{1,0:T(8,128)S(1)}, u32[]{:S(2)}, u32[]{:S(2)}) %collective-permute-start.7) | collective-permute-done | bytes 139296 | tf_op jit(solution)/shard_map/ppermute | solution.py:273
  18.1 3.1 %collective-permute-start.10 = (f32[64,128]{1,0:T(8,128)S(1)}, f32[64,128]{1,0:T(8,128)S(1)}, u32[]{:S(2)}, u32[]{:S(2)}) collective-permute-start(f32[64,128]{1,0:T(8,128)S(1)} %grads.1), channel_id=1, source_target_pairs={{0,6},{1,7},{2,4},{3,5},{4,2},{5,3},{6,0},{7,1},{8,14},{9,15},{10,... | collective-permute-start | bytes 98312 | tf_op jit(solution)/shard_map/ppermute | solution.py:273
  21.2 0.4 %collective-permute-start.9 = (f32[64,128]{1,0:T(8,128)S(1)}, f32[64,128]{1,0:T(8,128)S(1)}, u32[]{:S(2)}, u32[]{:S(2)}) collective-permute-start(f32[64,128]{1,0:T(8,128)S(1)} %grads.1), channel_id=1, source_target_pairs={{0,5},{1,4},{2,7},{3,6},{4,1},{5,0},{6,3},{7,2},{8,13},{9,12},{10,... | collective-permute-start | bytes 98312 | tf_op jit(solution)/shard_map/ppermute | solution.py:273
  21.5 0.4 %collective-permute-start.14 = (bf16[32,2048]{1,0:T(8,128)(2,1)S(1)}, bf16[32,2048]{1,0:T(8,128)(2,1)S(1)}, u32[]{:S(2)}, u32[]{:S(2)}) collective-permute-start(bf16[32,2048]{1,0:T(8,128)(2,1)S(1)} %get-tuple-element.26), channel_id=1, source_target_pairs={{0,1},{1,0},{2,3},{3,2},{4,5},{5,4},{6,7},{7,6},{8,9},{9,8},{10,11... | collective-permute-start | bytes 393224 | tf_op jit(solution)/shard_map/ppermute | solution.py:273
  21.9 1.2 %collective-permute-done.10 = f32[64,128]{1,0:T(8,128)S(1)} collective-permute-done((f32[64,128]{1,0:T(8,128)S(1)}, f32[64,128]{1,0:T(8,128)S(1)}, u32[]{:S(2)}, u32[]{:S(2)}) %collective-permute-start.10) | collective-permute-done | bytes 32800 | tf_op jit(solution)/shard_map/ppermute | solution.py:273
  23.1 1.5 %collective-permute-done.8 = f32[64,128]{1,0:T(8,128)S(1)} collective-permute-done((f32[64,128]{1,0:T(8,128)S(1)}, f32[64,128]{1,0:T(8,128)S(1)}, u32[]{:S(2)}, u32[]{:S(2)}) %collective-permute-start.8) | collective-permute-done | bytes 32800 | tf_op jit(solution)/shard_map/ppermute | solution.py:273
  24.6 3.4 %collective-permute-start.11 = (f32[64,128]{1,0:T(8,128)S(1)}, f32[64,128]{1,0:T(8,128)S(1)}, u32[]{:S(2)}, u32[]{:S(2)}) collective-permute-start(f32[64,128]{1,0:T(8,128)S(1)} %add_add_fusion.m0), channel_id=1, source_target_pairs={{0,25},{1,24},{2,27},{3,26},{4,29},{5,28},{6,31},{7,30},{8,17},{9,... | collective-permute-start | bytes 98312 | tf_op jit(solution)/shard_map/ppermute | solution.py:273
  28.1 0.7 %collective-permute-start.13 = (f32[64,128]{1,0:T(8,128)S(1)}, f32[64,128]{1,0:T(8,128)S(1)}, u32[]{:S(2)}, u32[]{:S(2)}) collective-permute-start(f32[64,128]{1,0:T(8,128)S(1)} %add_add_fusion.m0), channel_id=1, source_target_pairs={{0,8},{1,9},{2,10},{3,11},{4,12},{5,13},{6,14},{7,15},{8,0},{9,1},... | collective-permute-start | bytes 98312 | tf_op jit(solution)/shard_map/ppermute | solution.py:273
  28.8 1.0 %collective-permute-done.11.m3 = f32[64,128]{1,0:T(8,128)S(1)} collective-permute-done((f32[64,128]{1,0:T(8,128)S(1)}, f32[64,128]{1,0:T(8,128)S(1)}, u32[]{:S(2)}, u32[]{:S(2)}) %collective-permute-start.11) | collective-permute-done | bytes 32800 | tf_op jit(solution)/shard_map/ppermute | solution.py:273
  29.8 2.5 %collective-permute-done.12.m2 = f32[64,128]{1,0:T(8,128)S(1)} collective-permute-done((f32[64,128]{1,0:T(8,128)S(1)}, f32[64,128]{1,0:T(8,128)S(1)}, u32[]{:S(2)}, u32[]{:S(2)}) %collective-permute-start.12) | collective-permute-done | bytes 32800 | tf_op jit(solution)/shard_map/ppermute | solution.py:273
  32.3 0.4 %products.1.mine = f32[16,128]{1,0:T(8,128)S(1)} custom-call(f32[64,128]{1,0:T(8,128)S(1)} %add_add_fusion.m0, f32[64,128]{1,0:T(8,128)S(1)} %collective-permute-done.11.m3, f32[64,128]{1,0:T(8,128)S(1)} %collective-permute-done.12.m2, f32[64,128]{1,0:T(8,128)S(1)} %collective-permute-done.13.m1, bf16[32,2048]{1,0:T(8,128)(2,1)S(1)} %get-tuple-element.25.t_own, ...), custom_call_target="tpu_custom_call" | custom-call | tf_op jit(solution)/shard_map/products/pallas_call | solution.py:58
  33.1 0.9 %collective-permute-done.15.far = f32[16,128]{1,0:T(8,128)S(1)} collective-permute-done((f32[16,128]{1,0:T(8,128)S(1)}, f32[16,128]{1,0:T(8,128)S(1)}, u32[]{:S(2)}, u32[]{:S(2)}) %collective-permute-start.15) | collective-permute-done | bytes 8224 | tf_op jit(solution)/shard_map/ppermute | solution.py:273
  33.9 0.9 %solve.1 = f32[16,32]{1,0:T(8,128)} custom-call(f32[16,128]{1,0:T(8,128)S(1)} %products.1.mine, f32[16,128]{1,0:T(8,128)S(1)} %collective-permute-done.15.far, s32[16,128]{1,0:T(8,128)S(1)} %get-tuple-element.19._.rows), custom_call_target="tpu_custom_call" | custom-call | tf_op jit(solution)/shard_map/solve/pallas_call | solution.py:328
  (18 shorter events, 1.3 us)
Async XLA Ops:
  0.0 13.7 %collective-permute-start.5 = (bf16[128,14336]{1,0:T(8,128)(2,1)}, bf16[128,14336]{1,0:T(8,128)(2,1)S(1)}, u32[]{:S(2)}, u32[]{:S(2)}) collective-permute-start(bf16[128,14336]{1,0:T(8,128)(2,1)} %bitcast.4), channel_id=1, source_target_pairs={{0,1},{1,0},{2,3},{3,2},{4,5},{5,4},{6,7},{7,6},{8,9},{9,8},{10,11... | collective-permute-start | bytes 11010056 | tf_op jit(solution)/shard_map/ppermute | solution.py:273
  0.5 13.2 %collective-permute-start.6 = (bf16[128,4096]{1,0:T(8,128)(2,1)}, bf16[128,4096]{1,0:T(8,128)(2,1)S(1)}, u32[]{:S(2)}, u32[]{:S(2)}) collective-permute-start(bf16[128,4096]{1,0:T(8,128)(2,1)} %bitcast.6), channel_id=1, source_target_pairs={{0,1},{1,0},{2,3},{3,2},{4,5},{5,4},{6,7},{7,6},{8,9},{9,8},{10,11... | collective-permute-start | bytes 3145736 | tf_op jit(solution)/shard_map/ppermute | solution.py:273
  1.7 7.5 %collective-permute-start.2 = (bf16[64,1408]{1,0:T(8,128)(2,1)S(1)}, bf16[64,1408]{1,0:T(8,128)(2,1)S(1)}, u32[]{:S(2)}, u32[]{:S(2)}) collective-permute-start(bf16[64,1408]{1,0:T(8,128)(2,1)S(1)} %get-tuple-element.17), channel_id=1, source_target_pairs={{0,3},{1,4},{2,1},{3,6},{4,7},{5,0},{6,5},{7,2},{8,11},{9,12},{10,... | collective-permute-start | bytes 540680 | tf_op jit(solution)/shard_map/ppermute | solution.py:273
  4.3 9.4 %collective-permute-start.4 = (bf16[64,2304]{1,0:T(8,128)(2,1)S(1)}, bf16[64,2304]{1,0:T(8,128)(2,1)S(1)}, u32[]{:S(2)}, u32[]{:S(2)}) collective-permute-start(bf16[64,2304]{1,0:T(8,128)(2,1)S(1)} %get-tuple-element.18._.own), channel_id=1, source_target_pairs={{0,5},{1,2},{2,7},{3,0},{4,1},{5,6},{6,3},{7,4},{8,13},{9,10},{10,... | collective-permute-start | bytes 884744 | tf_op jit(solution)/shard_map/ppermute | solution.py:273
  4.4 7.2 %collective-permute-start = (bf16[64,896]{1,0:T(8,128)(2,1)S(1)}, bf16[64,896]{1,0:T(8,128)(2,1)S(1)}, u32[]{:S(2)}, u32[]{:S(2)}) collective-permute-start(bf16[64,896]{1,0:T(8,128)(2,1)S(1)} %get-tuple-element.16), channel_id=1, source_target_pairs={{0,3},{1,4},{2,1},{3,6},{4,7},{5,0},{6,5},{7,2},{8,11},{9,12},{10,... | collective-permute-start | bytes 344072 | tf_op jit(solution)/shard_map/ppermute | solution.py:273
  9.3 5.6 %collective-permute-start.3 = (bf16[64,1408]{1,0:T(8,128)(2,1)S(1)}, bf16[64,1408]{1,0:T(8,128)(2,1)S(1)}, u32[]{:S(2)}, u32[]{:S(2)}) collective-permute-start(bf16[64,1408]{1,0:T(8,128)(2,1)S(1)} %after.1.a1), channel_id=1, source_target_pairs={{0,3},{1,4},{2,1},{3,6},{4,7},{5,0},{6,5},{7,2},{8,11},{9,12},{10,... | collective-permute-start | bytes 540680 | tf_op jit(solution)/shard_map/ppermute | solution.py:273
  11.6 4.4 %collective-permute-start.1 = (bf16[64,896]{1,0:T(8,128)(2,1)S(1)}, bf16[64,896]{1,0:T(8,128)(2,1)S(1)}, u32[]{:S(2)}, u32[]{:S(2)}) collective-permute-start(bf16[64,896]{1,0:T(8,128)(2,1)S(1)} %collective-permute-done.a2), channel_id=1, source_target_pairs={{0,3},{1,4},{2,1},{3,6},{4,7},{5,0},{6,5},{7,2},{8,11},{9,12},{10,... | collective-permute-start | bytes 344072 | tf_op jit(solution)/shard_map/ppermute | solution.py:273
  16.3 1.4 %collective-permute-start.7 = (f32[136,256]{1,0:T(8,128)S(1)}, f32[136,256]{1,0:T(8,128)S(1)}, u32[]{:S(2)}, u32[]{:S(2)}) collective-permute-start(f32[136,256]{1,0:T(8,128)S(1)} %last.1.mine), channel_id=1, source_target_pairs={{0,1},{1,0},{2,3},{3,2},{4,5},{5,4},{6,7},{7,6},{8,9},{9,8},{10,11... | collective-permute-start | bytes 417800 | tf_op jit(solution)/shard_map/ppermute | solution.py:273
  18.1 5.0 %collective-permute-start.10 = (f32[64,128]{1,0:T(8,128)S(1)}, f32[64,128]{1,0:T(8,128)S(1)}, u32[]{:S(2)}, u32[]{:S(2)}) collective-permute-start(f32[64,128]{1,0:T(8,128)S(1)} %grads.1), channel_id=1, source_target_pairs={{0,6},{1,7},{2,4},{3,5},{4,2},{5,3},{6,0},{7,1},{8,14},{9,15},{10,... | collective-permute-start | bytes 98312 | tf_op jit(solution)/shard_map/ppermute | solution.py:273
  21.2 3.4 %collective-permute-start.8 = (f32[64,128]{1,0:T(8,128)S(1)}, f32[64,128]{1,0:T(8,128)S(1)}, u32[]{:S(2)}, u32[]{:S(2)}) collective-permute-start(f32[64,128]{1,0:T(8,128)S(1)} %grads.1), channel_id=1, source_target_pairs={{0,3},{1,2},{2,1},{3,0},{4,7},{5,6},{6,5},{7,4},{8,11},{9,10},{10,... | collective-permute-start | bytes 98312 | tf_op jit(solution)/shard_map/ppermute | solution.py:273
  21.2 3.4 %collective-permute-start.9 = (f32[64,128]{1,0:T(8,128)S(1)}, f32[64,128]{1,0:T(8,128)S(1)}, u32[]{:S(2)}, u32[]{:S(2)}) collective-permute-start(f32[64,128]{1,0:T(8,128)S(1)} %grads.1), channel_id=1, source_target_pairs={{0,5},{1,4},{2,7},{3,6},{4,1},{5,0},{6,3},{7,2},{8,13},{9,12},{10,... | collective-permute-start | bytes 98312 | tf_op jit(solution)/shard_map/ppermute | solution.py:273
  21.5 7.3 %collective-permute-start.14 = (bf16[32,2048]{1,0:T(8,128)(2,1)S(1)}, bf16[32,2048]{1,0:T(8,128)(2,1)S(1)}, u32[]{:S(2)}, u32[]{:S(2)}) collective-permute-start(bf16[32,2048]{1,0:T(8,128)(2,1)S(1)} %get-tuple-element.26), channel_id=1, source_target_pairs={{0,1},{1,0},{2,3},{3,2},{4,5},{5,4},{6,7},{7,6},{8,9},{9,8},{10,11... | collective-permute-start | bytes 393224 | tf_op jit(solution)/shard_map/ppermute | solution.py:273
  24.6 5.2 %collective-permute-start.11 = (f32[64,128]{1,0:T(8,128)S(1)}, f32[64,128]{1,0:T(8,128)S(1)}, u32[]{:S(2)}, u32[]{:S(2)}) collective-permute-start(f32[64,128]{1,0:T(8,128)S(1)} %add_add_fusion.m0), channel_id=1, source_target_pairs={{0,25},{1,24},{2,27},{3,26},{4,29},{5,28},{6,31},{7,30},{8,17},{9,... | collective-permute-start | bytes 98312 | tf_op jit(solution)/shard_map/ppermute | solution.py:273
  28.1 4.3 %collective-permute-start.12 = (f32[64,128]{1,0:T(8,128)S(1)}, f32[64,128]{1,0:T(8,128)S(1)}, u32[]{:S(2)}, u32[]{:S(2)}) collective-permute-start(f32[64,128]{1,0:T(8,128)S(1)} %add_add_fusion.m0), channel_id=1, source_target_pairs={{0,17},{1,16},{2,19},{3,18},{4,21},{5,20},{6,23},{7,22},{8,25},{9,... | collective-permute-start | bytes 98312 | tf_op jit(solution)/shard_map/ppermute | solution.py:273
  28.1 4.3 %collective-permute-start.13 = (f32[64,128]{1,0:T(8,128)S(1)}, f32[64,128]{1,0:T(8,128)S(1)}, u32[]{:S(2)}, u32[]{:S(2)}) collective-permute-start(f32[64,128]{1,0:T(8,128)S(1)} %add_add_fusion.m0), channel_id=1, source_target_pairs={{0,8},{1,9},{2,10},{3,11},{4,12},{5,13},{6,14},{7,15},{8,0},{9,1},... | collective-permute-start | bytes 98312 | tf_op jit(solution)/shard_map/ppermute | solution.py:273
  32.7 1.2 %collective-permute-start.15 = (f32[16,128]{1,0:T(8,128)S(1)}, f32[16,128]{1,0:T(8,128)S(1)}, u32[]{:S(2)}, u32[]{:S(2)}) collective-permute-start(f32[16,128]{1,0:T(8,128)S(1)} %products.1.mine), channel_id=1, source_target_pairs={{0,1},{1,0},{2,3},{3,2},{4,5},{5,4},{6,7},{7,6},{8,9},{9,8},{10,11... | collective-permute-start | bytes 24584 | tf_op jit(solution)/shard_map/ppermute | solution.py:273

commit v5 on v4

--- a/solution.py
+++ b/solution.py
@@ -75,20 +75,18 @@
 def weights_body(valid, blocks, out_t, in_t, first, second, whole, weights, valid_v, blocks_s, sems):
     seq, _, _ = here()
     rows_out, rows_in, size = out_t.shape[1], in_t.shape[1], first.shape[1]
-    rest = rows_out - size
     copies = [
-        pltpu.make_async_copy(out_t.at[:, pl.ds(0, size)], first, sems.at[0]),
-        pltpu.make_async_copy(out_t.at[:, pl.ds(size, rest)], second.at[:, pl.ds(0, rest)], sems.at[1]),
-        pltpu.make_async_copy(in_t, second.at[:, pl.ds(rest, rows_in)], sems.at[2]),
-        pltpu.make_async_copy(out_t, whole.at[:, pl.ds(0, rows_out)], sems.at[3]),
-        pltpu.make_async_copy(in_t, whole.at[:, pl.ds(rows_out, rows_in)], sems.at[4]),
-        pltpu.make_async_copy(valid, valid_v, sems.at[5]),
-        pltpu.make_async_copy(blocks, blocks_s, sems.at[6]),
+        pltpu.make_async_copy(valid, valid_v, sems.at[0]),
+        pltpu.make_async_copy(blocks, blocks_s, sems.at[1]),
+        pltpu.make_async_copy(out_t, whole.at[:, pl.ds(0, rows_out)], sems.at[2]),
+        pltpu.make_async_copy(in_t, whole.at[:, pl.ds(rows_out, rows_in)], sems.at[3]),
     ]
     for c in copies:
         c.start()
     for c in copies:
         c.wait()
+    first[...] = whole[:, :size]
+    second[...] = whole[:, size:]
     slots = valid.shape[1]
     blk = (seq * slots + lax.broadcasted_iota(jnp.int32, weights.shape, 1)) // BLOCK
     row = lax.broadcasted_iota(jnp.int32, weights.shape, 0)
@@ -283,7 +281,7 @@
         weights_body,
         [((width, size), bf), ((width, wo + wi - size), bf), ((width, wo + wi), bf), ((8, slots), F32)],
         [], hbm=[valid, doc_blocks, proj_out.T, proj_in.T],
-        scratch=[VMEM((1, slots), jnp.int32), pltpu.SMEM((1, docs), jnp.int32), pltpu.SemaphoreType.DMA((7,))],
+        scratch=[VMEM((1, slots), jnp.int32), pltpu.SMEM((1, docs), jnp.int32), pltpu.SemaphoreType.DMA((4,))],
         name="weights",
     )
     a1, a2, b = ring(first, 0), ring(second, 0), ring(whole, 1)

time: 35 us -> 34.9 us (level)
  no operation moved by 1% of the time
where the time goes in v5:
time: 34.9 us; the launch traced here: 34.7 us
  starting transfers between devices  17.6 us (50%)
  waiting for transfers between devices  10.7 us (31%)
  Pallas kernels  6.31 us (18%)
    ppermute x16, starting transfers between devices, move(): return lax.ppermute(x, ('dp', 'seq'), pairs)  17.6 us
    ppermute x16, waiting for transfers between devices, move(): return lax.ppermute(x, ('dp', 'seq'), pairs)  10.7 us
    pallas_call x8, Pallas kernels, vmem_call(): pl.pallas_call(body, out_shape=[VMEM(s, d) for s, d in outs], in_specs=sp...  5.36 us
    pallas_call x1, Pallas kernels, paired_chips(): pl.pallas_call(solve_body, out_shape=jax.ShapeDtypeStruct((ndocs, ntest),...  0.95 us
  transfers between devices with their start and end apart: 16, of which 9 were waited for; matrix products, arithmetic and copies ran while one was open for 0% of the time, Pallas kernels for 13%

profile of v5, /device:TPU:0, one launch (start us, length us, event | category | flops | bytes accessed | tf_op | source)
XLA Modules:
  0.0 34.7 jit_solution(12898481462977864911)
XLA Ops:
  0.0 0.5 %collective-permute-start.5 = (bf16[128,14336]{1,0:T(8,128)(2,1)}, bf16[128,14336]{1,0:T(8,128)(2,1)S(1)}, u32[]{:S(2)}, u32[]{:S(2)}) collective-permute-start(bf16[128,14336]{1,0:T(8,128)(2,1)} %bitcast.4), channel_id=1, source_target_pairs={{0,1},{1,0},{2,3},{3,2},{4,5},{5,4},{6,7},{7,6},{8,9},{9,8},{10,11... | collective-permute-start | bytes 11010056 | tf_op jit(solution)/shard_map/ppermute | solution.py:271
  0.5 1.0 %weights.1 = (bf16[64,1408]{1,0:T(8,128)(2,1)S(1)}, bf16[64,896]{1,0:T(8,128)(2,1)S(1)}, bf16[64,2304]{1,0:T(8,128)(2,1)S(1)}, f32[8,128]{1,0:T(8,128)S(1)}) custom-call(s32[1,128]{1,0:T(1,128)} %valid.1, s32[1,4]{1,0:T(1,128)} %blocks.1, bf16[64,1792]{1,0:T(8,128)(2,1)} %bitcast.8, bf16[64,512]{1,0:T(8,128)(2,1)} %bitcast.9), custom_call_target="tpu_custom_call" | custom-call | tf_op jit(solution)/shard_map/weights/pallas_call | solution.py:58
  1.5 2.6 %collective-permute-start.2 = (bf16[64,1408]{1,0:T(8,128)(2,1)S(1)}, bf16[64,1408]{1,0:T(8,128)(2,1)S(1)}, u32[]{:S(2)}, u32[]{:S(2)}) collective-permute-start(bf16[64,1408]{1,0:T(8,128)(2,1)S(1)} %get-tuple-element.17), channel_id=1, source_target_pairs={{0,3},{1,4},{2,1},{3,6},{4,7},{5,0},{6,5},{7,2},{8,11},{9,12},{10,... | collective-permute-start | bytes 540680 | tf_op jit(solution)/shard_map/ppermute | solution.py:271
  4.2 1.7 %collective-permute-start = (bf16[64,896]{1,0:T(8,128)(2,1)S(1)}, bf16[64,896]{1,0:T(8,128)(2,1)S(1)}, u32[]{:S(2)}, u32[]{:S(2)}) collective-permute-start(bf16[64,896]{1,0:T(8,128)(2,1)S(1)} %get-tuple-element.16), channel_id=1, source_target_pairs={{0,3},{1,4},{2,1},{3,6},{4,7},{5,0},{6,5},{7,2},{8,11},{9,12},{10,... | collective-permute-start | bytes 344072 | tf_op jit(solution)/shard_map/ppermute | solution.py:271
  5.9 1.8 %keep.1 = (bf16[128,6912]{1,0:T(8,128)(2,1)S(1)}, bf16[128,2304]{1,0:T(8,128)(2,1)S(1)}, bf16[32,2048]{1,0:T(8,128)(2,1)S(1)}, bf16[32,2048]{1,0:T(8,128)(2,1)S(1)}, s32[16,128]{1,0:T(8,128)S(1)}) custom-call(bf16[64,2304]{1,0:T(8,128)(2,1)S(1)} %get-tuple-element.18._.own, bf16[128,14336]{1,0:T(8,128)(2,1)} %bitcast.5, bf16[128,4096]{1,0:T(8,128)(2,1)} %bitcast.7, ...), custom_call_target="tpu_custom_call" | custom-call | tf_op jit(solution)/shard_map/keep/pallas_call | solution.py:58
  7.7 1.4 %collective-permute-done.2.x = bf16[64,1408]{1,0:T(8,128)(2,1)S(1)} collective-permute-done((bf16[64,1408]{1,0:T(8,128)(2,1)S(1)}, bf16[64,1408]{1,0:T(8,128)(2,1)S(1)}, u32[]{:S(2)}, u32[]{:S(2)}) %collective-permute-start.2) | collective-permute-done | bytes 180256 | tf_op jit(solution)/shard_map/ppermute | solution.py:271
  9.1 2.3 %collective-permute-start.3 = (bf16[64,1408]{1,0:T(8,128)(2,1)S(1)}, bf16[64,1408]{1,0:T(8,128)(2,1)S(1)}, u32[]{:S(2)}, u32[]{:S(2)}) collective-permute-start(bf16[64,1408]{1,0:T(8,128)(2,1)S(1)} %after.1.a1), channel_id=1, source_target_pairs={{0,3},{1,4},{2,1},{3,6},{4,7},{5,0},{6,5},{7,2},{8,11},{9,12},{10,... | collective-permute-start | bytes 540680 | tf_op jit(solution)/shard_map/ppermute | solution.py:271
  11.4 2.1 %collective-permute-start.1 = (bf16[64,896]{1,0:T(8,128)(2,1)S(1)}, bf16[64,896]{1,0:T(8,128)(2,1)S(1)}, u32[]{:S(2)}, u32[]{:S(2)}) collective-permute-start(bf16[64,896]{1,0:T(8,128)(2,1)S(1)} %collective-permute-done.a2), channel_id=1, source_target_pairs={{0,3},{1,4},{2,1},{3,6},{4,7},{5,0},{6,5},{7,2},{8,11},{9,12},{10,... | collective-permute-start | bytes 344072 | tf_op jit(solution)/shard_map/ppermute | solution.py:271
  13.5 1.2 %near.1 = (f32[64,256]{1,0:T(8,128)S(1)}, f32[64,256]{1,0:T(8,128)S(1)}) custom-call(bf16[64,2304]{1,0:T(8,128)(2,1)S(1)} %get-tuple-element.18._.own, bf16[64,1408]{1,0:T(8,128)(2,1)S(1)} %after.1.a1, bf16[64,896]{1,0:T(8,128)(2,1)S(1)} %collective-permute-done.a2, bf16[64,2304]{1,0:T(8,128)(2,1)S(1)} %collective-permute-done.4.b, ...), custom_call_target="tpu_custom_call" | custom-call | tf_op jit(solution)/shard_map/near/pallas_call | solution.py:58
  14.7 0.4 %diagonal.1.pg_in = f32[64,256]{1,0:T(8,128)S(1)} custom-call(bf16[64,1408]{1,0:T(8,128)(2,1)S(1)} %collective-permute-done.3.c1, f32[64,256]{1,0:T(8,128)S(1)} %get-tuple-element.21.pg_in, bf16[128,2304]{1,0:T(8,128)(2,1)S(1)} %get-tuple-element.22.near, bf16[128,14336]{1,0:T(8,128)(2,1)S(1)} %collective-permute-done.5.og2), custom_call_target="tpu_custom_call" | custom-call | tf_op jit(solution)/shard_map/diagonal/pallas_call | solution.py:58
  15.1 0.8 %collective-permute-done.1.c2 = bf16[64,896]{1,0:T(8,128)(2,1)S(1)} collective-permute-done((bf16[64,896]{1,0:T(8,128)(2,1)S(1)}, bf16[64,896]{1,0:T(8,128)(2,1)S(1)}, u32[]{:S(2)}, u32[]{:S(2)}) %collective-permute-start.1) | collective-permute-done | bytes 114720 | tf_op jit(solution)/shard_map/ppermute | solution.py:271
  16.2 1.3 %collective-permute-done.7.far = f32[136,256]{1,0:T(8,128)S(1)} collective-permute-done((f32[136,256]{1,0:T(8,128)S(1)}, f32[136,256]{1,0:T(8,128)S(1)}, u32[]{:S(2)}, u32[]{:S(2)}) %collective-permute-start.7) | collective-permute-done | bytes 139296 | tf_op jit(solution)/shard_map/ppermute | solution.py:271
  17.9 3.1 %collective-permute-start.10 = (f32[64,128]{1,0:T(8,128)S(1)}, f32[64,128]{1,0:T(8,128)S(1)}, u32[]{:S(2)}, u32[]{:S(2)}) collective-permute-start(f32[64,128]{1,0:T(8,128)S(1)} %grads.1), channel_id=1, source_target_pairs={{0,6},{1,7},{2,4},{3,5},{4,2},{5,3},{6,0},{7,1},{8,14},{9,15},{10,... | collective-permute-start | bytes 98312 | tf_op jit(solution)/shard_map/ppermute | solution.py:271
  21.0 0.4 %collective-permute-start.9 = (f32[64,128]{1,0:T(8,128)S(1)}, f32[64,128]{1,0:T(8,128)S(1)}, u32[]{:S(2)}, u32[]{:S(2)}) collective-permute-start(f32[64,128]{1,0:T(8,128)S(1)} %grads.1), channel_id=1, source_target_pairs={{0,5},{1,4},{2,7},{3,6},{4,1},{5,0},{6,3},{7,2},{8,13},{9,12},{10,... | collective-permute-start | bytes 98312 | tf_op jit(solution)/shard_map/ppermute | solution.py:271
  21.7 1.2 %collective-permute-done.10 = f32[64,128]{1,0:T(8,128)S(1)} collective-permute-done((f32[64,128]{1,0:T(8,128)S(1)}, f32[64,128]{1,0:T(8,128)S(1)}, u32[]{:S(2)}, u32[]{:S(2)}) %collective-permute-start.10) | collective-permute-done | bytes 32800 | tf_op jit(solution)/shard_map/ppermute | solution.py:271
  22.9 1.5 %collective-permute-done.8 = f32[64,128]{1,0:T(8,128)S(1)} collective-permute-done((f32[64,128]{1,0:T(8,128)S(1)}, f32[64,128]{1,0:T(8,128)S(1)}, u32[]{:S(2)}, u32[]{:S(2)}) %collective-permute-start.8) | collective-permute-done | bytes 32800 | tf_op jit(solution)/shard_map/ppermute | solution.py:271
  24.5 3.4 %collective-permute-start.11 = (f32[64,128]{1,0:T(8,128)S(1)}, f32[64,128]{1,0:T(8,128)S(1)}, u32[]{:S(2)}, u32[]{:S(2)}) collective-permute-start(f32[64,128]{1,0:T(8,128)S(1)} %add_add_fusion.m0), channel_id=1, source_target_pairs={{0,25},{1,24},{2,27},{3,26},{4,29},{5,28},{6,31},{7,30},{8,17},{9,... | collective-permute-start | bytes 98312 | tf_op jit(solution)/shard_map/ppermute | solution.py:271
  27.9 0.8 %collective-permute-start.13 = (f32[64,128]{1,0:T(8,128)S(1)}, f32[64,128]{1,0:T(8,128)S(1)}, u32[]{:S(2)}, u32[]{:S(2)}) collective-permute-start(f32[64,128]{1,0:T(8,128)S(1)} %add_add_fusion.m0), channel_id=1, source_target_pairs={{0,8},{1,9},{2,10},{3,11},{4,12},{5,13},{6,14},{7,15},{8,0},{9,1},... | collective-permute-start | bytes 98312 | tf_op jit(solution)/shard_map/ppermute | solution.py:271
  28.7 1.0 %collective-permute-done.11.m3 = f32[64,128]{1,0:T(8,128)S(1)} collective-permute-done((f32[64,128]{1,0:T(8,128)S(1)}, f32[64,128]{1,0:T(8,128)S(1)}, u32[]{:S(2)}, u32[]{:S(2)}) %collective-permute-start.11) | collective-permute-done | bytes 32800 | tf_op jit(solution)/shard_map/ppermute | solution.py:271
  29.7 2.5 %collective-permute-done.12.m2 = f32[64,128]{1,0:T(8,128)S(1)} collective-permute-done((f32[64,128]{1,0:T(8,128)S(1)}, f32[64,128]{1,0:T(8,128)S(1)}, u32[]{:S(2)}, u32[]{:S(2)}) %collective-permute-start.12) | collective-permute-done | bytes 32800 | tf_op jit(solution)/shard_map/ppermute | solution.py:271
  32.2 0.4 %products.1.mine = f32[16,128]{1,0:T(8,128)S(1)} custom-call(f32[64,128]{1,0:T(8,128)S(1)} %add_add_fusion.m0, f32[64,128]{1,0:T(8,128)S(1)} %collective-permute-done.11.m3, f32[64,128]{1,0:T(8,128)S(1)} %collective-permute-done.12.m2, f32[64,128]{1,0:T(8,128)S(1)} %collective-permute-done.13.m1, bf16[32,2048]{1,0:T(8,128)(2,1)S(1)} %get-tuple-element.25.t_own, ...), custom_call_target="tpu_custom_call" | custom-call | tf_op jit(solution)/shard_map/products/pallas_call | solution.py:58
  32.6 0.4 %collective-permute-start.15 = (f32[16,128]{1,0:T(8,128)S(1)}, f32[16,128]{1,0:T(8,128)S(1)}, u32[]{:S(2)}, u32[]{:S(2)}) collective-permute-start(f32[16,128]{1,0:T(8,128)S(1)} %products.1.mine), channel_id=1, source_target_pairs={{0,1},{1,0},{2,3},{3,2},{4,5},{5,4},{6,7},{7,6},{8,9},{9,8},{10,11... | collective-permute-start | bytes 24584 | tf_op jit(solution)/shard_map/ppermute | solution.py:271
  32.9 0.8 %collective-permute-done.15.far = f32[16,128]{1,0:T(8,128)S(1)} collective-permute-done((f32[16,128]{1,0:T(8,128)S(1)}, f32[16,128]{1,0:T(8,128)S(1)}, u32[]{:S(2)}, u32[]{:S(2)}) %collective-permute-start.15) | collective-permute-done | bytes 8224 | tf_op jit(solution)/shard_map/ppermute | solution.py:271
  33.8 0.9 %solve.1 = f32[16,32]{1,0:T(8,128)} custom-call(f32[16,128]{1,0:T(8,128)S(1)} %products.1.mine, f32[16,128]{1,0:T(8,128)S(1)} %collective-permute-done.15.far, s32[16,128]{1,0:T(8,128)S(1)} %get-tuple-element.19._.rows), custom_call_target="tpu_custom_call" | custom-call | tf_op jit(solution)/shard_map/solve/pallas_call | solution.py:326
  (18 shorter events, 1.3 us)
Async XLA Ops:
  0.0 13.5 %collective-permute-start.5 = (bf16[128,14336]{1,0:T(8,128)(2,1)}, bf16[128,14336]{1,0:T(8,128)(2,1)S(1)}, u32[]{:S(2)}, u32[]{:S(2)}) collective-permute-start(bf16[128,14336]{1,0:T(8,128)(2,1)} %bitcast.4), channel_id=1, source_target_pairs={{0,1},{1,0},{2,3},{3,2},{4,5},{5,4},{6,7},{7,6},{8,9},{9,8},{10,11... | collective-permute-start | bytes 11010056 | tf_op jit(solution)/shard_map/ppermute | solution.py:271
  0.5 13.1 %collective-permute-start.6 = (bf16[128,4096]{1,0:T(8,128)(2,1)}, bf16[128,4096]{1,0:T(8,128)(2,1)S(1)}, u32[]{:S(2)}, u32[]{:S(2)}) collective-permute-start(bf16[128,4096]{1,0:T(8,128)(2,1)} %bitcast.6), channel_id=1, source_target_pairs={{0,1},{1,0},{2,3},{3,2},{4,5},{5,4},{6,7},{7,6},{8,9},{9,8},{10,11... | collective-permute-start | bytes 3145736 | tf_op jit(solution)/shard_map/ppermute | solution.py:271
  1.5 7.5 %collective-permute-start.2 = (bf16[64,1408]{1,0:T(8,128)(2,1)S(1)}, bf16[64,1408]{1,0:T(8,128)(2,1)S(1)}, u32[]{:S(2)}, u32[]{:S(2)}) collective-permute-start(bf16[64,1408]{1,0:T(8,128)(2,1)S(1)} %get-tuple-element.17), channel_id=1, source_target_pairs={{0,3},{1,4},{2,1},{3,6},{4,7},{5,0},{6,5},{7,2},{8,11},{9,12},{10,... | collective-permute-start | bytes 540680 | tf_op jit(solution)/shard_map/ppermute | solution.py:271
  4.1 9.4 %collective-permute-start.4 = (bf16[64,2304]{1,0:T(8,128)(2,1)S(1)}, bf16[64,2304]{1,0:T(8,128)(2,1)S(1)}, u32[]{:S(2)}, u32[]{:S(2)}) collective-permute-start(bf16[64,2304]{1,0:T(8,128)(2,1)S(1)} %get-tuple-element.18._.own), channel_id=1, source_target_pairs={{0,5},{1,2},{2,7},{3,0},{4,1},{5,6},{6,3},{7,4},{8,13},{9,10},{10,... | collective-permute-start | bytes 884744 | tf_op jit(solution)/shard_map/ppermute | solution.py:271
  4.2 7.2 %collective-permute-start = (bf16[64,896]{1,0:T(8,128)(2,1)S(1)}, bf16[64,896]{1,0:T(8,128)(2,1)S(1)}, u32[]{:S(2)}, u32[]{:S(2)}) collective-permute-start(bf16[64,896]{1,0:T(8,128)(2,1)S(1)} %get-tuple-element.16), channel_id=1, source_target_pairs={{0,3},{1,4},{2,1},{3,6},{4,7},{5,0},{6,5},{7,2},{8,11},{9,12},{10,... | collective-permute-start | bytes 344072 | tf_op jit(solution)/shard_map/ppermute | solution.py:271
  9.1 5.6 %collective-permute-start.3 = (bf16[64,1408]{1,0:T(8,128)(2,1)S(1)}, bf16[64,1408]{1,0:T(8,128)(2,1)S(1)}, u32[]{:S(2)}, u32[]{:S(2)}) collective-permute-start(bf16[64,1408]{1,0:T(8,128)(2,1)S(1)} %after.1.a1), channel_id=1, source_target_pairs={{0,3},{1,4},{2,1},{3,6},{4,7},{5,0},{6,5},{7,2},{8,11},{9,12},{10,... | collective-permute-start | bytes 540680 | tf_op jit(solution)/shard_map/ppermute | solution.py:271
  11.4 4.4 %collective-permute-start.1 = (bf16[64,896]{1,0:T(8,128)(2,1)S(1)}, bf16[64,896]{1,0:T(8,128)(2,1)S(1)}, u32[]{:S(2)}, u32[]{:S(2)}) collective-permute-start(bf16[64,896]{1,0:T(8,128)(2,1)S(1)} %collective-permute-done.a2), channel_id=1, source_target_pairs={{0,3},{1,4},{2,1},{3,6},{4,7},{5,0},{6,5},{7,2},{8,11},{9,12},{10,... | collective-permute-start | bytes 344072 | tf_op jit(solution)/shard_map/ppermute | solution.py:271
  16.2 1.4 %collective-permute-start.7 = (f32[136,256]{1,0:T(8,128)S(1)}, f32[136,256]{1,0:T(8,128)S(1)}, u32[]{:S(2)}, u32[]{:S(2)}) collective-permute-start(f32[136,256]{1,0:T(8,128)S(1)} %last.1.mine), channel_id=1, source_target_pairs={{0,1},{1,0},{2,3},{3,2},{4,5},{5,4},{6,7},{7,6},{8,9},{9,8},{10,11... | collective-permute-start | bytes 417800 | tf_op jit(solution)/shard_map/ppermute | solution.py:271
  17.9 5.0 %collective-permute-start.10 = (f32[64,128]{1,0:T(8,128)S(1)}, f32[64,128]{1,0:T(8,128)S(1)}, u32[]{:S(2)}, u32[]{:S(2)}) collective-permute-start(f32[64,128]{1,0:T(8,128)S(1)} %grads.1), channel_id=1, source_target_pairs={{0,6},{1,7},{2,4},{3,5},{4,2},{5,3},{6,0},{7,1},{8,14},{9,15},{10,... | collective-permute-start | bytes 98312 | tf_op jit(solution)/shard_map/ppermute | solution.py:271
  21.0 3.4 %collective-permute-start.8 = (f32[64,128]{1,0:T(8,128)S(1)}, f32[64,128]{1,0:T(8,128)S(1)}, u32[]{:S(2)}, u32[]{:S(2)}) collective-permute-start(f32[64,128]{1,0:T(8,128)S(1)} %grads.1), channel_id=1, source_target_pairs={{0,3},{1,2},{2,1},{3,0},{4,7},{5,6},{6,5},{7,4},{8,11},{9,10},{10,... | collective-permute-start | bytes 98312 | tf_op jit(solution)/shard_map/ppermute | solution.py:271
  21.0 3.4 %collective-permute-start.9 = (f32[64,128]{1,0:T(8,128)S(1)}, f32[64,128]{1,0:T(8,128)S(1)}, u32[]{:S(2)}, u32[]{:S(2)}) collective-permute-start(f32[64,128]{1,0:T(8,128)S(1)} %grads.1), channel_id=1, source_target_pairs={{0,5},{1,4},{2,7},{3,6},{4,1},{5,0},{6,3},{7,2},{8,13},{9,12},{10,... | collective-permute-start | bytes 98312 | tf_op jit(solution)/shard_map/ppermute | solution.py:271
  21.4 7.3 %collective-permute-start.14 = (bf16[32,2048]{1,0:T(8,128)(2,1)S(1)}, bf16[32,2048]{1,0:T(8,128)(2,1)S(1)}, u32[]{:S(2)}, u32[]{:S(2)}) collective-permute-start(bf16[32,2048]{1,0:T(8,128)(2,1)S(1)} %get-tuple-element.26), channel_id=1, source_target_pairs={{0,1},{1,0},{2,3},{3,2},{4,5},{5,4},{6,7},{7,6},{8,9},{9,8},{10,11... | collective-permute-start | bytes 393224 | tf_op jit(solution)/shard_map/ppermute | solution.py:271
  24.5 5.2 %collective-permute-start.11 = (f32[64,128]{1,0:T(8,128)S(1)}, f32[64,128]{1,0:T(8,128)S(1)}, u32[]{:S(2)}, u32[]{:S(2)}) collective-permute-start(f32[64,128]{1,0:T(8,128)S(1)} %add_add_fusion.m0), channel_id=1, source_target_pairs={{0,25},{1,24},{2,27},{3,26},{4,29},{5,28},{6,31},{7,30},{8,17},{9,... | collective-permute-start | bytes 98312 | tf_op jit(solution)/shard_map/ppermute | solution.py:271
  27.9 4.3 %collective-permute-start.12 = (f32[64,128]{1,0:T(8,128)S(1)}, f32[64,128]{1,0:T(8,128)S(1)}, u32[]{:S(2)}, u32[]{:S(2)}) collective-permute-start(f32[64,128]{1,0:T(8,128)S(1)} %add_add_fusion.m0), channel_id=1, source_target_pairs={{0,17},{1,16},{2,19},{3,18},{4,21},{5,20},{6,23},{7,22},{8,25},{9,... | collective-permute-start | bytes 98312 | tf_op jit(solution)/shard_map/ppermute | solution.py:271
  27.9 4.3 %collective-permute-start.13 = (f32[64,128]{1,0:T(8,128)S(1)}, f32[64,128]{1,0:T(8,128)S(1)}, u32[]{:S(2)}, u32[]{:S(2)}) collective-permute-start(f32[64,128]{1,0:T(8,128)S(1)} %add_add_fusion.m0), channel_id=1, source_target_pairs={{0,8},{1,9},{2,10},{3,11},{4,12},{5,13},{6,14},{7,15},{8,0},{9,1},... | collective-permute-start | bytes 98312 | tf_op jit(solution)/shard_map/ppermute | solution.py:271
  32.6 1.2 %collective-permute-start.15 = (f32[16,128]{1,0:T(8,128)S(1)}, f32[16,128]{1,0:T(8,128)S(1)}, u32[]{:S(2)}, u32[]{:S(2)}) collective-permute-start(f32[16,128]{1,0:T(8,128)S(1)} %products.1.mine), channel_id=1, source_target_pairs={{0,1},{1,0},{2,3},{3,2},{4,5},{5,4},{6,7},{7,6},{8,9},{9,8},{10,11... | collective-permute-start | bytes 24584 | tf_op jit(solution)/shard_map/ppermute | solution.py:271

commit v6 on v5

--- a/solution.py
+++ b/solution.py
@@ -198,7 +198,9 @@
     for q in range(2):
         some = jnp.concatenate([pgs[u, pl.ds(q, pairs, stride=2), :] for u in range(2)], axis=1)
         weighted = jnp.concatenate([some * tokens[j:j + 1, :] for j in range(docs)], axis=0)
-        parts.append(nt(weighted, px, HIGH))
+        high, low = halves(weighted)
+        px_high, px_low = halves(px)
+        parts.append(nt(high, px_high) + (nt(high, px_low) + nt(low, px_high)))
     grads[...] = jnp.concatenate(parts, axis=1)
 
 

time: 34.9 us -> 34.8 us (level)
  no operation moved by 1% of the time
where the time goes in v6:
time: 34.8 us; the launch traced here: 34.7 us
  starting transfers between devices  17.7 us (51%)
  waiting for transfers between devices  10.7 us (31%)
  Pallas kernels  6.23 us (18%)
    ppermute x16, starting transfers between devices, move(): return lax.ppermute(x, ('dp', 'seq'), pairs)  17.7 us
    ppermute x16, waiting for transfers between devices, move(): return lax.ppermute(x, ('dp', 'seq'), pairs)  10.7 us
    pallas_call x8, Pallas kernels, vmem_call(): pl.pallas_call(body, out_shape=[VMEM(s, d) for s, d in outs], in_specs=sp...  5.28 us
    pallas_call x1, Pallas kernels, paired_chips(): pl.pallas_call(solve_body, out_shape=jax.ShapeDtypeStruct((ndocs, ntest),...  0.95 us
  transfers between devices with their start and end apart: 16, of which 9 were waited for; matrix products, arithmetic and copies ran while one was open for 0% of the time, Pallas kernels for 13%

profile of v6, /device:TPU:0, one launch (start us, length us, event | category | flops | bytes accessed | tf_op | source)
XLA Modules:
  0.0 34.7 jit_solution(6346625321707447084)
XLA Ops:
  0.0 0.5 %collective-permute-start.5 = (bf16[128,14336]{1,0:T(8,128)(2,1)}, bf16[128,14336]{1,0:T(8,128)(2,1)S(1)}, u32[]{:S(2)}, u32[]{:S(2)}) collective-permute-start(bf16[128,14336]{1,0:T(8,128)(2,1)} %bitcast.4), channel_id=1, source_target_pairs={{0,1},{1,0},{2,3},{3,2},{4,5},{5,4},{6,7},{7,6},{8,9},{9,8},{10,11... | collective-permute-start | bytes 11010056 | tf_op jit(solution)/shard_map/ppermute | solution.py:273
  0.5 1.0 %weights.1 = (bf16[64,1408]{1,0:T(8,128)(2,1)S(1)}, bf16[64,896]{1,0:T(8,128)(2,1)S(1)}, bf16[64,2304]{1,0:T(8,128)(2,1)S(1)}, f32[8,128]{1,0:T(8,128)S(1)}) custom-call(s32[1,128]{1,0:T(1,128)} %valid.1, s32[1,4]{1,0:T(1,128)} %blocks.1, bf16[64,1792]{1,0:T(8,128)(2,1)} %bitcast.8, bf16[64,512]{1,0:T(8,128)(2,1)} %bitcast.9), custom_call_target="tpu_custom_call" | custom-call | tf_op jit(solution)/shard_map/weights/pallas_call | solution.py:58
  1.5 2.6 %collective-permute-start.2 = (bf16[64,1408]{1,0:T(8,128)(2,1)S(1)}, bf16[64,1408]{1,0:T(8,128)(2,1)S(1)}, u32[]{:S(2)}, u32[]{:S(2)}) collective-permute-start(bf16[64,1408]{1,0:T(8,128)(2,1)S(1)} %get-tuple-element.17), channel_id=1, source_target_pairs={{0,3},{1,4},{2,1},{3,6},{4,7},{5,0},{6,5},{7,2},{8,11},{9,12},{10,... | collective-permute-start | bytes 540680 | tf_op jit(solution)/shard_map/ppermute | solution.py:273
  4.2 1.7 %collective-permute-start = (bf16[64,896]{1,0:T(8,128)(2,1)S(1)}, bf16[64,896]{1,0:T(8,128)(2,1)S(1)}, u32[]{:S(2)}, u32[]{:S(2)}) collective-permute-start(bf16[64,896]{1,0:T(8,128)(2,1)S(1)} %get-tuple-element.16), channel_id=1, source_target_pairs={{0,3},{1,4},{2,1},{3,6},{4,7},{5,0},{6,5},{7,2},{8,11},{9,12},{10,... | collective-permute-start | bytes 344072 | tf_op jit(solution)/shard_map/ppermute | solution.py:273
  5.9 1.8 %keep.1 = (bf16[128,6912]{1,0:T(8,128)(2,1)S(1)}, bf16[128,2304]{1,0:T(8,128)(2,1)S(1)}, bf16[32,2048]{1,0:T(8,128)(2,1)S(1)}, bf16[32,2048]{1,0:T(8,128)(2,1)S(1)}, s32[16,128]{1,0:T(8,128)S(1)}) custom-call(bf16[64,2304]{1,0:T(8,128)(2,1)S(1)} %get-tuple-element.18._.own, bf16[128,14336]{1,0:T(8,128)(2,1)} %bitcast.5, bf16[128,4096]{1,0:T(8,128)(2,1)} %bitcast.7, ...), custom_call_target="tpu_custom_call" | custom-call | tf_op jit(solution)/shard_map/keep/pallas_call | solution.py:58
  7.7 1.4 %collective-permute-done.2.x = bf16[64,1408]{1,0:T(8,128)(2,1)S(1)} collective-permute-done((bf16[64,1408]{1,0:T(8,128)(2,1)S(1)}, bf16[64,1408]{1,0:T(8,128)(2,1)S(1)}, u32[]{:S(2)}, u32[]{:S(2)}) %collective-permute-start.2) | collective-permute-done | bytes 180256 | tf_op jit(solution)/shard_map/ppermute | solution.py:273
  9.1 2.3 %collective-permute-start.3 = (bf16[64,1408]{1,0:T(8,128)(2,1)S(1)}, bf16[64,1408]{1,0:T(8,128)(2,1)S(1)}, u32[]{:S(2)}, u32[]{:S(2)}) collective-permute-start(bf16[64,1408]{1,0:T(8,128)(2,1)S(1)} %after.1.a1), channel_id=1, source_target_pairs={{0,3},{1,4},{2,1},{3,6},{4,7},{5,0},{6,5},{7,2},{8,11},{9,12},{10,... | collective-permute-start | bytes 540680 | tf_op jit(solution)/shard_map/ppermute | solution.py:273
  11.4 2.1 %collective-permute-start.1 = (bf16[64,896]{1,0:T(8,128)(2,1)S(1)}, bf16[64,896]{1,0:T(8,128)(2,1)S(1)}, u32[]{:S(2)}, u32[]{:S(2)}) collective-permute-start(bf16[64,896]{1,0:T(8,128)(2,1)S(1)} %collective-permute-done.a2), channel_id=1, source_target_pairs={{0,3},{1,4},{2,1},{3,6},{4,7},{5,0},{6,5},{7,2},{8,11},{9,12},{10,... | collective-permute-start | bytes 344072 | tf_op jit(solution)/shard_map/ppermute | solution.py:273
  13.5 1.2 %near.1 = (f32[64,256]{1,0:T(8,128)S(1)}, f32[64,256]{1,0:T(8,128)S(1)}) custom-call(bf16[64,2304]{1,0:T(8,128)(2,1)S(1)} %get-tuple-element.18._.own, bf16[64,1408]{1,0:T(8,128)(2,1)S(1)} %after.1.a1, bf16[64,896]{1,0:T(8,128)(2,1)S(1)} %collective-permute-done.a2, bf16[64,2304]{1,0:T(8,128)(2,1)S(1)} %collective-permute-done.4.b, ...), custom_call_target="tpu_custom_call" | custom-call | tf_op jit(solution)/shard_map/near/pallas_call | solution.py:58
  14.7 0.4 %diagonal.1.pg_in = f32[64,256]{1,0:T(8,128)S(1)} custom-call(bf16[64,1408]{1,0:T(8,128)(2,1)S(1)} %collective-permute-done.3.c1, f32[64,256]{1,0:T(8,128)S(1)} %get-tuple-element.21.pg_in, bf16[128,2304]{1,0:T(8,128)(2,1)S(1)} %get-tuple-element.22.near, bf16[128,14336]{1,0:T(8,128)(2,1)S(1)} %collective-permute-done.5.og2), custom_call_target="tpu_custom_call" | custom-call | tf_op jit(solution)/shard_map/diagonal/pallas_call | solution.py:58
  15.1 0.8 %collective-permute-done.1.c2 = bf16[64,896]{1,0:T(8,128)(2,1)S(1)} collective-permute-done((bf16[64,896]{1,0:T(8,128)(2,1)S(1)}, bf16[64,896]{1,0:T(8,128)(2,1)S(1)}, u32[]{:S(2)}, u32[]{:S(2)}) %collective-permute-start.1) | collective-permute-done | bytes 114720 | tf_op jit(solution)/shard_map/ppermute | solution.py:273
  16.2 1.3 %collective-permute-done.7.far = f32[136,256]{1,0:T(8,128)S(1)} collective-permute-done((f32[136,256]{1,0:T(8,128)S(1)}, f32[136,256]{1,0:T(8,128)S(1)}, u32[]{:S(2)}, u32[]{:S(2)}) %collective-permute-start.7) | collective-permute-done | bytes 139296 | tf_op jit(solution)/shard_map/ppermute | solution.py:273
  17.9 3.1 %collective-permute-start.10 = (f32[64,128]{1,0:T(8,128)S(1)}, f32[64,128]{1,0:T(8,128)S(1)}, u32[]{:S(2)}, u32[]{:S(2)}) collective-permute-start(f32[64,128]{1,0:T(8,128)S(1)} %grads.1), channel_id=1, source_target_pairs={{0,6},{1,7},{2,4},{3,5},{4,2},{5,3},{6,0},{7,1},{8,14},{9,15},{10,... | collective-permute-start | bytes 98312 | tf_op jit(solution)/shard_map/ppermute | solution.py:273
  21.0 0.4 %collective-permute-start.9 = (f32[64,128]{1,0:T(8,128)S(1)}, f32[64,128]{1,0:T(8,128)S(1)}, u32[]{:S(2)}, u32[]{:S(2)}) collective-permute-start(f32[64,128]{1,0:T(8,128)S(1)} %grads.1), channel_id=1, source_target_pairs={{0,5},{1,4},{2,7},{3,6},{4,1},{5,0},{6,3},{7,2},{8,13},{9,12},{10,... | collective-permute-start | bytes 98312 | tf_op jit(solution)/shard_map/ppermute | solution.py:273
  21.7 1.2 %collective-permute-done.10 = f32[64,128]{1,0:T(8,128)S(1)} collective-permute-done((f32[64,128]{1,0:T(8,128)S(1)}, f32[64,128]{1,0:T(8,128)S(1)}, u32[]{:S(2)}, u32[]{:S(2)}) %collective-permute-start.10) | collective-permute-done | bytes 32800 | tf_op jit(solution)/shard_map/ppermute | solution.py:273
  22.9 1.5 %collective-permute-done.8 = f32[64,128]{1,0:T(8,128)S(1)} collective-permute-done((f32[64,128]{1,0:T(8,128)S(1)}, f32[64,128]{1,0:T(8,128)S(1)}, u32[]{:S(2)}, u32[]{:S(2)}) %collective-permute-start.8) | collective-permute-done | bytes 32800 | tf_op jit(solution)/shard_map/ppermute | solution.py:273
  24.4 3.4 %collective-permute-start.11 = (f32[64,128]{1,0:T(8,128)S(1)}, f32[64,128]{1,0:T(8,128)S(1)}, u32[]{:S(2)}, u32[]{:S(2)}) collective-permute-start(f32[64,128]{1,0:T(8,128)S(1)} %add_add_fusion.m0), channel_id=1, source_target_pairs={{0,25},{1,24},{2,27},{3,26},{4,29},{5,28},{6,31},{7,30},{8,17},{9,... | collective-permute-start | bytes 98312 | tf_op jit(solution)/shard_map/ppermute | solution.py:273
  27.8 0.8 %collective-permute-start.13 = (f32[64,128]{1,0:T(8,128)S(1)}, f32[64,128]{1,0:T(8,128)S(1)}, u32[]{:S(2)}, u32[]{:S(2)}) collective-permute-start(f32[64,128]{1,0:T(8,128)S(1)} %add_add_fusion.m0), channel_id=1, source_target_pairs={{0,8},{1,9},{2,10},{3,11},{4,12},{5,13},{6,14},{7,15},{8,0},{9,1},... | collective-permute-start | bytes 98312 | tf_op jit(solution)/shard_map/ppermute | solution.py:273
  28.6 1.0 %collective-permute-done.11.m3 = f32[64,128]{1,0:T(8,128)S(1)} collective-permute-done((f32[64,128]{1,0:T(8,128)S(1)}, f32[64,128]{1,0:T(8,128)S(1)}, u32[]{:S(2)}, u32[]{:S(2)}) %collective-permute-start.11) | collective-permute-done | bytes 32800 | tf_op jit(solution)/shard_map/ppermute | solution.py:273
  29.7 2.5 %collective-permute-done.12.m2 = f32[64,128]{1,0:T(8,128)S(1)} collective-permute-done((f32[64,128]{1,0:T(8,128)S(1)}, f32[64,128]{1,0:T(8,128)S(1)}, u32[]{:S(2)}, u32[]{:S(2)}) %collective-permute-start.12) | collective-permute-done | bytes 32800 | tf_op jit(solution)/shard_map/ppermute | solution.py:273
  32.1 0.4 %products.1.mine = f32[16,128]{1,0:T(8,128)S(1)} custom-call(f32[64,128]{1,0:T(8,128)S(1)} %add_add_fusion.m0, f32[64,128]{1,0:T(8,128)S(1)} %collective-permute-done.11.m3, f32[64,128]{1,0:T(8,128)S(1)} %collective-permute-done.12.m2, f32[64,128]{1,0:T(8,128)S(1)} %collective-permute-done.13.m1, bf16[32,2048]{1,0:T(8,128)(2,1)S(1)} %get-tuple-element.25.t_own, ...), custom_call_target="tpu_custom_call" | custom-call | tf_op jit(solution)/shard_map/products/pallas_call | solution.py:58
  32.5 0.4 %collective-permute-start.15 = (f32[16,128]{1,0:T(8,128)S(1)}, f32[16,128]{1,0:T(8,128)S(1)}, u32[]{:S(2)}, u32[]{:S(2)}) collective-permute-start(f32[16,128]{1,0:T(8,128)S(1)} %products.1.mine), channel_id=1, source_target_pairs={{0,1},{1,0},{2,3},{3,2},{4,5},{5,4},{6,7},{7,6},{8,9},{9,8},{10,11... | collective-permute-start | bytes 24584 | tf_op jit(solution)/shard_map/ppermute | solution.py:273
  32.9 0.9 %collective-permute-done.15.far = f32[16,128]{1,0:T(8,128)S(1)} collective-permute-done((f32[16,128]{1,0:T(8,128)S(1)}, f32[16,128]{1,0:T(8,128)S(1)}, u32[]{:S(2)}, u32[]{:S(2)}) %collective-permute-start.15) | collective-permute-done | bytes 8224 | tf_op jit(solution)/shard_map/ppermute | solution.py:273
  33.7 0.9 %solve.1 = f32[16,32]{1,0:T(8,128)} custom-call(f32[16,128]{1,0:T(8,128)S(1)} %products.1.mine, f32[16,128]{1,0:T(8,128)S(1)} %collective-permute-done.15.far, s32[16,128]{1,0:T(8,128)S(1)} %get-tuple-element.19._.rows), custom_call_target="tpu_custom_call" | custom-call | tf_op jit(solution)/shard_map/solve/pallas_call | solution.py:328
  (18 shorter events, 1.2 us)
Async XLA Ops:
  0.0 13.5 %collective-permute-start.5 = (bf16[128,14336]{1,0:T(8,128)(2,1)}, bf16[128,14336]{1,0:T(8,128)(2,1)S(1)}, u32[]{:S(2)}, u32[]{:S(2)}) collective-permute-start(bf16[128,14336]{1,0:T(8,128)(2,1)} %bitcast.4), channel_id=1, source_target_pairs={{0,1},{1,0},{2,3},{3,2},{4,5},{5,4},{6,7},{7,6},{8,9},{9,8},{10,11... | collective-permute-start | bytes 11010056 | tf_op jit(solution)/shard_map/ppermute | solution.py:273
  0.5 13.1 %collective-permute-start.6 = (bf16[128,4096]{1,0:T(8,128)(2,1)}, bf16[128,4096]{1,0:T(8,128)(2,1)S(1)}, u32[]{:S(2)}, u32[]{:S(2)}) collective-permute-start(bf16[128,4096]{1,0:T(8,128)(2,1)} %bitcast.6), channel_id=1, source_target_pairs={{0,1},{1,0},{2,3},{3,2},{4,5},{5,4},{6,7},{7,6},{8,9},{9,8},{10,11... | collective-permute-start | bytes 3145736 | tf_op jit(solution)/shard_map/ppermute | solution.py:273
  1.5 7.5 %collective-permute-start.2 = (bf16[64,1408]{1,0:T(8,128)(2,1)S(1)}, bf16[64,1408]{1,0:T(8,128)(2,1)S(1)}, u32[]{:S(2)}, u32[]{:S(2)}) collective-permute-start(bf16[64,1408]{1,0:T(8,128)(2,1)S(1)} %get-tuple-element.17), channel_id=1, source_target_pairs={{0,3},{1,4},{2,1},{3,6},{4,7},{5,0},{6,5},{7,2},{8,11},{9,12},{10,... | collective-permute-start | bytes 540680 | tf_op jit(solution)/shard_map/ppermute | solution.py:273
  4.1 9.4 %collective-permute-start.4 = (bf16[64,2304]{1,0:T(8,128)(2,1)S(1)}, bf16[64,2304]{1,0:T(8,128)(2,1)S(1)}, u32[]{:S(2)}, u32[]{:S(2)}) collective-permute-start(bf16[64,2304]{1,0:T(8,128)(2,1)S(1)} %get-tuple-element.18._.own), channel_id=1, source_target_pairs={{0,5},{1,2},{2,7},{3,0},{4,1},{5,6},{6,3},{7,4},{8,13},{9,10},{10,... | collective-permute-start | bytes 884744 | tf_op jit(solution)/shard_map/ppermute | solution.py:273
  4.2 7.2 %collective-permute-start = (bf16[64,896]{1,0:T(8,128)(2,1)S(1)}, bf16[64,896]{1,0:T(8,128)(2,1)S(1)}, u32[]{:S(2)}, u32[]{:S(2)}) collective-permute-start(bf16[64,896]{1,0:T(8,128)(2,1)S(1)} %get-tuple-element.16), channel_id=1, source_target_pairs={{0,3},{1,4},{2,1},{3,6},{4,7},{5,0},{6,5},{7,2},{8,11},{9,12},{10,... | collective-permute-start | bytes 344072 | tf_op jit(solution)/shard_map/ppermute | solution.py:273
  9.1 5.6 %collective-permute-start.3 = (bf16[64,1408]{1,0:T(8,128)(2,1)S(1)}, bf16[64,1408]{1,0:T(8,128)(2,1)S(1)}, u32[]{:S(2)}, u32[]{:S(2)}) collective-permute-start(bf16[64,1408]{1,0:T(8,128)(2,1)S(1)} %after.1.a1), channel_id=1, source_target_pairs={{0,3},{1,4},{2,1},{3,6},{4,7},{5,0},{6,5},{7,2},{8,11},{9,12},{10,... | collective-permute-start | bytes 540680 | tf_op jit(solution)/shard_map/ppermute | solution.py:273
  11.4 4.4 %collective-permute-start.1 = (bf16[64,896]{1,0:T(8,128)(2,1)S(1)}, bf16[64,896]{1,0:T(8,128)(2,1)S(1)}, u32[]{:S(2)}, u32[]{:S(2)}) collective-permute-start(bf16[64,896]{1,0:T(8,128)(2,1)S(1)} %collective-permute-done.a2), channel_id=1, source_target_pairs={{0,3},{1,4},{2,1},{3,6},{4,7},{5,0},{6,5},{7,2},{8,11},{9,12},{10,... | collective-permute-start | bytes 344072 | tf_op jit(solution)/shard_map/ppermute | solution.py:273
  16.2 1.4 %collective-permute-start.7 = (f32[136,256]{1,0:T(8,128)S(1)}, f32[136,256]{1,0:T(8,128)S(1)}, u32[]{:S(2)}, u32[]{:S(2)}) collective-permute-start(f32[136,256]{1,0:T(8,128)S(1)} %last.1.mine), channel_id=1, source_target_pairs={{0,1},{1,0},{2,3},{3,2},{4,5},{5,4},{6,7},{7,6},{8,9},{9,8},{10,11... | collective-permute-start | bytes 417800 | tf_op jit(solution)/shard_map/ppermute | solution.py:273
  17.9 5.0 %collective-permute-start.10 = (f32[64,128]{1,0:T(8,128)S(1)}, f32[64,128]{1,0:T(8,128)S(1)}, u32[]{:S(2)}, u32[]{:S(2)}) collective-permute-start(f32[64,128]{1,0:T(8,128)S(1)} %grads.1), channel_id=1, source_target_pairs={{0,6},{1,7},{2,4},{3,5},{4,2},{5,3},{6,0},{7,1},{8,14},{9,15},{10,... | collective-permute-start | bytes 98312 | tf_op jit(solution)/shard_map/ppermute | solution.py:273
  21.0 3.4 %collective-permute-start.8 = (f32[64,128]{1,0:T(8,128)S(1)}, f32[64,128]{1,0:T(8,128)S(1)}, u32[]{:S(2)}, u32[]{:S(2)}) collective-permute-start(f32[64,128]{1,0:T(8,128)S(1)} %grads.1), channel_id=1, source_target_pairs={{0,3},{1,2},{2,1},{3,0},{4,7},{5,6},{6,5},{7,4},{8,11},{9,10},{10,... | collective-permute-start | bytes 98312 | tf_op jit(solution)/shard_map/ppermute | solution.py:273
  21.0 3.4 %collective-permute-start.9 = (f32[64,128]{1,0:T(8,128)S(1)}, f32[64,128]{1,0:T(8,128)S(1)}, u32[]{:S(2)}, u32[]{:S(2)}) collective-permute-start(f32[64,128]{1,0:T(8,128)S(1)} %grads.1), channel_id=1, source_target_pairs={{0,5},{1,4},{2,7},{3,6},{4,1},{5,0},{6,3},{7,2},{8,13},{9,12},{10,... | collective-permute-start | bytes 98312 | tf_op jit(solution)/shard_map/ppermute | solution.py:273
  21.3 7.3 %collective-permute-start.14 = (bf16[32,2048]{1,0:T(8,128)(2,1)S(1)}, bf16[32,2048]{1,0:T(8,128)(2,1)S(1)}, u32[]{:S(2)}, u32[]{:S(2)}) collective-permute-start(bf16[32,2048]{1,0:T(8,128)(2,1)S(1)} %get-tuple-element.26), channel_id=1, source_target_pairs={{0,1},{1,0},{2,3},{3,2},{4,5},{5,4},{6,7},{7,6},{8,9},{9,8},{10,11... | collective-permute-start | bytes 393224 | tf_op jit(solution)/shard_map/ppermute | solution.py:273
  24.4 5.2 %collective-permute-start.11 = (f32[64,128]{1,0:T(8,128)S(1)}, f32[64,128]{1,0:T(8,128)S(1)}, u32[]{:S(2)}, u32[]{:S(2)}) collective-permute-start(f32[64,128]{1,0:T(8,128)S(1)} %add_add_fusion.m0), channel_id=1, source_target_pairs={{0,25},{1,24},{2,27},{3,26},{4,29},{5,28},{6,31},{7,30},{8,17},{9,... | collective-permute-start | bytes 98312 | tf_op jit(solution)/shard_map/ppermute | solution.py:273
  27.8 4.3 %collective-permute-start.12 = (f32[64,128]{1,0:T(8,128)S(1)}, f32[64,128]{1,0:T(8,128)S(1)}, u32[]{:S(2)}, u32[]{:S(2)}) collective-permute-start(f32[64,128]{1,0:T(8,128)S(1)} %add_add_fusion.m0), channel_id=1, source_target_pairs={{0,17},{1,16},{2,19},{3,18},{4,21},{5,20},{6,23},{7,22},{8,25},{9,... | collective-permute-start | bytes 98312 | tf_op jit(solution)/shard_map/ppermute | solution.py:273
  27.8 4.3 %collective-permute-start.13 = (f32[64,128]{1,0:T(8,128)S(1)}, f32[64,128]{1,0:T(8,128)S(1)}, u32[]{:S(2)}, u32[]{:S(2)}) collective-permute-start(f32[64,128]{1,0:T(8,128)S(1)} %add_add_fusion.m0), channel_id=1, source_target_pairs={{0,8},{1,9},{2,10},{3,11},{4,12},{5,13},{6,14},{7,15},{8,0},{9,1},... | collective-permute-start | bytes 98312 | tf_op jit(solution)/shard_map/ppermute | solution.py:273
  32.5 1.2 %collective-permute-start.15 = (f32[16,128]{1,0:T(8,128)S(1)}, f32[16,128]{1,0:T(8,128)S(1)}, u32[]{:S(2)}, u32[]{:S(2)}) collective-permute-start(f32[16,128]{1,0:T(8,128)S(1)} %products.1.mine), channel_id=1, source_target_pairs={{0,1},{1,0},{2,3},{3,2},{4,5},{5,4},{6,7},{7,6},{8,9},{9,8},{10,11... | collective-permute-start | bytes 24584 | tf_op jit(solution)/shard_map/ppermute | solution.py:273

commit v7 on v6

--- a/solution.py
+++ b/solution.py
@@ -83,10 +83,8 @@
     ]
     for c in copies:
         c.start()
-    for c in copies:
+    for c in copies[:2]:
         c.wait()
-    first[...] = whole[:, :size]
-    second[...] = whole[:, size:]
     slots = valid.shape[1]
     blk = (seq * slots + lax.broadcasted_iota(jnp.int32, weights.shape, 1)) // BLOCK
     row = lax.broadcasted_iota(jnp.int32, weights.shape, 0)
@@ -96,6 +94,10 @@
         end = end + blocks_s[0, j]
         owner = owner + (blk >= end).astype(jnp.int32)
     weights[...] = jnp.where((owner == row) & (valid_v[...] == 1), 1.0, 0.0)
+    for c in copies[2:]:
+        c.wait()
+    first[...] = whole[:, :size]
+    second[...] = whole[:, size:]
 
 
 def column_copies(og, inp, three, last, mine, sems):

time: 34.8 us -> 34.8 us (level)
  no operation moved by 1% of the time
where the time goes in v7:
time: 34.8 us; the launch traced here: 34.7 us
  starting transfers between devices  17.6 us (51%)
  waiting for transfers between devices  10.7 us (31%)
  Pallas kernels  6.23 us (18%)
    ppermute x16, starting transfers between devices, move(): return lax.ppermute(x, ('dp', 'seq'), pairs)  17.6 us
    ppermute x16, waiting for transfers between devices, move(): return lax.ppermute(x, ('dp', 'seq'), pairs)  10.7 us
    pallas_call x8, Pallas kernels, vmem_call(): pl.pallas_call(body, out_shape=[VMEM(s, d) for s, d in outs], in_specs=sp...  5.28 us
    pallas_call x1, Pallas kernels, paired_chips(): pl.pallas_call(solve_body, out_shape=jax.ShapeDtypeStruct((ndocs, ntest),...  0.95 us
  transfers between devices with their start and end apart: 16, of which 9 were waited for; matrix products, arithmetic and copies ran while one was open for 0% of the time, Pallas kernels for 13%

profile of v7, /device:TPU:0, one launch (start us, length us, event | category | flops | bytes accessed | tf_op | source)
XLA Modules:
  0.0 34.7 jit_solution(1788715416023739978)
XLA Ops:
  0.0 0.5 %collective-permute-start.5 = (bf16[128,14336]{1,0:T(8,128)(2,1)}, bf16[128,14336]{1,0:T(8,128)(2,1)S(1)}, u32[]{:S(2)}, u32[]{:S(2)}) collective-permute-start(bf16[128,14336]{1,0:T(8,128)(2,1)} %bitcast.4), channel_id=1, source_target_pairs={{0,1},{1,0},{2,3},{3,2},{4,5},{5,4},{6,7},{7,6},{8,9},{9,8},{10,11... | collective-permute-start | bytes 11010056 | tf_op jit(solution)/shard_map/ppermute | solution.py:275
  0.5 1.0 %weights.1 = (bf16[64,1408]{1,0:T(8,128)(2,1)S(1)}, bf16[64,896]{1,0:T(8,128)(2,1)S(1)}, bf16[64,2304]{1,0:T(8,128)(2,1)S(1)}, f32[8,128]{1,0:T(8,128)S(1)}) custom-call(s32[1,128]{1,0:T(1,128)} %valid.1, s32[1,4]{1,0:T(1,128)} %blocks.1, bf16[64,1792]{1,0:T(8,128)(2,1)} %bitcast.8, bf16[64,512]{1,0:T(8,128)(2,1)} %bitcast.9), custom_call_target="tpu_custom_call" | custom-call | tf_op jit(solution)/shard_map/weights/pallas_call | solution.py:58
  1.5 2.6 %collective-permute-start.2 = (bf16[64,1408]{1,0:T(8,128)(2,1)S(1)}, bf16[64,1408]{1,0:T(8,128)(2,1)S(1)}, u32[]{:S(2)}, u32[]{:S(2)}) collective-permute-start(bf16[64,1408]{1,0:T(8,128)(2,1)S(1)} %get-tuple-element.17), channel_id=1, source_target_pairs={{0,3},{1,4},{2,1},{3,6},{4,7},{5,0},{6,5},{7,2},{8,11},{9,12},{10,... | collective-permute-start | bytes 540680 | tf_op jit(solution)/shard_map/ppermute | solution.py:275
  4.2 1.7 %collective-permute-start = (bf16[64,896]{1,0:T(8,128)(2,1)S(1)}, bf16[64,896]{1,0:T(8,128)(2,1)S(1)}, u32[]{:S(2)}, u32[]{:S(2)}) collective-permute-start(bf16[64,896]{1,0:T(8,128)(2,1)S(1)} %get-tuple-element.16), channel_id=1, source_target_pairs={{0,3},{1,4},{2,1},{3,6},{4,7},{5,0},{6,5},{7,2},{8,11},{9,12},{10,... | collective-permute-start | bytes 344072 | tf_op jit(solution)/shard_map/ppermute | solution.py:275
  5.9 1.8 %keep.1 = (bf16[128,6912]{1,0:T(8,128)(2,1)S(1)}, bf16[128,2304]{1,0:T(8,128)(2,1)S(1)}, bf16[32,2048]{1,0:T(8,128)(2,1)S(1)}, bf16[32,2048]{1,0:T(8,128)(2,1)S(1)}, s32[16,128]{1,0:T(8,128)S(1)}) custom-call(bf16[64,2304]{1,0:T(8,128)(2,1)S(1)} %get-tuple-element.18._.own, bf16[128,14336]{1,0:T(8,128)(2,1)} %bitcast.5, bf16[128,4096]{1,0:T(8,128)(2,1)} %bitcast.7, ...), custom_call_target="tpu_custom_call" | custom-call | tf_op jit(solution)/shard_map/keep/pallas_call | solution.py:58
  7.7 1.4 %collective-permute-done.2.x = bf16[64,1408]{1,0:T(8,128)(2,1)S(1)} collective-permute-done((bf16[64,1408]{1,0:T(8,128)(2,1)S(1)}, bf16[64,1408]{1,0:T(8,128)(2,1)S(1)}, u32[]{:S(2)}, u32[]{:S(2)}) %collective-permute-start.2) | collective-permute-done | bytes 180256 | tf_op jit(solution)/shard_map/ppermute | solution.py:275
  9.1 2.3 %collective-permute-start.3 = (bf16[64,1408]{1,0:T(8,128)(2,1)S(1)}, bf16[64,1408]{1,0:T(8,128)(2,1)S(1)}, u32[]{:S(2)}, u32[]{:S(2)}) collective-permute-start(bf16[64,1408]{1,0:T(8,128)(2,1)S(1)} %after.1.a1), channel_id=1, source_target_pairs={{0,3},{1,4},{2,1},{3,6},{4,7},{5,0},{6,5},{7,2},{8,11},{9,12},{10,... | collective-permute-start | bytes 540680 | tf_op jit(solution)/shard_map/ppermute | solution.py:275
  11.4 2.1 %collective-permute-start.1 = (bf16[64,896]{1,0:T(8,128)(2,1)S(1)}, bf16[64,896]{1,0:T(8,128)(2,1)S(1)}, u32[]{:S(2)}, u32[]{:S(2)}) collective-permute-start(bf16[64,896]{1,0:T(8,128)(2,1)S(1)} %collective-permute-done.a2), channel_id=1, source_target_pairs={{0,3},{1,4},{2,1},{3,6},{4,7},{5,0},{6,5},{7,2},{8,11},{9,12},{10,... | collective-permute-start | bytes 344072 | tf_op jit(solution)/shard_map/ppermute | solution.py:275
  13.5 1.2 %near.1 = (f32[64,256]{1,0:T(8,128)S(1)}, f32[64,256]{1,0:T(8,128)S(1)}) custom-call(bf16[64,2304]{1,0:T(8,128)(2,1)S(1)} %get-tuple-element.18._.own, bf16[64,1408]{1,0:T(8,128)(2,1)S(1)} %after.1.a1, bf16[64,896]{1,0:T(8,128)(2,1)S(1)} %collective-permute-done.a2, bf16[64,2304]{1,0:T(8,128)(2,1)S(1)} %collective-permute-done.4.b, ...), custom_call_target="tpu_custom_call" | custom-call | tf_op jit(solution)/shard_map/near/pallas_call | solution.py:58
  14.7 0.4 %diagonal.1.pg_in = f32[64,256]{1,0:T(8,128)S(1)} custom-call(bf16[64,1408]{1,0:T(8,128)(2,1)S(1)} %collective-permute-done.3.c1, f32[64,256]{1,0:T(8,128)S(1)} %get-tuple-element.21.pg_in, bf16[128,2304]{1,0:T(8,128)(2,1)S(1)} %get-tuple-element.22.near, bf16[128,14336]{1,0:T(8,128)(2,1)S(1)} %collective-permute-done.5.og2), custom_call_target="tpu_custom_call" | custom-call | tf_op jit(solution)/shard_map/diagonal/pallas_call | solution.py:58
  15.1 0.8 %collective-permute-done.1.c2 = bf16[64,896]{1,0:T(8,128)(2,1)S(1)} collective-permute-done((bf16[64,896]{1,0:T(8,128)(2,1)S(1)}, bf16[64,896]{1,0:T(8,128)(2,1)S(1)}, u32[]{:S(2)}, u32[]{:S(2)}) %collective-permute-start.1) | collective-permute-done | bytes 114720 | tf_op jit(solution)/shard_map/ppermute | solution.py:275
  16.2 1.3 %collective-permute-done.7.far = f32[136,256]{1,0:T(8,128)S(1)} collective-permute-done((f32[136,256]{1,0:T(8,128)S(1)}, f32[136,256]{1,0:T(8,128)S(1)}, u32[]{:S(2)}, u32[]{:S(2)}) %collective-permute-start.7) | collective-permute-done | bytes 139296 | tf_op jit(solution)/shard_map/ppermute | solution.py:275
  17.8 3.1 %collective-permute-start.10 = (f32[64,128]{1,0:T(8,128)S(1)}, f32[64,128]{1,0:T(8,128)S(1)}, u32[]{:S(2)}, u32[]{:S(2)}) collective-permute-start(f32[64,128]{1,0:T(8,128)S(1)} %grads.1), channel_id=1, source_target_pairs={{0,6},{1,7},{2,4},{3,5},{4,2},{5,3},{6,0},{7,1},{8,14},{9,15},{10,... | collective-permute-start | bytes 98312 | tf_op jit(solution)/shard_map/ppermute | solution.py:275
  21.0 0.4 %collective-permute-start.9 = (f32[64,128]{1,0:T(8,128)S(1)}, f32[64,128]{1,0:T(8,128)S(1)}, u32[]{:S(2)}, u32[]{:S(2)}) collective-permute-start(f32[64,128]{1,0:T(8,128)S(1)} %grads.1), channel_id=1, source_target_pairs={{0,5},{1,4},{2,7},{3,6},{4,1},{5,0},{6,3},{7,2},{8,13},{9,12},{10,... | collective-permute-start | bytes 98312 | tf_op jit(solution)/shard_map/ppermute | solution.py:275
  21.7 1.2 %collective-permute-done.10 = f32[64,128]{1,0:T(8,128)S(1)} collective-permute-done((f32[64,128]{1,0:T(8,128)S(1)}, f32[64,128]{1,0:T(8,128)S(1)}, u32[]{:S(2)}, u32[]{:S(2)}) %collective-permute-start.10) | collective-permute-done | bytes 32800 | tf_op jit(solution)/shard_map/ppermute | solution.py:275
  22.9 1.5 %collective-permute-done.8 = f32[64,128]{1,0:T(8,128)S(1)} collective-permute-done((f32[64,128]{1,0:T(8,128)S(1)}, f32[64,128]{1,0:T(8,128)S(1)}, u32[]{:S(2)}, u32[]{:S(2)}) %collective-permute-start.8) | collective-permute-done | bytes 32800 | tf_op jit(solution)/shard_map/ppermute | solution.py:275
  24.4 3.4 %collective-permute-start.11 = (f32[64,128]{1,0:T(8,128)S(1)}, f32[64,128]{1,0:T(8,128)S(1)}, u32[]{:S(2)}, u32[]{:S(2)}) collective-permute-start(f32[64,128]{1,0:T(8,128)S(1)} %add_add_fusion.m0), channel_id=1, source_target_pairs={{0,25},{1,24},{2,27},{3,26},{4,29},{5,28},{6,31},{7,30},{8,17},{9,... | collective-permute-start | bytes 98312 | tf_op jit(solution)/shard_map/ppermute | solution.py:275
  27.8 0.8 %collective-permute-start.13 = (f32[64,128]{1,0:T(8,128)S(1)}, f32[64,128]{1,0:T(8,128)S(1)}, u32[]{:S(2)}, u32[]{:S(2)}) collective-permute-start(f32[64,128]{1,0:T(8,128)S(1)} %add_add_fusion.m0), channel_id=1, source_target_pairs={{0,8},{1,9},{2,10},{3,11},{4,12},{5,13},{6,14},{7,15},{8,0},{9,1},... | collective-permute-start | bytes 98312 | tf_op jit(solution)/shard_map/ppermute | solution.py:275
  28.6 1.0 %collective-permute-done.11.m3 = f32[64,128]{1,0:T(8,128)S(1)} collective-permute-done((f32[64,128]{1,0:T(8,128)S(1)}, f32[64,128]{1,0:T(8,128)S(1)}, u32[]{:S(2)}, u32[]{:S(2)}) %collective-permute-start.11) | collective-permute-done | bytes 32800 | tf_op jit(solution)/shard_map/ppermute | solution.py:275
  29.6 2.5 %collective-permute-done.12.m2 = f32[64,128]{1,0:T(8,128)S(1)} collective-permute-done((f32[64,128]{1,0:T(8,128)S(1)}, f32[64,128]{1,0:T(8,128)S(1)}, u32[]{:S(2)}, u32[]{:S(2)}) %collective-permute-start.12) | collective-permute-done | bytes 32800 | tf_op jit(solution)/shard_map/ppermute | solution.py:275
  32.1 0.4 %products.1.mine = f32[16,128]{1,0:T(8,128)S(1)} custom-call(f32[64,128]{1,0:T(8,128)S(1)} %add_add_fusion.m0, f32[64,128]{1,0:T(8,128)S(1)} %collective-permute-done.11.m3, f32[64,128]{1,0:T(8,128)S(1)} %collective-permute-done.12.m2, f32[64,128]{1,0:T(8,128)S(1)} %collective-permute-done.13.m1, bf16[32,2048]{1,0:T(8,128)(2,1)S(1)} %get-tuple-element.25.t_own, ...), custom_call_target="tpu_custom_call" | custom-call | tf_op jit(solution)/shard_map/products/pallas_call | solution.py:58
  32.5 0.4 %collective-permute-start.15 = (f32[16,128]{1,0:T(8,128)S(1)}, f32[16,128]{1,0:T(8,128)S(1)}, u32[]{:S(2)}, u32[]{:S(2)}) collective-permute-start(f32[16,128]{1,0:T(8,128)S(1)} %products.1.mine), channel_id=1, source_target_pairs={{0,1},{1,0},{2,3},{3,2},{4,5},{5,4},{6,7},{7,6},{8,9},{9,8},{10,11... | collective-permute-start | bytes 24584 | tf_op jit(solution)/shard_map/ppermute | solution.py:275
  32.9 0.8 %collective-permute-done.15.far = f32[16,128]{1,0:T(8,128)S(1)} collective-permute-done((f32[16,128]{1,0:T(8,128)S(1)}, f32[16,128]{1,0:T(8,128)S(1)}, u32[]{:S(2)}, u32[]{:S(2)}) %collective-permute-start.15) | collective-permute-done | bytes 8224 | tf_op jit(solution)/shard_map/ppermute | solution.py:275
  33.7 0.9 %solve.1 = f32[16,32]{1,0:T(8,128)} custom-call(f32[16,128]{1,0:T(8,128)S(1)} %products.1.mine, f32[16,128]{1,0:T(8,128)S(1)} %collective-permute-done.15.far, s32[16,128]{1,0:T(8,128)S(1)} %get-tuple-element.19._.rows), custom_call_target="tpu_custom_call" | custom-call | tf_op jit(solution)/shard_map/solve/pallas_call | solution.py:330
  (18 shorter events, 1.2 us)
Async XLA Ops:
  0.0 13.5 %collective-permute-start.5 = (bf16[128,14336]{1,0:T(8,128)(2,1)}, bf16[128,14336]{1,0:T(8,128)(2,1)S(1)}, u32[]{:S(2)}, u32[]{:S(2)}) collective-permute-start(bf16[128,14336]{1,0:T(8,128)(2,1)} %bitcast.4), channel_id=1, source_target_pairs={{0,1},{1,0},{2,3},{3,2},{4,5},{5,4},{6,7},{7,6},{8,9},{9,8},{10,11... | collective-permute-start | bytes 11010056 | tf_op jit(solution)/shard_map/ppermute | solution.py:275
  0.5 13.1 %collective-permute-start.6 = (bf16[128,4096]{1,0:T(8,128)(2,1)}, bf16[128,4096]{1,0:T(8,128)(2,1)S(1)}, u32[]{:S(2)}, u32[]{:S(2)}) collective-permute-start(bf16[128,4096]{1,0:T(8,128)(2,1)} %bitcast.6), channel_id=1, source_target_pairs={{0,1},{1,0},{2,3},{3,2},{4,5},{5,4},{6,7},{7,6},{8,9},{9,8},{10,11... | collective-permute-start | bytes 3145736 | tf_op jit(solution)/shard_map/ppermute | solution.py:275
  1.5 7.5 %collective-permute-start.2 = (bf16[64,1408]{1,0:T(8,128)(2,1)S(1)}, bf16[64,1408]{1,0:T(8,128)(2,1)S(1)}, u32[]{:S(2)}, u32[]{:S(2)}) collective-permute-start(bf16[64,1408]{1,0:T(8,128)(2,1)S(1)} %get-tuple-element.17), channel_id=1, source_target_pairs={{0,3},{1,4},{2,1},{3,6},{4,7},{5,0},{6,5},{7,2},{8,11},{9,12},{10,... | collective-permute-start | bytes 540680 | tf_op jit(solution)/shard_map/ppermute | solution.py:275
  4.1 9.4 %collective-permute-start.4 = (bf16[64,2304]{1,0:T(8,128)(2,1)S(1)}, bf16[64,2304]{1,0:T(8,128)(2,1)S(1)}, u32[]{:S(2)}, u32[]{:S(2)}) collective-permute-start(bf16[64,2304]{1,0:T(8,128)(2,1)S(1)} %get-tuple-element.18._.own), channel_id=1, source_target_pairs={{0,5},{1,2},{2,7},{3,0},{4,1},{5,6},{6,3},{7,4},{8,13},{9,10},{10,... | collective-permute-start | bytes 884744 | tf_op jit(solution)/shard_map/ppermute | solution.py:275
  4.2 7.2 %collective-permute-start = (bf16[64,896]{1,0:T(8,128)(2,1)S(1)}, bf16[64,896]{1,0:T(8,128)(2,1)S(1)}, u32[]{:S(2)}, u32[]{:S(2)}) collective-permute-start(bf16[64,896]{1,0:T(8,128)(2,1)S(1)} %get-tuple-element.16), channel_id=1, source_target_pairs={{0,3},{1,4},{2,1},{3,6},{4,7},{5,0},{6,5},{7,2},{8,11},{9,12},{10,... | collective-permute-start | bytes 344072 | tf_op jit(solution)/shard_map/ppermute | solution.py:275
  9.1 5.6 %collective-permute-start.3 = (bf16[64,1408]{1,0:T(8,128)(2,1)S(1)}, bf16[64,1408]{1,0:T(8,128)(2,1)S(1)}, u32[]{:S(2)}, u32[]{:S(2)}) collective-permute-start(bf16[64,1408]{1,0:T(8,128)(2,1)S(1)} %after.1.a1), channel_id=1, source_target_pairs={{0,3},{1,4},{2,1},{3,6},{4,7},{5,0},{6,5},{7,2},{8,11},{9,12},{10,... | collective-permute-start | bytes 540680 | tf_op jit(solution)/shard_map/ppermute | solution.py:275
  11.4 4.4 %collective-permute-start.1 = (bf16[64,896]{1,0:T(8,128)(2,1)S(1)}, bf16[64,896]{1,0:T(8,128)(2,1)S(1)}, u32[]{:S(2)}, u32[]{:S(2)}) collective-permute-start(bf16[64,896]{1,0:T(8,128)(2,1)S(1)} %collective-permute-done.a2), channel_id=1, source_target_pairs={{0,3},{1,4},{2,1},{3,6},{4,7},{5,0},{6,5},{7,2},{8,11},{9,12},{10,... | collective-permute-start | bytes 344072 | tf_op jit(solution)/shard_map/ppermute | solution.py:275
  16.2 1.4 %collective-permute-start.7 = (f32[136,256]{1,0:T(8,128)S(1)}, f32[136,256]{1,0:T(8,128)S(1)}, u32[]{:S(2)}, u32[]{:S(2)}) collective-permute-start(f32[136,256]{1,0:T(8,128)S(1)} %last.1.mine), channel_id=1, source_target_pairs={{0,1},{1,0},{2,3},{3,2},{4,5},{5,4},{6,7},{7,6},{8,9},{9,8},{10,11... | collective-permute-start | bytes 417800 | tf_op jit(solution)/shard_map/ppermute | solution.py:275
  17.8 5.0 %collective-permute-start.10 = (f32[64,128]{1,0:T(8,128)S(1)}, f32[64,128]{1,0:T(8,128)S(1)}, u32[]{:S(2)}, u32[]{:S(2)}) collective-permute-start(f32[64,128]{1,0:T(8,128)S(1)} %grads.1), channel_id=1, source_target_pairs={{0,6},{1,7},{2,4},{3,5},{4,2},{5,3},{6,0},{7,1},{8,14},{9,15},{10,... | collective-permute-start | bytes 98312 | tf_op jit(solution)/shard_map/ppermute | solution.py:275
  21.0 3.4 %collective-permute-start.8 = (f32[64,128]{1,0:T(8,128)S(1)}, f32[64,128]{1,0:T(8,128)S(1)}, u32[]{:S(2)}, u32[]{:S(2)}) collective-permute-start(f32[64,128]{1,0:T(8,128)S(1)} %grads.1), channel_id=1, source_target_pairs={{0,3},{1,2},{2,1},{3,0},{4,7},{5,6},{6,5},{7,4},{8,11},{9,10},{10,... | collective-permute-start | bytes 98312 | tf_op jit(solution)/shard_map/ppermute | solution.py:275
  21.0 3.4 %collective-permute-start.9 = (f32[64,128]{1,0:T(8,128)S(1)}, f32[64,128]{1,0:T(8,128)S(1)}, u32[]{:S(2)}, u32[]{:S(2)}) collective-permute-start(f32[64,128]{1,0:T(8,128)S(1)} %grads.1), channel_id=1, source_target_pairs={{0,5},{1,4},{2,7},{3,6},{4,1},{5,0},{6,3},{7,2},{8,13},{9,12},{10,... | collective-permute-start | bytes 98312 | tf_op jit(solution)/shard_map/ppermute | solution.py:275
  21.3 7.3 %collective-permute-start.14 = (bf16[32,2048]{1,0:T(8,128)(2,1)S(1)}, bf16[32,2048]{1,0:T(8,128)(2,1)S(1)}, u32[]{:S(2)}, u32[]{:S(2)}) collective-permute-start(bf16[32,2048]{1,0:T(8,128)(2,1)S(1)} %get-tuple-element.26), channel_id=1, source_target_pairs={{0,1},{1,0},{2,3},{3,2},{4,5},{5,4},{6,7},{7,6},{8,9},{9,8},{10,11... | collective-permute-start | bytes 393224 | tf_op jit(solution)/shard_map/ppermute | solution.py:275
  24.4 5.2 %collective-permute-start.11 = (f32[64,128]{1,0:T(8,128)S(1)}, f32[64,128]{1,0:T(8,128)S(1)}, u32[]{:S(2)}, u32[]{:S(2)}) collective-permute-start(f32[64,128]{1,0:T(8,128)S(1)} %add_add_fusion.m0), channel_id=1, source_target_pairs={{0,25},{1,24},{2,27},{3,26},{4,29},{5,28},{6,31},{7,30},{8,17},{9,... | collective-permute-start | bytes 98312 | tf_op jit(solution)/shard_map/ppermute | solution.py:275
  27.8 4.3 %collective-permute-start.12 = (f32[64,128]{1,0:T(8,128)S(1)}, f32[64,128]{1,0:T(8,128)S(1)}, u32[]{:S(2)}, u32[]{:S(2)}) collective-permute-start(f32[64,128]{1,0:T(8,128)S(1)} %add_add_fusion.m0), channel_id=1, source_target_pairs={{0,17},{1,16},{2,19},{3,18},{4,21},{5,20},{6,23},{7,22},{8,25},{9,... | collective-permute-start | bytes 98312 | tf_op jit(solution)/shard_map/ppermute | solution.py:275
  27.8 4.3 %collective-permute-start.13 = (f32[64,128]{1,0:T(8,128)S(1)}, f32[64,128]{1,0:T(8,128)S(1)}, u32[]{:S(2)}, u32[]{:S(2)}) collective-permute-start(f32[64,128]{1,0:T(8,128)S(1)} %add_add_fusion.m0), channel_id=1, source_target_pairs={{0,8},{1,9},{2,10},{3,11},{4,12},{5,13},{6,14},{7,15},{8,0},{9,1},... | collective-permute-start | bytes 98312 | tf_op jit(solution)/shard_map/ppermute | solution.py:275
  32.5 1.2 %collective-permute-start.15 = (f32[16,128]{1,0:T(8,128)S(1)}, f32[16,128]{1,0:T(8,128)S(1)}, u32[]{:S(2)}, u32[]{:S(2)}) collective-permute-start(f32[16,128]{1,0:T(8,128)S(1)} %products.1.mine), channel_id=1, source_target_pairs={{0,1},{1,0},{2,3},{3,2},{4,5},{5,4},{6,7},{7,6},{8,9},{9,8},{10,11... | collective-permute-start | bytes 24584 | tf_op jit(solution)/shard_map/ppermute | solution.py:275
